TPU v7x, 512 devices: a whole 4x8x8 slice. The times are simulated.
512 devices in a mesh: value: 64 (over x, z, core), replica: 8 (over y).
Axes of the slice: x: 4, y: 8, z: 8, core: 2. Of those that a mesh axis runs over, the one named last changes fastest.
Arguments:
- key_blocks: int32 [65536, 2], P(('value', 'replica')), may hold values from 0 to 63, all different within a row; in each aligned block of 128 rows (0 to 127, 128 to 255, ...) at most 5 rows name the same one
- key_rows: int32 [65536, 32], P(('value', 'replica')), may hold values from 0 to 127, as said below
- weights: float32 [65536, 32], P(('value', 'replica')), may hold values from 0.02 to 0.5
- value_table: bfloat16 [8192, 4096], P('value'), may hold values from -6 to 6
- cotangent: bfloat16 [65536, 4096], P(('value', 'replica')), may hold values from -0.75 to 0.75
Outputs:
- memory_out: bfloat16 [65536, 4096], P(('value', 'replica'))
- weight_grad: bfloat16 [65536, 32], P(('value', 'replica'))
- table_grad: bfloat16 [8192, 4096], P(('value', 'replica'))
Inputs may be any that keep to these rules, and one draw needn't show every extreme that they name: `key_blocks`: in each row the 2 numbers differ; among the rows of one device (aligned blocks of 128 rows) no number appears more than 5 times, and some number appears exactly 5 times. `key_rows`: the 16 numbers of one key block (positions 16 g to 16 g + 15) differ.
All inputs are finite; a program needn't handle non-finite values.
Results may differ from a plain program's by a relative error of at most 0.017.
Values may be sent and summed in bfloat16 or wider, within the bound.
No kernel may reach another device: no remote copies, remote signals or barrier semaphores. Data moves between devices by JAX's collectives and lax.ppermute only.
A program may use at most 64 MiB of HBM per device.

v0:
```python
import jax
import jax.numpy as jnp
from jax import lax
from jax.sharding import PartitionSpec as P


def serve_lookup(rows_in, weights_in, value_table):
    shard_rows = value_table.shape[0]
    hits = rows_in[:, :, None] == jnp.arange(shard_rows, dtype=jnp.int32)[None, None, :]
    mixing = jnp.sum(jnp.where(hits, weights_in.astype(jnp.float32)[:, :, None], 0.0), axis=1)
    mixing = mixing.astype(jnp.bfloat16)
    partial_value = jnp.dot(mixing, value_table, preferred_element_type=jnp.float32).astype(
        jnp.bfloat16
    )
    return (mixing, partial_value)


def serve_grads(rows_in, mixing, grads_in, value_table):
    table_part = lax.dot_general(
        mixing, grads_in, (((0,), (0,)), ((), ())), preferred_element_type=jnp.float32
    )
    scores = lax.dot_general(
        grads_in, value_table, (((1,), (1,)), ((), ())), preferred_element_type=jnp.float32
    )
    weight_part = jnp.take_along_axis(scores, rows_in, axis=1).astype(jnp.bfloat16)
    return (table_part, weight_part)


def on_device(key_blocks, key_rows, weights, value_table, cotangent):
    owner_count = lax.axis_size("value")
    token_count, groups = key_blocks.shape
    select_count = key_rows.shape[1]
    pick_count = select_count // groups
    row_width = value_table.shape[1]
    capacity = 5 * token_count * groups // (4 * owner_count)
    slot_count = owner_count * capacity
    entries = token_count * groups
    owner_ids = key_blocks.reshape(entries)
    onehot = (owner_ids[:, None] == jnp.arange(owner_count, dtype=jnp.int32)[None, :]).astype(
        jnp.int32
    )
    before = jnp.cumsum(onehot, axis=0) - onehot
    place_rank = jnp.sum(before * onehot, axis=1)
    slot_index = owner_ids * capacity + place_rank
    token_of = jnp.arange(entries, dtype=jnp.int32) // groups
    send_rows = (
        jnp.zeros((slot_count, pick_count), jnp.int32)
        .at[slot_index]
        .set(key_rows.reshape(entries, pick_count))
        .reshape(owner_count, capacity, pick_count)
    )
    send_weights = (
        jnp.zeros((slot_count, pick_count), jnp.bfloat16)
        .at[slot_index]
        .set(weights.astype(jnp.bfloat16).reshape(entries, pick_count))
        .reshape(owner_count, capacity, pick_count)
    )
    send_grads = (
        jnp.zeros((slot_count, row_width), jnp.bfloat16)
        .at[slot_index]
        .set(cotangent[token_of])
        .reshape(owner_count, capacity, row_width)
    )
    got_rows, got_weights = (
        lax.all_to_all(send_rows, "value", split_axis=0, concat_axis=0, tiled=True),
        lax.all_to_all(send_weights, "value", split_axis=0, concat_axis=0, tiled=True),
    )
    rows_flat = got_rows.reshape(slot_count, pick_count)
    mixing, partial_value = serve_lookup(
        rows_flat, got_weights.reshape(slot_count, pick_count), value_table
    )
    back_sums = lax.all_to_all(
        partial_value.reshape(owner_count, capacity, row_width),
        "value",
        split_axis=0,
        concat_axis=0,
        tiled=True,
    )
    got_grads = lax.all_to_all(send_grads, "value", split_axis=0, concat_axis=0, tiled=True)
    table_part, weight_part = serve_grads(
        rows_flat, mixing, got_grads.reshape(slot_count, row_width), value_table
    )
    back_grads = lax.all_to_all(
        weight_part.reshape(owner_count, capacity, pick_count),
        "value",
        split_axis=0,
        concat_axis=0,
        tiled=True,
    )
    picked_sums = back_sums.reshape(slot_count, row_width)[slot_index]
    memory_out = jnp.sum(
        picked_sums.reshape(token_count, groups, row_width).astype(jnp.float32), axis=1
    ).astype(jnp.bfloat16)
    weight_grad = back_grads.reshape(slot_count, pick_count)[slot_index].reshape(
        token_count, select_count
    )
    table_grad = lax.psum_scatter(
        table_part.astype(jnp.bfloat16), "replica", scatter_dimension=0, tiled=True
    )
    return (memory_out, weight_grad, table_grad)


def solution(mesh):
    return jax.shard_map(
        on_device,
        mesh=mesh,
        in_specs=(
            P(("value", "replica"), None),
            P(("value", "replica"), None),
            P(("value", "replica"), None),
            P("value", None),
            P(("value", "replica"), None),
        ),
        out_specs=(
            P(("value", "replica"), None),
            P(("value", "replica"), None),
            P(("value", "replica"), None),
        ),
        check_vma=False,
    )
```

profile of v0, /device:TPU:1, one launch (start us, length us, event | category | flops | bytes accessed | tf_op | source)
XLA Modules:
  0.0 362.5 jit_solution(6773826387875233154)
XLA Ops:
  7.2 0.8 broadcast_multiply_fusion
  8.0 0.8 copy.17
  8.7 0.1 eq.44
  8.9 0.1 eq.40
  9.0 0.7 convert_element_type.37
  9.7 0.1 copy.21
  9.9 0.1 reshape.234
  10.0 0.1 copy.16
  10.1 0.1 mul.21
  10.2 0.6 reduce-window.6
  10.8 0.2 slice_reduce_fusion
  11.1 0.1 fusion.10
  11.2 1.2 scatter_custom_fusion.1
  12.4 0.7 reshape.182
  13.1 14.8 %all-to-all-start.1 = ((bf16[64,5,16]{2,1,0:T(8,128)(2,1)}), bf16[64,5,16]{2,1,0:T(8,128)(2,1)S(1)}, u32[]{:S(2)}, u32[]{:S(2)}) async-start(bf16[64,5,16]{2,1,0:T(8,128)(2,1)} %reshape.182), calls=%async_computation.1 | async-start | bytes 262144 | tf_op jit(solution)/shard_map/all_to_all | solution.py:66
  27.9 0.8 copy.20
  28.8 0.1 reshape.226
  28.8 1.2 scatter_custom_fusion
  30.0 0.7 reshape.180
  30.8 7.5 %all-to-all-done.1 = bf16[64,5,16]{2,1,0:T(8,128)(2,1)S(1)} async-done(((bf16[64,5,16]{2,1,0:T(8,128)(2,1)}), bf16[64,5,16]{2,1,0:T(8,128)(2,1)S(1)}, u32[]{:S(2)}, u32[]{:S(2)}) %all-to-all-start.1) | async-done | bytes 10272 | tf_op jit(solution)/shard_map/all_to_all | solution.py:66
  38.3 4.9 %all-to-all-start = ((s32[64,5,16]{2,1,0:T(8,128)}), s32[64,5,16]{2,1,0:T(8,128)S(1)}, u32[]{:S(2)}, u32[]{:S(2)}) async-start(s32[64,5,16]{2,1,0:T(8,128)} %reshape.180), calls=%async_computation | async-start | bytes 524288 | tf_op jit(solution)/shard_map/all_to_all | solution.py:65
  43.2 10.8 %scatter_custom_fusion.2 = bf16[320,4096]{1,0:T(8,128)(2,1)} fusion(s32[256]{0:T(256)S(1)} %bitcast.36, bf16[128,4096]{1,0:T(8,128)(2,1)} %param.9, s32[1024]{0:T(1024)S(1)} %pad_clamp_fusion, bf16[]{:T(256)} %constant.42.clone.1), kind=kCustom, calls=%fused_computation.11 | custom fusion | bytes 2621952 | tf_op jit(solution)/shard_map/scatter | solution.py:61
  53.9 4.7 %reshape.186 = bf16[64,5,4096]{2,1,0:T(8,128)(2,1)} reshape(bf16[320,4096]{1,0:T(8,128)(2,1)} %scatter_custom_fusion.2) | data formatting | bytes 5242880 | tf_op jit(solution)/shard_map/reshape | solution.py:62
  58.6 10.5 %all-to-all-start.3 = ((bf16[64,5,4096]{2,1,0:T(8,128)(2,1)}), bf16[64,5,4096]{2,1,0:T(8,128)(2,1)}, u32[]{:S(2)}, u32[]{:S(2)}) async-start(bf16[64,5,4096]{2,1,0:T(8,128)(2,1)} %reshape.186), calls=%async_computation.3 | async-start | bytes 8388608 | tf_op jit(solution)/shard_map/all_to_all | solution.py:79
  69.2 0.1 fusion.5
  69.3 0.1 reshape.216
  69.5 1.9 select_reduce_fusion
  71.4 93.7 %all-to-all-done.3 = bf16[64,5,4096]{2,1,0:T(8,128)(2,1)} async-done(((bf16[64,5,4096]{2,1,0:T(8,128)(2,1)}), bf16[64,5,4096]{2,1,0:T(8,128)(2,1)}, u32[]{:S(2)}, u32[]{:S(2)}) %all-to-all-start.3) | async-done | bytes 2621472 | tf_op jit(solution)/shard_map/all_to_all | solution.py:79
  165.1 4.9 %reshape.187 = bf16[320,4096]{1,0:T(8,128)(2,1)} reshape(bf16[64,5,4096]{2,1,0:T(8,128)(2,1)} %all-to-all-done.3) | data formatting | bytes 5242880 | tf_op jit(solution)/shard_map/reshape | solution.py:81
  169.9 2.6 fusion.16
  172.5 42.0 %gather_fusion.2 = bf16[5120]{0:T(1024)(128)(2,1)S(1)} fusion(bf16[320,128]{1,0:T(8,128)(2,1)S(1)} %fusion.16, s32[5120]{0:T(1024)S(1)} %reshape.216), kind=kCustom, calls=%fused_computation.3 | custom fusion | bytes 61440 | tf_op jit(solution)/shard_map/jit(take_along_axis)/gather | solution.py:25
  214.5 0.1 gather.18
  214.6 0.7 select_convert_fusion
  215.3 5.7 %all-to-all-start.4 = ((bf16[64,5,16]{2,1,0:T(8,128)(2,1)}), bf16[64,5,16]{2,1,0:T(8,128)(2,1)S(1)}, u32[]{:S(2)}, u32[]{:S(2)}) async-start(bf16[64,5,16]{2,1,0:T(8,128)(2,1)} %select_convert_fusion), calls=%async_computation.4 | async-start | bytes 262144 | tf_op jit(solution)/shard_map/all_to_all | solution.py:83
  221.1 2.3 convolution_convert_fusion
  223.4 4.7 %reshape.183 = bf16[64,5,4096]{2,1,0:T(8,128)(2,1)} reshape(bf16[320,4096]{1,0:T(8,128)(2,1)} %convolution_convert_fusion) | data formatting | bytes 5242880 | tf_op jit(solution)/shard_map/reshape | solution.py:73
  228.1 3.3 all-to-all-done.4
  231.5 7.2 %all-to-all-start.2 = ((bf16[64,5,4096]{2,1,0:T(8,128)(2,1)}), bf16[64,5,4096]{2,1,0:T(8,128)(2,1)}, u32[]{:S(2)}, u32[]{:S(2)}) async-start(bf16[64,5,4096]{2,1,0:T(8,128)(2,1)} %reshape.183), calls=%async_computation.2 | async-start | bytes 8388608 | tf_op jit(solution)/shard_map/all_to_all | solution.py:72
  238.7 0.3 reduce-scatter.2.cloned.1.call-start
  238.9 3.5 convolution_convert_fusion.1
  242.5 0.9 gather_fusion.1
  243.3 0.1 reshape.190
  243.4 0.7 copy.22
  244.1 90.4 %all-to-all-done.2 = bf16[64,5,4096]{2,1,0:T(8,128)(2,1)} async-done(((bf16[64,5,4096]{2,1,0:T(8,128)(2,1)}), bf16[64,5,4096]{2,1,0:T(8,128)(2,1)}, u32[]{:S(2)}, u32[]{:S(2)}) %all-to-all-start.2) | async-done | bytes 2621472 | tf_op jit(solution)/shard_map/all_to_all | solution.py:72
  334.5 4.8 %reshape.184 = bf16[320,4096]{1,0:T(8,128)(2,1)} reshape(bf16[64,5,4096]{2,1,0:T(8,128)(2,1)} %all-to-all-done.2) | data formatting | bytes 5242880 | tf_op jit(solution)/shard_map/reshape | solution.py:90
  339.3 6.0 %gather_fusion = bf16[256,4096]{1,0:T(8,128)(2,1)S(1)} fusion(bf16[320,4096]{1,0:T(8,128)(2,1)} %reshape.184, s32[1024]{0:T(1024)S(1)} %pad_clamp_fusion.1), kind=kCustom, calls=%fused_computation | custom fusion | bytes 4195328 | tf_op jit(solution)/shard_map/gather | solution.py:90
  345.3 2.7 reshape.185
  348.0 7.7 %reduce_sum.35 = bf16[128,4096]{1,0:T(8,128)(2,1)} reduce(bf16[128,2,4096]{2,1,0:T(2,128)(2,1)} %reshape.185, bf16[]{:T(256)} %constant.42.clone.1), dimensions={1}, to_apply=%region_6.7 | reduce | flops 524288 | bytes 3145730 | tf_op jit(solution)/shard_map/reduce_sum | solution.py:91
  (16 shorter events, 0.3 us)
Async XLA Ops:
  7.2 162.8 %copy-start = (bf16[128,4096]{1,0:T(8,128)(2,1)S(1)}, bf16[128,4096]{1,0:T(8,128)(2,1)}, u32[]{:S(2)}) copy-start(bf16[128,4096]{1,0:T(8,128)(2,1)} %param.8) | copy-start | bytes 3145732
  13.1 25.2 %all-to-all-start.1 = ((bf16[64,5,16]{2,1,0:T(8,128)(2,1)}), bf16[64,5,16]{2,1,0:T(8,128)(2,1)S(1)}, u32[]{:S(2)}, u32[]{:S(2)}) async-start(bf16[64,5,16]{2,1,0:T(8,128)(2,1)} %reshape.182), calls=%async_computation.1 | async-start | bytes 262144 | tf_op jit(solution)/shard_map/all_to_all | solution.py:66
  38.3 20.4 %all-to-all-start = ((s32[64,5,16]{2,1,0:T(8,128)}), s32[64,5,16]{2,1,0:T(8,128)S(1)}, u32[]{:S(2)}, u32[]{:S(2)}) async-start(s32[64,5,16]{2,1,0:T(8,128)} %reshape.180), calls=%async_computation | async-start | bytes 524288 | tf_op jit(solution)/shard_map/all_to_all | solution.py:65
  58.6 106.4 %all-to-all-start.3 = ((bf16[64,5,4096]{2,1,0:T(8,128)(2,1)}), bf16[64,5,4096]{2,1,0:T(8,128)(2,1)}, u32[]{:S(2)}, u32[]{:S(2)}) async-start(bf16[64,5,4096]{2,1,0:T(8,128)(2,1)} %reshape.186), calls=%async_computation.3 | async-start | bytes 8388608 | tf_op jit(solution)/shard_map/all_to_all | solution.py:79
  215.3 16.1 %all-to-all-start.4 = ((bf16[64,5,16]{2,1,0:T(8,128)(2,1)}), bf16[64,5,16]{2,1,0:T(8,128)(2,1)S(1)}, u32[]{:S(2)}, u32[]{:S(2)}) async-start(bf16[64,5,16]{2,1,0:T(8,128)(2,1)} %select_convert_fusion), calls=%async_computation.4 | async-start | bytes 262144 | tf_op jit(solution)/shard_map/all_to_all | solution.py:83
  231.5 103.1 %all-to-all-start.2 = ((bf16[64,5,4096]{2,1,0:T(8,128)(2,1)}), bf16[64,5,4096]{2,1,0:T(8,128)(2,1)}, u32[]{:S(2)}, u32[]{:S(2)}) async-start(bf16[64,5,4096]{2,1,0:T(8,128)(2,1)} %reshape.183), calls=%async_computation.2 | async-start | bytes 8388608 | tf_op jit(solution)/shard_map/all_to_all | solution.py:72
  238.7 117.0 %reduce-scatter.2.cloned.1.call-start = ((), (), s32[]{:S(2)}) async-start(), calls=%async_computation.6 | async-start | bytes 1179648 | tf_op jit(solution)/shard_map/reduce_scatter | solution.py:97
Sparse Core Ops, SparseCore 0:
  242.9 38.1 reduce-scatter.1
where the time goes:
time: 364 us; the launch traced here: 362 us
  waiting for transfers between devices  195 us (54%)
  local copies, waits for them, and re-layouts  88.8 us (24%)
  starting transfers between devices  43.4 us (12%)
  between operations  14.2 us (4%)
  other arithmetic  12.7 us (3%)
  matrix products  8.38 us (2%)
    all_to_all x1, waiting for transfers between devices, on_device(): lax.all_to_all(send_grads, 'value', split_axis=0, concat_axis=0, tiled=True)  93.7 us
    all_to_all x1, waiting for transfers between devices, on_device(): lax.all_to_all(partial_value.reshape(owner_count, capacity, row_width), '...  90.4 us
    gather x3, local copies, waits for them, and re-layouts, serve_grads(): jnp.take_along_axis(scores, rows_in, axis=1).astype(jnp.bfloat16)  42.2 us
    all_to_all x1, starting transfers between devices, on_device(): lax.all_to_all(send_weights, 'value', split_axis=0, concat_axis=0, tiled=...  14.8 us
    scatter x1, local copies, waits for them, and re-layouts, on_device(): send_grads = jnp.zeros((slot_count, row_width), jnp.bfloat16).at[slot_ind...  10.8 us
    all_to_all x1, starting transfers between devices, on_device(): lax.all_to_all(send_grads, 'value', split_axis=0, concat_axis=0, tiled=True)  10.5 us
    reduce_sum x1, other arithmetic, on_device(): jnp.sum(picked_sums.reshape(token_count, groups, row_width).astype(jnp.fl...  7.69 us
    all_to_all x1, waiting for transfers between devices, on_device(): lax.all_to_all(send_weights, 'value', split_axis=0, concat_axis=0, tiled=...  7.51 us
  transfers between devices with their start and end apart: 6, of which 4 were waited for; matrix products, arithmetic and copies ran while one was open for 15% of the time, Pallas kernels for 0%

commit v1 on v0

v1 whole, which is shorter than its diff:
```python
import functools

import jax
import jax.numpy as jnp
import numpy as np
from jax import lax
from jax.experimental import pallas as pl
from jax.experimental.pallas import tpu as pltpu
from jax.sharding import Mesh
from jax.sharding import PartitionSpec as P

CAP = 5
CHIPS = 32
GROUP_SLOTS = 512
TAGS = 384
BF16 = jnp.bfloat16
F32 = jnp.float32
VMEM_LIMIT = 56 * 1024 * 1024


def iota(shape, dim):
    return lax.broadcasted_iota(jnp.int32, shape, dim)


def contract(a, b, da, db):
    return lax.dot_general(a, b, (((da,), (db,)), ((), ())), preferred_element_type=F32)


def spread_table():
    m = np.zeros((TAGS, 2 * GROUP_SLOTS), np.float32)
    for lane in range(2 * CHIPS * CAP):
        core, rest = divmod(lane, CHIPS * CAP)
        m[lane, rest // CAP * 16 + core * 8 + rest % CAP] = 1
    for i in range(2 * CAP):
        m[2 * CHIPS * CAP + i, GROUP_SLOTS + i // CAP * 8 + i % CAP :: 16] = 1
    return m


def tag_kernel(place_ref, blocks_ref, rows_ref, weights_ref, own_ref, other_ref):
    core = place_ref[0]
    n = 256
    owner = jnp.concatenate([blocks_ref[:, 0:1], blocks_ref[:, 1:2]], axis=0)
    hot = (owner == iota((n, 64), 1)).astype(F32)
    lower = (iota((n, n), 1) < iota((n, n), 0)).astype(BF16)
    before = contract(lower, hot.astype(BF16), 1, 0)
    rank = jnp.sum(before * hot, axis=1, keepdims=True).astype(jnp.int32)
    half = owner & 1
    chip = owner >> 1
    rows = rows_ref[...].astype(F32).astype(BF16)
    rows = jnp.concatenate([rows[:, :16], rows[:, 16:]], axis=0)
    weights = weights_ref[...].astype(BF16)
    weights = jnp.concatenate([weights[:, :16], weights[:, 16:]], axis=0)
    entry = iota((n, CHIPS), 0) + 1
    lanes = iota((n, TAGS), 1)
    token_place = (lanes == 2 * CHIPS * CAP + core * CAP + rank).astype(F32).astype(BF16)
    for out, mine in ((own_ref, core), (other_ref, 1 - core)):
        slot = jnp.where(half == mine, core * (CHIPS * CAP) + chip * CAP + rank, -1)
        hits = (lanes == slot).astype(F32).astype(BF16)
        tokens = jnp.where(jnp.where(half == mine, chip, -1) == iota((n, CHIPS), 1), entry, 0)
        tokens = tokens.astype(F32).astype(BF16)
        tags = jnp.concatenate([contract(rows, hits, 0, 0), contract(weights, hits, 0, 0)], axis=0)
        tags = (tags + contract(tokens, token_place, 0, 0)).astype(BF16)
        for i in range(3):
            out[i] = tags[:, 128 * i : 128 * (i + 1)]


def mix_kernel(place_ref, spread_ref, got_ref, mix_ref, pick_ref, token_ref, tags_ref, wide_ref):
    core = place_ref[0]
    flip = place_ref[1] * 16
    for g in range(CHIPS):
        for i in range(3):
            tags_ref[g * 32 : (g + 1) * 32, 128 * i : 128 * (i + 1)] = got_ref[g, 32 * i : 32 * (i + 1), :]
    for i in range(4):
        cols = slice(256 * i, 256 * (i + 1))
        wide_ref[:, cols] = contract(tags_ref[...], spread_ref[:, cols], 1, 0)
    shard_of = iota((CHIPS, GROUP_SLOTS), 1) // 16 == iota((CHIPS, GROUP_SLOTS), 0)
    second = (iota((1, GROUP_SLOTS), 1) & 8) != 0
    far = jnp.where(second, 1 - core, core).astype(F32)
    position = iota((128, GROUP_SLOTS), 0).astype(F32).astype(BF16)

    def group(g, _):
        at = pl.multiple_of(g * 32, 32)
        rows = wide_ref[pl.ds(at, 16), 0:GROUP_SLOTS]
        weights = wide_ref[pl.ds(at + 16, 16), 0:GROUP_SLOTS].astype(BF16)
        tokens = wide_ref[pl.ds(at, 32), GROUP_SLOTS : 2 * GROUP_SLOTS]
        tag = jnp.sum(jnp.where(shard_of, tokens, 0.0), axis=0, keepdims=True)
        valid = tag > 0.5
        second_block = (tag > 128.5).astype(F32)
        token = tag - 1.0 - 128.0 * second_block
        quarter = (
            (token > 31.5).astype(F32) + (token > 63.5).astype(F32) + (token > 95.5).astype(F32)
        )
        full_place = jnp.where(valid, far * 128.0 + token, -1.0)
        fold_place = jnp.where(valid, far * 32.0 + token - 32.0 * quarter, -1.0)
        part = jnp.where(valid, quarter * 2.0 + second_block, -1.0)
        token_ref[g, 0:1, :] = full_place
        token_ref[g, 1:2, :] = fold_place
        rows = (rows.astype(jnp.int32) ^ flip).astype(F32)
        picks = jnp.concatenate([jnp.where(part == float(i), rows, -1.0) for i in range(8)], axis=0)
        picks = picks.astype(BF16)
        rows = rows.astype(BF16)
        mix = jnp.zeros((128, GROUP_SLOTS), BF16)
        for k in range(16):
            mix = jnp.where(rows[k : k + 1, :] == position, weights[k : k + 1, :], mix)
        here = pl.ds(pl.multiple_of(g * 16, 16), 16)
        mix_ref[:, here, :] = mix.T.reshape(CHIPS, 16, 128)
        pick_ref[:, here, :] = picks.T.reshape(CHIPS, 16, 128)
        return 0

    lax.fori_loop(0, CHIPS, group, 0)


def value_kernel(mix_ref, token_ref, table_ref, out_ref, sums_ref):
    def shard(o, _):
        table = table_ref[:, o].reshape(128, 128)
        sums_ref[o] = contract(mix_ref[o], table, 1, 0).astype(BF16)
        return 0

    lax.fori_loop(0, CHIPS, shard, 0)
    token_rows = iota((256, GROUP_SLOTS), 0).astype(F32).astype(BF16)

    def group(g, _):
        sums = sums_ref[:, pl.ds(pl.multiple_of(g * 16, 16), 16), :].reshape(GROUP_SLOTS, 128)
        place = token_ref[g, 0:1, :].astype(BF16)
        hits = jnp.where(place == token_rows, jnp.ones((), BF16), jnp.zeros((), BF16))
        out = contract(hits, sums, 1, 0).astype(BF16)
        out_ref[0, g] = out[:128]
        out_ref[1, g] = out[128:]
        return 0

    lax.fori_loop(0, CHIPS, group, 0)


def grad_kernel(
    mix_ref, pick_ref, token_ref, table_ref, near_ref, far_ref, table_grad_ref, weight_ref, rows_ref
):
    token_rows = iota((256, GROUP_SLOTS), 0).astype(F32).astype(BF16)
    fold_rows = iota((64, GROUP_SLOTS), 0).astype(F32).astype(BF16)

    def gather(g, _):
        place = token_ref[g, 0:1, :].astype(BF16)
        hits = jnp.where(place == token_rows, jnp.ones((), BF16), jnp.zeros((), BF16))
        grads = jnp.concatenate([near_ref[g], far_ref[g]], axis=0)
        rows = contract(hits, grads, 0, 0).astype(BF16)
        rows_ref[:, pl.ds(pl.multiple_of(g * 16, 16), 16), :] = rows.reshape(CHIPS, 16, 128)
        return 0

    lax.fori_loop(0, CHIPS, gather, 0)

    def shard(o, _):
        rows = rows_ref[o]
        table_grad = contract(mix_ref[o], rows, 0, 0).astype(BF16)
        table_grad_ref[:, o] = table_grad.reshape(8, 16, 128)
        scores = contract(rows, table_ref[:, o].reshape(128, 128), 1, 1)
        picks = pick_ref[o].astype(F32).astype(jnp.int32)
        found = jnp.take_along_axis(
            scores, jnp.maximum(picks, 0), axis=1, mode="promise_in_bounds"
        )
        rows_ref[o] = jnp.where(picks >= 0, found, 0.0).astype(BF16)
        return 0

    lax.fori_loop(0, CHIPS, shard, 0)

    def group(g, _):
        found = rows_ref[:, pl.ds(pl.multiple_of(g * 16, 16), 16), :].reshape(GROUP_SLOTS, 128)
        place = token_ref[g, 1:2, :].astype(BF16)
        hits = jnp.where(place == fold_rows, jnp.ones((), BF16), jnp.zeros((), BF16))
        out = contract(hits, found, 1, 0).astype(BF16)
        weight_ref[0, g] = out[:32]
        weight_ref[1, g] = out[32:]
        return 0

    lax.fori_loop(0, CHIPS, group, 0)


def finish_kernel(got_ref, weight_ref, table_ref):
    def add(j, total):
        return total + got_ref[j, 0:32, :].astype(F32)

    total = lax.fori_loop(0, CHIPS, add, jnp.zeros((32, 128), F32))
    for i in range(4):
        weight_ref[32 * i : 32 * (i + 1), :] = total[:, 32 * i : 32 * (i + 1)].astype(BF16)
    for j in range(CHIPS):
        table_ref[:, 128 * j : 128 * (j + 1)] = got_ref[j, 32:48, :]


def call(kernel, out_shapes, *operands, scalars=0, scratch=(), cost=(0, 0)):
    vmem = pl.BlockSpec(memory_space=pltpu.VMEM)
    smem = pl.BlockSpec(memory_space=pltpu.SMEM)
    outs = tuple(jax.ShapeDtypeStruct(s, d) for s, d in out_shapes)
    return pl.pallas_call(
        kernel,
        out_shape=outs,
        in_specs=[smem] * scalars + [vmem] * (len(operands) - scalars),
        out_specs=tuple(vmem for _ in outs),
        scratch_shapes=[pltpu.VMEM(s, d) for s, d in scratch],
        compiler_params=pltpu.CompilerParams(vmem_limit_bytes=VMEM_LIMIT),
        cost_estimate=pl.CostEstimate(flops=cost[0], bytes_accessed=cost[1], transcendentals=0),
    )(*operands)


def swap_cores(v):
    return lax.ppermute(v, "core", [(0, 1), (1, 0)])


def across(v, bit):
    return lax.ppermute(v, "y", [(i, i ^ bit) for i in range(8)])


def exchange(v):
    return lax.all_to_all(v, ("x", "z"), split_axis=0, concat_axis=0, tiled=True)


def on_device(key_blocks, key_rows, weights, value_table, cotangent):
    core = lax.axis_index("core")
    y = lax.axis_index("y")
    place = jnp.stack([core, y]).astype(jnp.int32)

    own, other = call(
        tag_kernel,
        [((3, 32, 128), BF16)] * 2,
        place,
        key_blocks,
        key_rows,
        weights,
        scalars=1,
    )
    tags = (own + swap_cores(other)).reshape(1, 96, 128)
    table_part = lax.dynamic_slice_in_dim(value_table, y * 16, 16, axis=0)
    table_part = jnp.transpose(table_part.reshape(16, CHIPS, 128), (1, 0, 2))
    first = jnp.concatenate([jnp.broadcast_to(tags, (CHIPS, 96, 128)), table_part], axis=1)
    got_first = exchange(first)

    grads = jnp.transpose(cotangent.reshape(128, CHIPS, 128), (1, 0, 2))
    near_grads = exchange(lax.optimization_barrier((grads, got_first))[0])

    mix, picks, tokens = call(
        mix_kernel,
        [((CHIPS, GROUP_SLOTS, 128), BF16)] * 2 + [((CHIPS, 8, GROUP_SLOTS), F32)],
        place,
        jnp.asarray(spread_table(), BF16),
        got_first,
        scalars=1,
        scratch=[((CHIPS * 32, TAGS), BF16), ((CHIPS * 32, 2 * GROUP_SLOTS), F32)],
        cost=(10**9, 10 * 2**20),
    )
    table = got_first[:, 96:, :].reshape(1, CHIPS, 16, 128)
    for bit in (1, 2, 4):
        table = jnp.concatenate([table, across(table, bit)], axis=0)
    (sums,) = call(
        value_kernel,
        [((2, CHIPS, 128, 128), BF16)],
        mix,
        tokens,
        table,
        scratch=[((CHIPS, GROUP_SLOTS, 128), BF16)],
        cost=(2 * 10**9, 8 * 2**20),
    )
    out = (sums[0].astype(F32) + swap_cores(sums[1]).astype(F32)).astype(BF16)
    got_out = exchange(lax.optimization_barrier((out, near_grads))[0])

    far_grads = swap_cores(near_grads)
    table_grad, weight_grad = call(
        grad_kernel,
        [((8, CHIPS, 16, 128), BF16), ((2, CHIPS, 32, 128), BF16)],
        mix,
        picks,
        tokens,
        table,
        near_grads,
        far_grads,
        scratch=[((CHIPS, GROUP_SLOTS, 128), BF16)],
        cost=(2 * 10**9, 12 * 2**20),
    )
    for count in (4, 2, 1):
        received = across(table_grad[count:], count)
        table_grad = (table_grad[:count].astype(F32) + received.astype(F32)).astype(BF16)
    weight_grad = (
        weight_grad[0].astype(F32) + swap_cores(weight_grad[1]).astype(F32)
    ).astype(BF16)
    last = jnp.concatenate([weight_grad, table_grad[0]], axis=1)
    got_last = exchange(lax.optimization_barrier((last, got_out))[0])
    memory_out = jnp.transpose(got_out, (1, 0, 2)).reshape(128, 4096)
    weight_out, table_out = call(
        finish_kernel, [((128, 32), BF16), ((16, 4096), BF16)], got_last
    )
    return memory_out, weight_out, table_out


def solution(mesh):
    fine = Mesh(mesh.devices.reshape(4, 8, 2, 8), ("x", "z", "core", "y"))
    tokens = P(("x", "z", "core", "y"), None)
    return jax.shard_map(
        on_device,
        mesh=fine,
        in_specs=(tokens, tokens, tokens, P(("x", "z", "core"), None), tokens),
        out_specs=(tokens, tokens, tokens),
        check_vma=False,
    )
```

time: 364 us -> 258 us (0.71)
  the two profiles are of different devices: /device:TPU:1 before, /device:TPU:64 now
where the time goes in v1:
time: 258 us; the launch traced here: 257 us
  Pallas kernels  70.6 us (27%)
  waiting for transfers between devices  67.9 us (26%)
  starting transfers between devices  56 us (22%)
  blocking collectives  38.6 us (15%)
  local copies, waits for them, and re-layouts  15.3 us (6%)
  other arithmetic  7.33 us (3%)
    pallas_call x5, Pallas kernels, call(): pl.pallas_call(kernel, out_shape=outs, in_specs=[smem] * scalars + [vmem]...  70.6 us
    ppermute x6, waiting for transfers between devices, across(): return lax.ppermute(v, 'y', [(i, i ^ bit) for i in range(8)])  54.8 us
    all_to_all x1, blocking collectives, exchange(): lax.all_to_all(v, ('x', 'z'), split_axis=0, concat_axis=0, tiled=True)  38.6 us
    all_to_all x3, starting transfers between devices, exchange(): lax.all_to_all(v, ('x', 'z'), split_axis=0, concat_axis=0, tiled=True)  24.7 us
    ppermute x6, starting transfers between devices, across(): return lax.ppermute(v, 'y', [(i, i ^ bit) for i in range(8)])  23.1 us
    all_to_all x3, waiting for transfers between devices, exchange(): lax.all_to_all(v, ('x', 'z'), split_axis=0, concat_axis=0, tiled=True)  11.2 us
    unnamed x16, local copies, waits for them, and re-layouts  9.52 us
    ppermute x4, starting transfers between devices, swap_cores(): return lax.ppermute(v, 'core', [(0, 1), (1, 0)])  8.15 us
  transfers between devices with their start and end apart: 13, of which 8 were waited for; matrix products, arithmetic and copies ran while one was open for 6% of the time, Pallas kernels for 26%

profile of v1, /device:TPU:64, one launch (start us, length us, event | category | flops | bytes accessed | tf_op | source)
XLA Modules:
  0.0 256.6 jit_solution(1302049963467126570)
XLA Ops:
  0.7 1.5 copy.13.blocks_ref
  2.2 1.4 copy.14.rows_ref
  3.6 1.4 copy.15.weights_ref
  5.0 0.6 pad_add_fusion.place_ref
  5.6 2.3 shard_map.85
  7.9 1.9 collective-permute-start
  9.9 1.3 collective-permute-done
  11.2 0.7 add.21
  12.0 0.1 broadcast_in_dim.8
  12.1 0.1 pad_maximum_fusion.1
  12.2 38.6 %all_to_all.20.got_ref = bf16[32,112,128]{2,1,0:T(8,128)(2,1)S(1)} all-to-all(bf16[32,112,128]{2,1,0:T(8,128)(2,1)S(1)} %pad_maximum_fusion.1), channel_id=1, replica_groups=mesh['x'=4,'z'=8,'core'=2,'y'=8] {'x','z'}, dimensions={0} | all-to-all | bytes 1835008 | tf_op jit(solution)/shard_map/all_to_all | solution.py:211
  50.7 3.5 %collective-permute-start.1 = (bf16[1,32,16,128]{3,2,1,0:T(8,128)(2,1)S(1)}, bf16[1,32,16,128]{3,2,1,0:T(8,128)(2,1)S(1)}, u32[]{:S(2)}, u32[]{:S(2)}) collective-permute-start(bf16[1,32,16,128]{3,2,1,0:T(8,128)(2,1)S(1)} %slice_bitcast_fusion.3), channel_id=1, source_target_pairs={{0,1},{1,0},{2,3},{3,2},{4,5},{5,4},{6,7},{7,6},{8,9},{9,8},{10,11... | collective-permute-start | bytes 393224 | tf_op jit(solution)/shard_map/ppermute | solution.py:207
  54.2 1.6 copy.17
  55.9 1.3 copy.18
  57.2 5.1 %all-to-all-start.1 = ((bf16[32,128,128]{2,1,0:T(8,128)(2,1)}), bf16[32,128,128]{2,1,0:T(8,128)(2,1)}, u32[]{:S(2)}, u32[]{:S(2)}) async-start(bf16[32,128,128]{2,1,0:T(8,128)(2,1)} %bitcast.8), calls=%async_computation.1 | async-start | bytes 2097152 | tf_op jit(solution)/shard_map/all_to_all | solution.py:211
  62.4 4.5 %collective-permute-start.2 = (bf16[2,32,16,128]{3,2,1,0:T(8,128)(2,1)S(1)}, bf16[2,32,16,128]{3,2,1,0:T(8,128)(2,1)S(1)}, u32[]{:S(2)}, u32[]{:S(2)}) collective-permute-start(bf16[2,32,16,128]{3,2,1,0:T(8,128)(2,1)S(1)} %pad_maximum_fusion.4), channel_id=1, source_target_pairs={{0,2},{1,3},{2,0},{3,1},{4,6},{5,7},{6,4},{7,5},{8,10},{9,11},{10,... | collective-permute-start | bytes 786440 | tf_op jit(solution)/shard_map/ppermute | solution.py:207
  66.9 10.5 %collective-permute-done.2 = bf16[2,32,16,128]{3,2,1,0:T(8,128)(2,1)S(1)} collective-permute-done((bf16[2,32,16,128]{3,2,1,0:T(8,128)(2,1)S(1)}, bf16[2,32,16,128]{3,2,1,0:T(8,128)(2,1)S(1)}, u32[]{:S(2)}, u32[]{:S(2)}) %collective-permute-start.2) | collective-permute-done | bytes 262176 | tf_op jit(solution)/shard_map/ppermute | solution.py:207
  77.4 6.9 %collective-permute-start.3 = (bf16[4,32,16,128]{3,2,1,0:T(8,128)(2,1)S(1)}, bf16[4,32,16,128]{3,2,1,0:T(8,128)(2,1)S(1)}, u32[]{:S(2)}, u32[]{:S(2)}) collective-permute-start(bf16[4,32,16,128]{3,2,1,0:T(8,128)(2,1)S(1)} %pad_maximum_fusion.2), channel_id=1, source_target_pairs={{0,4},{1,5},{2,6},{3,7},{4,0},{5,1},{6,2},{7,3},{8,12},{9,13},{10,... | collective-permute-start | bytes 1572872 | tf_op jit(solution)/shard_map/ppermute | solution.py:207
  84.4 14.8 %shard_map.86 = (bf16[32,512,128]{2,1,0:T(8,128)(2,1)}, bf16[32,512,128]{2,1,0:T(8,128)(2,1)}, f32[32,8,512]{2,1,0:T(8,128)}) custom-call(s32[2]{0:T(128)} %pad_add_fusion.place_ref, bf16[384,1024]{1,0:T(8,128)(2,1)} %constant.17.clone.spread_ref, bf16[32,112,128]{2,1,0:T(8,128)(2,1)} %copy-done.3), custom_call_target="tpu_custom_call" | custom-call | flops 1000000000 | bytes 10485760 | tf_op jit(solution)/shard_map/pallas_call | solution.py:191
  99.2 9.2 %collective-permute-done.3 = bf16[4,32,16,128]{3,2,1,0:T(8,128)(2,1)S(1)} collective-permute-done((bf16[4,32,16,128]{3,2,1,0:T(8,128)(2,1)S(1)}, bf16[4,32,16,128]{3,2,1,0:T(8,128)(2,1)S(1)}, u32[]{:S(2)}, u32[]{:S(2)}) %collective-permute-start.3) | collective-permute-done | bytes 524320 | tf_op jit(solution)/shard_map/ppermute | solution.py:207
  108.4 1.1 pad_maximum_fusion.table_ref
  109.5 16.7 %shard_map.87 = bf16[2,32,128,128]{3,2,1,0:T(8,128)(2,1)} custom-call(bf16[32,512,128]{2,1,0:T(8,128)(2,1)} %get-tuple-element.17.mix_ref, f32[32,8,512]{2,1,0:T(8,128)} %get-tuple-element.18.token_ref, bf16[8,32,16,128]{3,2,1,0:T(8,128)(2,1)} %pad_maximum_fusion.table_ref), custom_call_target="tpu_custom_call" | custom-call | flops 2000000000 | bytes 8388608 | tf_op jit(solution)/shard_map/pallas_call | solution.py:191
  126.2 2.5 slice_bitcast_fusion
  128.6 1.9 collective-permute-start.4
  130.6 2.4 collective-permute-start.5
  133.0 0.5 collective-permute-done.4
  133.5 2.6 %fusion = bf16[32,128,128]{2,1,0:T(8,128)(2,1)} fusion(bf16[32,128,128]{2,1,0:T(8,128)(2,1)} %collective-permute-done.4, bf16[2,32,128,128]{3,2,1,0:T(8,128)(2,1)S(1)} %copy-done.1), kind=kLoop, calls=%fused_computation.1 | loop fusion | flops 2097152 | bytes 3145728 | tf_op jit(solution)/shard_map/convert_element_type | solution.py:259
  136.2 9.8 %all-to-all-start.2 = ((bf16[32,128,128]{2,1,0:T(8,128)(2,1)}), bf16[32,128,128]{2,1,0:T(8,128)(2,1)S(1)}, u32[]{:S(2)}, u32[]{:S(2)}) async-start(bf16[32,128,128]{2,1,0:T(8,128)(2,1)} %fusion), calls=%async_computation.2 | async-start | bytes 2097152 | tf_op jit(solution)/shard_map/all_to_all | solution.py:211
  146.0 35.0 %shard_map.88 = (bf16[8,32,16,128]{3,2,1,0:T(8,128)(2,1)}, bf16[2,32,32,128]{3,2,1,0:T(8,128)(2,1)}) custom-call(bf16[32,512,128]{2,1,0:T(8,128)(2,1)} %get-tuple-element.17.mix_ref, bf16[32,512,128]{2,1,0:T(8,128)(2,1)} %get-tuple-element.21.pick_ref, f32[32,8,512]{2,1,0:T(8,128)} %get-tuple-element.18.token_ref, ...), custom_call_target="tpu_custom_call" | custom-call | flops 2000000000 | bytes 12582912 | tf_op jit(solution)/shard_map/pallas_call | solution.py:191
  180.9 1.1 slice.39
  182.1 4.4 %collective-permute-start.7 = (bf16[4,32,16,128]{3,2,1,0:T(8,128)(2,1)S(1)}, bf16[4,32,16,128]{3,2,1,0:T(8,128)(2,1)S(1)}, u32[]{:S(2)}, u32[]{:S(2)}) collective-permute-start(bf16[4,32,16,128]{3,2,1,0:T(8,128)(2,1)S(1)} %slice.39), channel_id=1, source_target_pairs={{0,4},{1,5},{2,6},{3,7},{4,0},{5,1},{6,2},{7,3},{8,12},{9,13},{10,... | collective-permute-start | bytes 1572872 | tf_op jit(solution)/shard_map/ppermute | solution.py:207
  186.4 17.5 %collective-permute-done.7 = bf16[4,32,16,128]{3,2,1,0:T(8,128)(2,1)S(1)} collective-permute-done((bf16[4,32,16,128]{3,2,1,0:T(8,128)(2,1)S(1)}, bf16[4,32,16,128]{3,2,1,0:T(8,128)(2,1)S(1)}, u32[]{:S(2)}, u32[]{:S(2)}) %collective-permute-start.7) | collective-permute-done | bytes 524320 | tf_op jit(solution)/shard_map/ppermute | solution.py:207
  204.0 1.2 add_convert_fusion
  205.2 1.9 collective-permute-start.8
  207.1 1.9 collective-permute-start.6
  209.1 12.7 %collective-permute-done.8 = bf16[2,32,16,128]{3,2,1,0:T(8,128)(2,1)S(1)} collective-permute-done((bf16[2,32,16,128]{3,2,1,0:T(8,128)(2,1)S(1)}, bf16[2,32,16,128]{3,2,1,0:T(8,128)(2,1)S(1)}, u32[]{:S(2)}, u32[]{:S(2)}) %collective-permute-start.8) | collective-permute-done | bytes 262176 | tf_op jit(solution)/shard_map/ppermute | solution.py:207
  221.8 0.1 add_convert_fusion.1
  221.9 1.9 collective-permute-start.9
  223.8 0.1 fusion.1
  223.9 4.8 %collective-permute-done.9 = bf16[1,32,16,128]{3,2,1,0:T(8,128)(2,1)S(1)} collective-permute-done((bf16[1,32,16,128]{3,2,1,0:T(8,128)(2,1)S(1)}, bf16[1,32,16,128]{3,2,1,0:T(8,128)(2,1)S(1)}, u32[]{:S(2)}, u32[]{:S(2)}) %collective-permute-start.9) | collective-permute-done | bytes 131104 | tf_op jit(solution)/shard_map/ppermute | solution.py:207
  228.8 0.8 pad_maximum_fusion.3
  229.6 9.8 %all-to-all-start.3 = ((bf16[32,48,128]{2,1,0:T(8,128)(2,1)}), bf16[32,48,128]{2,1,0:T(8,128)(2,1)S(1)}, u32[]{:S(2)}, u32[]{:S(2)}) async-start(bf16[32,48,128]{2,1,0:T(8,128)(2,1)} %pad_maximum_fusion.3), calls=%async_computation.3 | async-start | bytes 786432 | tf_op jit(solution)/shard_map/all_to_all | solution.py:211
  239.4 0.7 copy.19
  240.1 1.3 copy.20
  241.4 11.2 %all-to-all-done.3.got_ref = bf16[32,48,128]{2,1,0:T(8,128)(2,1)S(1)} async-done(((bf16[32,48,128]{2,1,0:T(8,128)(2,1)}), bf16[32,48,128]{2,1,0:T(8,128)(2,1)S(1)}, u32[]{:S(2)}, u32[]{:S(2)}) %all-to-all-start.3) | async-done | bytes 393248 | tf_op jit(solution)/shard_map/all_to_all | solution.py:211
  252.6 0.7 copy-done.2
  253.3 1.9 shard_map.89
  255.2 1.4 copy.21
  (22 shorter events, 0.2 us)
Async XLA Ops:
  0.6 9.2 %copy-start = (bf16[128,4096]{1,0:T(8,128)(2,1)S(1)}, bf16[128,4096]{1,0:T(8,128)(2,1)}, u32[]{:S(2)}) copy-start(bf16[128,4096]{1,0:T(8,128)(2,1)} %param.9) | copy-start | bytes 3145732
  7.9 3.3 %collective-permute-start = (bf16[3,32,128]{2,1,0:T(8,128)(2,1)}, bf16[3,32,128]{2,1,0:T(8,128)(2,1)S(1)}, u32[]{:S(2)}, u32[]{:S(2)}) collective-permute-start(bf16[3,32,128]{2,1,0:T(8,128)(2,1)} %get-tuple-element.16), channel_id=1, source_target_pairs={{0,8},{8,0},{1,9},{9,1},{2,10},{10,2},{3,11},{11,3},{4,12},{12,4},... | collective-permute-start | bytes 73736 | tf_op jit(solution)/shard_map/ppermute | solution.py:203
  50.7 6.5 %copy-start.3 = (bf16[32,112,128]{2,1,0:T(8,128)(2,1)}, bf16[32,112,128]{2,1,0:T(8,128)(2,1)S(1)}, u32[]{:S(2)}) copy-start(bf16[32,112,128]{2,1,0:T(8,128)(2,1)S(1)} %all_to_all.20.got_ref) | copy-start | bytes 2752516
  50.7 11.6 %collective-permute-start.1 = (bf16[1,32,16,128]{3,2,1,0:T(8,128)(2,1)S(1)}, bf16[1,32,16,128]{3,2,1,0:T(8,128)(2,1)S(1)}, u32[]{:S(2)}, u32[]{:S(2)}) collective-permute-start(bf16[1,32,16,128]{3,2,1,0:T(8,128)(2,1)S(1)} %slice_bitcast_fusion.3), channel_id=1, source_target_pairs={{0,1},{1,0},{2,3},{3,2},{4,5},{5,4},{6,7},{7,6},{8,9},{9,8},{10,11... | collective-permute-start | bytes 393224 | tf_op jit(solution)/shard_map/ppermute | solution.py:207
  57.2 73.4 %all-to-all-start.1 = ((bf16[32,128,128]{2,1,0:T(8,128)(2,1)}), bf16[32,128,128]{2,1,0:T(8,128)(2,1)}, u32[]{:S(2)}, u32[]{:S(2)}) async-start(bf16[32,128,128]{2,1,0:T(8,128)(2,1)} %bitcast.8), calls=%async_computation.1 | async-start | bytes 2097152 | tf_op jit(solution)/shard_map/all_to_all | solution.py:211
  62.4 15.0 %collective-permute-start.2 = (bf16[2,32,16,128]{3,2,1,0:T(8,128)(2,1)S(1)}, bf16[2,32,16,128]{3,2,1,0:T(8,128)(2,1)S(1)}, u32[]{:S(2)}, u32[]{:S(2)}) collective-permute-start(bf16[2,32,16,128]{3,2,1,0:T(8,128)(2,1)S(1)} %pad_maximum_fusion.4), channel_id=1, source_target_pairs={{0,2},{1,3},{2,0},{3,1},{4,6},{5,7},{6,4},{7,5},{8,10},{9,11},{10,... | collective-permute-start | bytes 786440 | tf_op jit(solution)/shard_map/ppermute | solution.py:207
  77.4 31.0 %collective-permute-start.3 = (bf16[4,32,16,128]{3,2,1,0:T(8,128)(2,1)S(1)}, bf16[4,32,16,128]{3,2,1,0:T(8,128)(2,1)S(1)}, u32[]{:S(2)}, u32[]{:S(2)}) collective-permute-start(bf16[4,32,16,128]{3,2,1,0:T(8,128)(2,1)S(1)} %pad_maximum_fusion.2), channel_id=1, source_target_pairs={{0,4},{1,5},{2,6},{3,7},{4,0},{5,1},{6,2},{7,3},{8,12},{9,13},{10,... | collective-permute-start | bytes 1572872 | tf_op jit(solution)/shard_map/ppermute | solution.py:207
  126.2 7.4 %copy-start.1 = (bf16[2,32,128,128]{3,2,1,0:T(8,128)(2,1)S(1)}, bf16[2,32,128,128]{3,2,1,0:T(8,128)(2,1)}, u32[]{:S(2)}) copy-start(bf16[2,32,128,128]{3,2,1,0:T(8,128)(2,1)} %shard_map.87) | copy-start | bytes 6291460
  128.6 4.9 %collective-permute-start.4 = (bf16[32,128,128]{2,1,0:T(8,128)(2,1)}, bf16[32,128,128]{2,1,0:T(8,128)(2,1)}, u32[]{:S(2)}, u32[]{:S(2)}) collective-permute-start(bf16[32,128,128]{2,1,0:T(8,128)(2,1)} %slice_bitcast_fusion), channel_id=1, source_target_pairs={{0,8},{8,0},{1,9},{9,1},{2,10},{10,2},{3,11},{11,3},{4,12},{12,4},... | collective-permute-start | bytes 3145736 | tf_op jit(solution)/shard_map/ppermute | solution.py:203
  130.6 15.4 %collective-permute-start.5 = (bf16[32,128,128]{2,1,0:T(8,128)(2,1)}, bf16[32,128,128]{2,1,0:T(8,128)(2,1)}, u32[]{:S(2)}, u32[]{:S(2)}) collective-permute-start(bf16[32,128,128]{2,1,0:T(8,128)(2,1)} %all-to-all-done.1.near_ref), channel_id=1, source_target_pairs={{0,8},{8,0},{1,9},{9,1},{2,10},{10,2},{3,11},{11,3},{4,12},{12,4},... | collective-permute-start | bytes 3145736 | tf_op jit(solution)/shard_map/ppermute | solution.py:203
  136.2 93.4 %all-to-all-start.2 = ((bf16[32,128,128]{2,1,0:T(8,128)(2,1)}), bf16[32,128,128]{2,1,0:T(8,128)(2,1)S(1)}, u32[]{:S(2)}, u32[]{:S(2)}) async-start(bf16[32,128,128]{2,1,0:T(8,128)(2,1)} %fusion), calls=%async_computation.2 | async-start | bytes 2097152 | tf_op jit(solution)/shard_map/all_to_all | solution.py:211
  180.9 26.2 %copy-start.4 = (bf16[2,32,32,128]{3,2,1,0:T(8,128)(2,1)S(1)}, bf16[2,32,32,128]{3,2,1,0:T(8,128)(2,1)}, u32[]{:S(2)}) copy-start(bf16[2,32,32,128]{3,2,1,0:T(8,128)(2,1)} %get-tuple-element.22) | copy-start | bytes 1572868
  182.1 21.9 %collective-permute-start.7 = (bf16[4,32,16,128]{3,2,1,0:T(8,128)(2,1)S(1)}, bf16[4,32,16,128]{3,2,1,0:T(8,128)(2,1)S(1)}, u32[]{:S(2)}, u32[]{:S(2)}) collective-permute-start(bf16[4,32,16,128]{3,2,1,0:T(8,128)(2,1)S(1)} %slice.39), channel_id=1, source_target_pairs={{0,4},{1,5},{2,6},{3,7},{4,0},{5,1},{6,2},{7,3},{8,12},{9,13},{10,... | collective-permute-start | bytes 1572872 | tf_op jit(solution)/shard_map/ppermute | solution.py:207
  205.2 16.6 %collective-permute-start.8 = (bf16[2,32,16,128]{3,2,1,0:T(8,128)(2,1)S(1)}, bf16[2,32,16,128]{3,2,1,0:T(8,128)(2,1)S(1)}, u32[]{:S(2)}, u32[]{:S(2)}) collective-permute-start(bf16[2,32,16,128]{3,2,1,0:T(8,128)(2,1)S(1)} %slice.48), channel_id=1, source_target_pairs={{0,2},{1,3},{2,0},{3,1},{4,6},{5,7},{6,4},{7,5},{8,10},{9,11},{10,... | collective-permute-start | bytes 786440 | tf_op jit(solution)/shard_map/ppermute | solution.py:207
  207.1 16.7 %collective-permute-start.6 = (bf16[32,32,128]{2,1,0:T(8,128)(2,1)S(1)}, bf16[32,32,128]{2,1,0:T(8,128)(2,1)S(1)}, u32[]{:S(2)}, u32[]{:S(2)}) collective-permute-start(bf16[32,32,128]{2,1,0:T(8,128)(2,1)S(1)} %slice_bitcast_fusion.2), channel_id=1, source_target_pairs={{0,8},{8,0},{1,9},{9,1},{2,10},{10,2},{3,11},{11,3},{4,12},{12,4},... | collective-permute-start | bytes 786440 | tf_op jit(solution)/shard_map/ppermute | solution.py:203
  221.9 6.9 %collective-permute-start.9 = (bf16[1,32,16,128]{3,2,1,0:T(8,128)(2,1)S(1)}, bf16[1,32,16,128]{3,2,1,0:T(8,128)(2,1)S(1)}, u32[]{:S(2)}, u32[]{:S(2)}) collective-permute-start(bf16[1,32,16,128]{3,2,1,0:T(8,128)(2,1)S(1)} %slice.50), channel_id=1, source_target_pairs={{0,1},{1,0},{2,3},{3,2},{4,5},{5,4},{6,7},{7,6},{8,9},{9,8},{10,11... | collective-permute-start | bytes 393224 | tf_op jit(solution)/shard_map/ppermute | solution.py:207
  229.6 23.0 %all-to-all-start.3 = ((bf16[32,48,128]{2,1,0:T(8,128)(2,1)}), bf16[32,48,128]{2,1,0:T(8,128)(2,1)S(1)}, u32[]{:S(2)}, u32[]{:S(2)}) async-start(bf16[32,48,128]{2,1,0:T(8,128)(2,1)} %pad_maximum_fusion.3), calls=%async_computation.3 | async-start | bytes 786432 | tf_op jit(solution)/shard_map/all_to_all | solution.py:211
  252.6 0.8 copy-start.2

commit v2 on v1

v2 whole, which is shorter than its diff:
```python
import jax
import jax.numpy as jnp
import numpy as np
from jax import lax
from jax.experimental import pallas as pl
from jax.experimental.pallas import tpu as pltpu
from jax.sharding import Mesh
from jax.sharding import PartitionSpec as P

CAP = 5
CHIPS = 32
GROUP_SLOTS = 512
TAGS = 384
BF16 = jnp.bfloat16
F32 = jnp.float32


def iota(shape, dim):
    return lax.broadcasted_iota(jnp.int32, shape, dim)


def contract(a, b, da, db):
    return lax.dot_general(a, b, (((da,), (db,)), ((), ())), preferred_element_type=F32)


def spread_table():
    m = np.zeros((TAGS, 2 * GROUP_SLOTS), np.float32)
    for lane in range(2 * CHIPS * CAP):
        core, rest = divmod(lane, CHIPS * CAP)
        m[lane, rest // CAP * 16 + core * 8 + rest % CAP] = 1
    for i in range(2 * CAP):
        m[2 * CHIPS * CAP + i, GROUP_SLOTS + i // CAP * 8 + i % CAP :: 16] = 1
    return m


def tag_kernel(blocks_ref, rows_ref, weights_ref, own_ref, other_ref):
    core = lax.axis_index("core")
    n = 256
    owner = jnp.concatenate([blocks_ref[0:1, :], blocks_ref[1:2, :]], axis=1)
    hot = (owner == iota((64, n), 0)).astype(F32)
    upper = (iota((n, n), 0) < iota((n, n), 1)).astype(BF16)
    before = contract(hot.astype(BF16), upper, 1, 0)
    rank = jnp.sum(before * hot, axis=0, keepdims=True).astype(jnp.int32)
    half = owner & 1
    chip = owner >> 1
    rows = rows_ref[...].astype(F32).astype(BF16)
    rows = jnp.concatenate([rows[:16], rows[16:]], axis=1)
    weights = weights_ref[...].astype(BF16)
    weights = jnp.concatenate([weights[:16], weights[16:]], axis=1)
    entry = iota((CHIPS, n), 1) + 1
    lanes = iota((TAGS, n), 0)
    token_place = (lanes == 2 * CHIPS * CAP + core * CAP + rank).astype(F32).astype(BF16)
    for out, mine in ((own_ref, core), (other_ref, 1 - core)):
        slot = jnp.where(half == mine, core * (CHIPS * CAP) + chip * CAP + rank, -1)
        hits = (lanes == slot).astype(F32).astype(BF16)
        tokens = jnp.where(jnp.where(half == mine, chip, -1) == iota((CHIPS, n), 0), entry, 0)
        tokens = tokens.astype(F32).astype(BF16)
        tags = jnp.concatenate([contract(rows, hits, 1, 1), contract(weights, hits, 1, 1)], axis=0)
        tags = (tags + contract(tokens, token_place, 1, 1)).astype(BF16)
        for i in range(3):
            out[i] = tags[:, 128 * i : 128 * (i + 1)]


def split_kernel(grads_ref, out_ref):
    for j in range(CHIPS):
        out_ref[j] = grads_ref[:, 128 * j : 128 * (j + 1)]


def first_kernel(own_ref, other_ref, table_ref, out_ref):
    y = lax.axis_index("y")
    tags = own_ref[...].reshape(96, 128) + other_ref[...].reshape(96, 128)
    for j in range(CHIPS):
        out_ref[j, 0:96, :] = tags
    for i in range(4):
        block = (((y >> 1) ^ i) << 1) | (y & 1)
        rows = pl.ds(pl.multiple_of(block * 16, 16), 16)
        for j in range(CHIPS):
            out_ref[j, 96 + 16 * i : 112 + 16 * i, :] = table_ref[rows, 128 * j : 128 * (j + 1)]


def mix_kernel(spread_ref, got_ref, mix_ref, pick_ref, token_ref, tags_ref, wide_ref):
    core = lax.axis_index("core")
    flip = lax.axis_index("y") * 16
    for g in range(CHIPS):
        for i in range(3):
            tags_ref[g * 32 : (g + 1) * 32, 128 * i : 128 * (i + 1)] = got_ref[g, 32 * i : 32 * (i + 1), :]
    for i in range(4):
        cols = slice(256 * i, 256 * (i + 1))
        wide_ref[:, cols] = contract(tags_ref[...], spread_ref[:, cols], 1, 0)
    shard_of = iota((CHIPS, GROUP_SLOTS), 1) // 16 == iota((CHIPS, GROUP_SLOTS), 0)
    second = (iota((1, GROUP_SLOTS), 1) & 8) != 0
    far = jnp.where(second, 1 - core, core).astype(F32)
    position = iota((128, GROUP_SLOTS), 0).astype(F32).astype(BF16)

    def group(g, _):
        at = pl.multiple_of(g * 32, 32)
        rows = wide_ref[pl.ds(at, 16), 0:GROUP_SLOTS]
        weights = wide_ref[pl.ds(at + 16, 16), 0:GROUP_SLOTS].astype(BF16)
        tokens = wide_ref[pl.ds(at, 32), GROUP_SLOTS : 2 * GROUP_SLOTS]
        tag = jnp.sum(jnp.where(shard_of, tokens, 0.0), axis=0, keepdims=True)
        valid = tag > 0.5
        second_block = (tag > 128.5).astype(F32)
        token = tag - 1.0 - 128.0 * second_block
        quarter = (
            (token > 31.5).astype(F32) + (token > 63.5).astype(F32) + (token > 95.5).astype(F32)
        )
        full_place = jnp.where(valid, far * 128.0 + token, -1.0)
        fold_place = jnp.where(valid, far * 32.0 + token - 32.0 * quarter, -1.0)
        part = jnp.where(valid, quarter * 2.0 + second_block, -1.0)
        token_ref[g, 0:1, :] = full_place
        token_ref[g, 1:2, :] = fold_place
        rows = (rows.astype(jnp.int32) ^ flip).astype(F32)
        picks = jnp.concatenate([jnp.where(part == float(i), rows, -1.0) for i in range(8)], axis=0)
        picks = picks.astype(BF16)
        rows = rows.astype(BF16)
        mix = jnp.zeros((128, GROUP_SLOTS), BF16)
        for k in range(16):
            mix = jnp.where(rows[k : k + 1, :] == position, weights[k : k + 1, :], mix)
        here = pl.ds(pl.multiple_of(g * 16, 16), 16)
        mix_ref[:, here, :] = mix.T.reshape(CHIPS, 16, 128)
        pick_ref[:, here, :] = picks.T.reshape(CHIPS, 16, 128)
        return 0

    lax.fori_loop(0, CHIPS, group, 0, unroll=4)


def table_of(got_ref, table_ref, o):
    pieces = []
    for i in range(4):
        pieces += [got_ref[o, 96 + 16 * i : 112 + 16 * i, :], table_ref[o, 16 * i : 16 * (i + 1), :]]
    return jnp.concatenate(pieces, axis=0)


def value_kernel(mix_ref, token_ref, got_ref, table_ref, near_ref, far_ref, sums_ref):
    def shard(o, _):
        sums_ref[o] = contract(mix_ref[o], table_of(got_ref, table_ref, o), 1, 0).astype(BF16)
        return 0

    lax.fori_loop(0, CHIPS, shard, 0, unroll=8)
    token_rows = iota((256, GROUP_SLOTS), 0).astype(F32).astype(BF16)

    def group(g, _):
        sums = sums_ref[:, pl.ds(pl.multiple_of(g * 16, 16), 16), :].reshape(GROUP_SLOTS, 128)
        place = token_ref[g, 0:1, :].astype(BF16)
        hits = jnp.where(place == token_rows, jnp.ones((), BF16), jnp.zeros((), BF16))
        out = contract(hits, sums, 1, 0).astype(BF16)
        near_ref[g] = out[:128]
        far_ref[g] = out[128:]
        return 0

    lax.fori_loop(0, CHIPS, group, 0, unroll=8)


def table_grad_kernel(mix_ref, token_ref, near_ref, far_ref, rows_ref, *grad_refs):
    token_rows = iota((256, GROUP_SLOTS), 0).astype(F32).astype(BF16)

    def gather(g, _):
        place = token_ref[g, 0:1, :].astype(BF16)
        hits = jnp.where(place == token_rows, jnp.ones((), BF16), jnp.zeros((), BF16))
        grads = jnp.concatenate([near_ref[g], far_ref[g]], axis=0)
        rows = contract(hits, grads, 0, 0).astype(BF16)
        rows_ref[:, pl.ds(pl.multiple_of(g * 16, 16), 16), :] = rows.reshape(CHIPS, 16, 128)
        return 0

    lax.fori_loop(0, CHIPS, gather, 0, unroll=8)

    def shard(o, _):
        grad = contract(mix_ref[o], rows_ref[o], 0, 0).astype(BF16)
        for m in range(8):
            grad_refs[m][o] = grad[16 * m : 16 * (m + 1)]
        return 0

    lax.fori_loop(0, CHIPS, shard, 0, unroll=8)


def weight_grad_kernel(rows_ref, pick_ref, token_ref, got_ref, table_ref, near_ref, far_ref, found_ref):
    fold_rows = iota((64, GROUP_SLOTS), 0).astype(F32).astype(BF16)

    def shard(o, _):
        scores = contract(rows_ref[o], table_of(got_ref, table_ref, o), 1, 1)
        picks = pick_ref[o].astype(F32).astype(jnp.int32)
        found = jnp.take_along_axis(scores, jnp.maximum(picks, 0), axis=1, mode="promise_in_bounds")
        found_ref[o] = jnp.where(picks >= 0, found, 0.0).astype(BF16)
        return 0

    lax.fori_loop(0, CHIPS, shard, 0, unroll=8)

    def group(g, _):
        found = found_ref[:, pl.ds(pl.multiple_of(g * 16, 16), 16), :].reshape(GROUP_SLOTS, 128)
        place = token_ref[g, 1:2, :].astype(BF16)
        hits = jnp.where(place == fold_rows, jnp.ones((), BF16), jnp.zeros((), BF16))
        out = contract(hits, found, 1, 0).astype(BF16)
        near_ref[g] = out[:32]
        far_ref[g] = out[32:]
        return 0

    lax.fori_loop(0, CHIPS, group, 0, unroll=8)


def last_kernel(near_ref, far_ref, *refs):
    out_ref = refs[-1]

    def chip(j, _):
        out_ref[j, 0:32, :] = (near_ref[j].astype(F32) + far_ref[j].astype(F32)).astype(BF16)
        total = refs[0][j].astype(F32)
        for ref in refs[1:-1]:
            total += ref[j].astype(F32)
        out_ref[j, 32:48, :] = total.astype(BF16)
        return 0

    lax.fori_loop(0, CHIPS, chip, 0, unroll=4)


def finish_kernel(got_ref, weight_ref, table_ref):
    def add(j, total):
        return total + got_ref[j, 0:32, :].astype(F32)

    total = lax.fori_loop(0, CHIPS, add, jnp.zeros((32, 128), F32), unroll=8)
    total = jnp.concatenate([total[:, 32 * i : 32 * (i + 1)] for i in range(4)], axis=0)
    weight_ref[...] = total.T.astype(BF16)
    for j in range(CHIPS):
        table_ref[:, 128 * j : 128 * (j + 1)] = got_ref[j, 32:48, :]


def call(kernel, out_shapes, *operands, scratch=(), cost=(0, 0), limit=16):
    vmem = pl.BlockSpec(memory_space=pltpu.VMEM)
    outs = tuple(jax.ShapeDtypeStruct(s, BF16) if not isinstance(s, jax.ShapeDtypeStruct) else s for s in out_shapes)
    return pl.pallas_call(
        kernel,
        out_shape=outs,
        in_specs=[vmem] * len(operands),
        out_specs=tuple(vmem for _ in outs),
        scratch_shapes=[pltpu.VMEM(s, d) for s, d in scratch],
        compiler_params=pltpu.CompilerParams(vmem_limit_bytes=limit * 2**20),
        cost_estimate=pl.CostEstimate(flops=cost[0], bytes_accessed=cost[1], transcendentals=0),
    )(*operands)


def swap_cores(v):
    return lax.ppermute(v, "core", [(0, 1), (1, 0)])


def across(v, bits):
    return lax.ppermute(v, "y", [(i, i ^ bits) for i in range(8)])


def exchange(v):
    return lax.all_to_all(v, ("x", "z"), split_axis=0, concat_axis=0, tiled=True)


def after(v, *others):
    return lax.optimization_barrier((v, *others))[0]


def on_device(key_blocks, key_rows, weights, value_table, cotangent):
    own, other = call(
        tag_kernel, [(3, 32, 128)] * 2, key_blocks.T, key_rows.T, weights.T, cost=(10**8, 2**20)
    )
    other = swap_cores(other)
    (grads,) = call(split_kernel, [(CHIPS, 128, 128)], cotangent, cost=(0, 2 * 2**20))
    other, grads = lax.optimization_barrier((other, grads))
    (first,) = call(first_kernel, [(CHIPS, 160, 128)], own, other, value_table, cost=(0, 3 * 2**20))
    got_first = exchange(first)
    near_grads = exchange(after(grads, got_first))

    table = across(got_first[:, 96:, :], 1)
    mix, picks, tokens = call(
        mix_kernel,
        [(CHIPS, GROUP_SLOTS, 128)] * 2 + [jax.ShapeDtypeStruct((CHIPS, 8, GROUP_SLOTS), F32)],
        jnp.asarray(spread_table(), BF16),
        got_first,
        scratch=[((CHIPS * 32, TAGS), BF16), ((CHIPS * 32, 2 * GROUP_SLOTS), F32)],
        cost=(10**9, 10 * 2**20),
        limit=24,
    )
    near, far = call(
        value_kernel,
        [(CHIPS, 128, 128)] * 2,
        mix,
        tokens,
        got_first,
        table,
        scratch=[((CHIPS, GROUP_SLOTS, 128), BF16)],
        cost=(2 * 10**9, 8 * 2**20),
    )
    out = (near.astype(F32) + swap_cores(far).astype(F32)).astype(BF16)
    got_out = exchange(after(out, near_grads))

    far_grads = swap_cores(near_grads)
    rows, *table_grads = call(
        table_grad_kernel,
        [(CHIPS, GROUP_SLOTS, 128)] + [(CHIPS, 16, 128)] * 8,
        mix,
        tokens,
        near_grads,
        far_grads,
        cost=(2 * 10**9, 12 * 2**20),
    )
    table_grads = [table_grads[0]] + [across(table_grads[m], m) for m in range(1, 8)]
    near, far = call(
        weight_grad_kernel,
        [(CHIPS, 32, 128)] * 2,
        rows,
        picks,
        tokens,
        got_first,
        table,
        scratch=[((CHIPS, GROUP_SLOTS, 128), BF16)],
        cost=(2 * 10**9, 12 * 2**20),
    )
    (last,) = call(
        last_kernel, [(CHIPS, 48, 128)], near, swap_cores(far), *table_grads, cost=(0, 2 * 2**20)
    )
    got_last = exchange(after(last, got_out))
    memory_out = jnp.transpose(got_out, (1, 0, 2)).reshape(128, 4096)
    weight_out, table_out = call(finish_kernel, [(32, 128), (16, 4096)], got_last)
    return memory_out, weight_out.T, table_out


def solution(mesh):
    fine = Mesh(mesh.devices.reshape(4, 8, 2, 8), ("x", "z", "core", "y"))
    tokens = P(("x", "z", "core", "y"), None)
    return jax.shard_map(
        on_device,
        mesh=fine,
        in_specs=(tokens, tokens, tokens, P(("x", "z", "core"), None), tokens),
        out_specs=(tokens, tokens, tokens),
        check_vma=False,
    )
```

time: 258 us -> 190 us (0.74)
  Pallas kernels: 70.6 us -> 29.9 us
  waiting for transfers between devices: 67.9 us -> 38.6 us
  blocking collectives: 38.6 us -> 47.8 us
  other arithmetic: 7.33 us -> 1.34 us
  local copies, waits for them, and re-layouts: 15.3 us -> 12.6 us
    pallas_call x5 -> x9, Pallas kernels: 70.6 us -> 29.9 us  [call(): pl.pallas_call(kernel, out_shape=outs, in_specs=[vmem] * len(operands), o...]
    ppermute x6 -> x8, waiting for transfers between devices: 54.8 us -> 15 us  [across(): return lax.ppermute(v, 'y', [(i, i ^ bits) for i in range(8)])]
    all_to_all x1, blocking collectives: 38.6 us -> 47.8 us  [exchange(): lax.all_to_all(v, ('x', 'z'), split_axis=0, concat_axis=0, tiled=True)]
    ppermute x6 -> x8, starting transfers between devices: 23.1 us -> 30.4 us  [across(): return lax.ppermute(v, 'y', [(i, i ^ bits) for i in range(8)])]
    all_to_all x3, waiting for transfers between devices: 11.2 us -> 18.3 us  [exchange(): lax.all_to_all(v, ('x', 'z'), split_axis=0, concat_axis=0, tiled=True)]
    all_to_all x3, starting transfers between devices: 24.7 us -> 19.6 us  [exchange(): lax.all_to_all(v, ('x', 'z'), split_axis=0, concat_axis=0, tiled=True)]
    ppermute x4, waiting for transfers between devices: 1.87 us -> 5.26 us  [swap_cores(): return lax.ppermute(v, 'core', [(0, 1), (1, 0)])]
    convert_element_type x4 -> x1, other arithmetic: 3.97 us -> 1.34 us  [on_device(): out = (near.astype(F32) + swap_cores(far).astype(F32)).astype(BF16)]
  transfers between devices with their start and end apart: 13 -> 15, of which waited for: 8 -> 6; matrix products, arithmetic and copies ran while one was open for 6% -> 2% of each run, Pallas kernels for 26% -> 15%
where the time goes in v2:
time: 190 us; the launch traced here: 189 us
  starting transfers between devices  58 us (31%)
  blocking collectives  47.8 us (25%)
  waiting for transfers between devices  38.6 us (20%)
  Pallas kernels  29.9 us (16%)
  local copies, waits for them, and re-layouts  12.6 us (7%)
    all_to_all x1, blocking collectives, exchange(): lax.all_to_all(v, ('x', 'z'), split_axis=0, concat_axis=0, tiled=True)  47.8 us
    ppermute x8, starting transfers between devices, across(): return lax.ppermute(v, 'y', [(i, i ^ bits) for i in range(8)])  30.4 us
    pallas_call x9, Pallas kernels, call(): pl.pallas_call(kernel, out_shape=outs, in_specs=[vmem] * len(operands), o...  29.9 us
    all_to_all x3, starting transfers between devices, exchange(): lax.all_to_all(v, ('x', 'z'), split_axis=0, concat_axis=0, tiled=True)  19.6 us
    all_to_all x3, waiting for transfers between devices, exchange(): lax.all_to_all(v, ('x', 'z'), split_axis=0, concat_axis=0, tiled=True)  18.3 us
    ppermute x8, waiting for transfers between devices, across(): return lax.ppermute(v, 'y', [(i, i ^ bits) for i in range(8)])  15 us
    unnamed x21, local copies, waits for them, and re-layouts  10.1 us
    ppermute x4, starting transfers between devices, swap_cores(): return lax.ppermute(v, 'core', [(0, 1), (1, 0)])  7.95 us
  transfers between devices with their start and end apart: 15, of which 6 were waited for; matrix products, arithmetic and copies ran while one was open for 2% of the time, Pallas kernels for 15%

profile of v2, /device:TPU:64, one launch (start us, length us, event | category | flops | bytes accessed | tf_op | source)
XLA Modules:
  0.0 189.1 jit_solution(856988080184997117)
XLA Ops:
  0.7 0.8 copy-done.4
  1.4 0.7 copy-done.5
  2.2 0.7 copy-done.6
  2.8 0.6 shard_map.85
  3.5 1.9 %collective-permute-start = (bf16[3,32,128]{2,1,0:T(8,128)(2,1)S(1)}, bf16[3,32,128]{2,1,0:T(8,128)(2,1)S(1)}, u32[]{:S(2)}, u32[]{:S(2)}) collective-permute-start(bf16[3,32,128]{2,1,0:T(8,128)(2,1)S(1)} %get-tuple-element.29), channel_id=1, source_target_pairs={{0,8},{8,0},{1,9},{9,1},{2,10},{10,2},{3,11},{11,3},{4,12},{12,4},... | collective-permute-start | bytes 73736 | tf_op jit(solution)/shard_map/ppermute | solution.py:240
  5.4 0.0 copy-start.3
  5.4 1.2 copy-done.3
  6.7 1.2 shard_map.86
  7.9 0.0 collective-permute-done.other_ref
  7.9 0.1 shard_map.87
  8.0 47.8 %all_to_all.20.got_ref = bf16[32,160,128]{2,1,0:T(8,128)(2,1)S(1)} all-to-all(bf16[32,160,128]{2,1,0:T(8,128)(2,1)S(1)} %shard_map.87), channel_id=1, replica_groups=mesh['x'=4,'z'=8,'core'=2,'y'=8] {'x','z'}, dimensions={0} | all-to-all | bytes 2621440 | tf_op jit(solution)/shard_map/all_to_all | solution.py:248
  55.8 0.9 slice.4
  56.6 3.5 %collective-permute-start.1 = (bf16[32,64,128]{2,1,0:T(8,128)(2,1)}, bf16[32,64,128]{2,1,0:T(8,128)(2,1)S(1)}, u32[]{:S(2)}, u32[]{:S(2)}) collective-permute-start(bf16[32,64,128]{2,1,0:T(8,128)(2,1)} %slice.4), channel_id=1, source_target_pairs={{0,1},{1,0},{2,3},{3,2},{4,5},{5,4},{6,7},{7,6},{8,9},{9,8},{10,11... | collective-permute-start | bytes 1572872 | tf_op jit(solution)/shard_map/ppermute | solution.py:244
  60.1 4.6 %all-to-all-start.1 = ((bf16[32,128,128]{2,1,0:T(8,128)(2,1)}), bf16[32,128,128]{2,1,0:T(8,128)(2,1)S(1)}, u32[]{:S(2)}, u32[]{:S(2)}) async-start(bf16[32,128,128]{2,1,0:T(8,128)(2,1)} %shard_map.86), calls=%async_computation.1 | async-start | bytes 2097152 | tf_op jit(solution)/shard_map/all_to_all | solution.py:248
  64.8 0.0 copy-start.7
  64.8 1.1 copy-done.7
  65.9 8.6 %shard_map.88 = (bf16[32,512,128]{2,1,0:T(8,128)(2,1)S(1)}, bf16[32,512,128]{2,1,0:T(8,128)(2,1)S(1)}, f32[32,8,512]{2,1,0:T(8,128)S(1)}) custom-call(bf16[384,1024]{1,0:T(8,128)(2,1)S(1)} %copy-done.7, bf16[32,160,128]{2,1,0:T(8,128)(2,1)S(1)} %all_to_all.20.got_ref), custom_call_target="tpu_custom_call" | custom-call | flops 1000000000 | bytes 10485760 | tf_op jit(solution)/shard_map/pallas_call | solution.py:228
  74.5 4.5 %shard_map.89 = (bf16[32,128,128]{2,1,0:T(8,128)(2,1)S(1)}, bf16[32,128,128]{2,1,0:T(8,128)(2,1)S(1)}) custom-call(bf16[32,512,128]{2,1,0:T(8,128)(2,1)S(1)} %get-tuple-element.31.mix_ref, f32[32,8,512]{2,1,0:T(8,128)S(1)} %get-tuple-element.32.token_ref, bf16[32,160,128]{2,1,0:T(8,128)(2,1)S(1)} %all_to_all.20.got_ref, ...), custom_call_target="tpu_custom_call" | custom-call | flops 2000000000 | bytes 8388608 | tf_op jit(solution)/shard_map/pallas_call | solution.py:228
  79.1 2.0 %copy-done.8 = bf16[32,512,128]{2,1,0:T(8,128)(2,1)} copy-done((bf16[32,512,128]{2,1,0:T(8,128)(2,1)}, bf16[32,512,128]{2,1,0:T(8,128)(2,1)S(1)}, u32[]{:S(2)}) %copy-start.8) | copy-done | bytes 4194328
  81.1 1.9 %collective-permute-start.2 = (bf16[32,128,128]{2,1,0:T(8,128)(2,1)S(1)}, bf16[32,128,128]{2,1,0:T(8,128)(2,1)S(1)}, u32[]{:S(2)}, u32[]{:S(2)}) collective-permute-start(bf16[32,128,128]{2,1,0:T(8,128)(2,1)S(1)} %get-tuple-element.34), channel_id=1, source_target_pairs={{0,8},{8,0},{1,9},{9,1},{2,10},{10,2},{3,11},{11,3},{4,12},{12,4},... | collective-permute-start | bytes 3145736 | tf_op jit(solution)/shard_map/ppermute | solution.py:240
  83.0 2.6 %collective-permute-done.2 = bf16[32,128,128]{2,1,0:T(8,128)(2,1)S(1)} collective-permute-done((bf16[32,128,128]{2,1,0:T(8,128)(2,1)S(1)}, bf16[32,128,128]{2,1,0:T(8,128)(2,1)S(1)}, u32[]{:S(2)}, u32[]{:S(2)}) %collective-permute-start.2) | collective-permute-done | bytes 1048608 | tf_op jit(solution)/shard_map/ppermute | solution.py:240
  85.6 1.3 add_convert_fusion
  87.0 6.0 %all-to-all-done.1.near_ref = bf16[32,128,128]{2,1,0:T(8,128)(2,1)S(1)} async-done(((bf16[32,128,128]{2,1,0:T(8,128)(2,1)}), bf16[32,128,128]{2,1,0:T(8,128)(2,1)S(1)}, u32[]{:S(2)}, u32[]{:S(2)}) %all-to-all-start.1) | async-done | bytes 1048608 | tf_op jit(solution)/shard_map/all_to_all | solution.py:248
  93.0 5.2 %all-to-all-start.2 = ((bf16[32,128,128]{2,1,0:T(8,128)(2,1)}), bf16[32,128,128]{2,1,0:T(8,128)(2,1)}, u32[]{:S(2)}, u32[]{:S(2)}) async-start(bf16[32,128,128]{2,1,0:T(8,128)(2,1)} %add_convert_fusion), calls=%async_computation.2 | async-start | bytes 2097152 | tf_op jit(solution)/shard_map/all_to_all | solution.py:248
  98.2 2.2 %collective-permute-start.3 = (bf16[32,128,128]{2,1,0:T(8,128)(2,1)S(1)}, bf16[32,128,128]{2,1,0:T(8,128)(2,1)S(1)}, u32[]{:S(2)}, u32[]{:S(2)}) collective-permute-start(bf16[32,128,128]{2,1,0:T(8,128)(2,1)S(1)} %all-to-all-done.1.near_ref), channel_id=1, source_target_pairs={{0,8},{8,0},{1,9},{9,1},{2,10},{10,2},{3,11},{11,3},{4,12},{12,4},... | collective-permute-start | bytes 3145736 | tf_op jit(solution)/shard_map/ppermute | solution.py:240
  100.4 2.6 %collective-permute-done.3.far_ref = bf16[32,128,128]{2,1,0:T(8,128)(2,1)S(1)} collective-permute-done((bf16[32,128,128]{2,1,0:T(8,128)(2,1)S(1)}, bf16[32,128,128]{2,1,0:T(8,128)(2,1)S(1)}, u32[]{:S(2)}, u32[]{:S(2)}) %collective-permute-start.3) | collective-permute-done | bytes 1048608 | tf_op jit(solution)/shard_map/ppermute | solution.py:240
  103.1 2.2 %copy-done.9 = bf16[32,512,128]{2,1,0:T(8,128)(2,1)S(1)} copy-done((bf16[32,512,128]{2,1,0:T(8,128)(2,1)S(1)}, bf16[32,512,128]{2,1,0:T(8,128)(2,1)}, u32[]{:S(2)}) %copy-start.9) | copy-done | bytes 4194328
  105.3 5.1 %shard_map.90 = (bf16[32,512,128]{2,1,0:T(8,128)(2,1)S(1)}, bf16[32,16,128]{2,1,0:T(8,128)(2,1)S(1)}, bf16[32,16,128]{2,1,0:T(8,128)(2,1)S(1)}, bf16[32,16,128]{...) custom-call(bf16[32,512,128]{2,1,0:T(8,128)(2,1)S(1)} %copy-done.9, ...), custom_call_target="tpu_custom_call" | custom-call | flops 2000000000 | bytes 12582912 | tf_op jit(solution)/shard_map/pallas_call | solution.py:228
  110.4 5.3 %collective-permute-start.10 = (bf16[32,16,128]{2,1,0:T(8,128)(2,1)S(1)}, bf16[32,16,128]{2,1,0:T(8,128)(2,1)S(1)}, u32[]{:S(2)}, u32[]{:S(2)}) collective-permute-start(bf16[32,16,128]{2,1,0:T(8,128)(2,1)S(1)} %get-tuple-element.48), channel_id=1, source_target_pairs={{0,6},{1,7},{2,4},{3,5},{4,2},{5,3},{6,0},{7,1},{8,14},{9,15},{10,... | collective-permute-start | bytes 393224 | tf_op jit(solution)/shard_map/ppermute | solution.py:244
  115.6 1.9 %collective-permute-start.11 = (bf16[32,16,128]{2,1,0:T(8,128)(2,1)S(1)}, bf16[32,16,128]{2,1,0:T(8,128)(2,1)S(1)}, u32[]{:S(2)}, u32[]{:S(2)}) collective-permute-start(bf16[32,16,128]{2,1,0:T(8,128)(2,1)S(1)} %get-tuple-element.49), channel_id=1, source_target_pairs={{0,7},{1,6},{2,5},{3,4},{4,3},{5,2},{6,1},{7,0},{8,15},{9,14},{10,... | collective-permute-start | bytes 393224 | tf_op jit(solution)/shard_map/ppermute | solution.py:244
  117.6 4.1 %collective-permute-start.5 = (bf16[32,16,128]{2,1,0:T(8,128)(2,1)S(1)}, bf16[32,16,128]{2,1,0:T(8,128)(2,1)S(1)}, u32[]{:S(2)}, u32[]{:S(2)}) collective-permute-start(bf16[32,16,128]{2,1,0:T(8,128)(2,1)S(1)} %get-tuple-element.43), channel_id=1, source_target_pairs={{0,1},{1,0},{2,3},{3,2},{4,5},{5,4},{6,7},{7,6},{8,9},{9,8},{10,11... | collective-permute-start | bytes 393224 | tf_op jit(solution)/shard_map/ppermute | solution.py:244
  121.7 7.9 %shard_map.91 = (bf16[32,32,128]{2,1,0:T(8,128)(2,1)S(1)}, bf16[32,32,128]{2,1,0:T(8,128)(2,1)S(1)}) custom-call(bf16[32,512,128]{2,1,0:T(8,128)(2,1)S(1)} %get-tuple-element.38.rows_ref, bf16[32,512,128]{2,1,0:T(8,128)(2,1)S(1)} %copy-done.1, f32[32,8,512]{2,1,0:T(8,128)S(1)} %get-tuple-element.32.token_ref, bf16[32,160,128]{2,1,0:T(8,128)(2,1)S(1)} %all_to_all.20.got_ref, ...), custom_call_target="tpu_custom_call" | custom-call | flops 2000000000 | bytes 12582912 | tf_op jit(solution)/shard_map/pallas_call | solution.py:228
  129.6 1.9 %collective-permute-start.4 = (bf16[32,32,128]{2,1,0:T(8,128)(2,1)S(1)}, bf16[32,32,128]{2,1,0:T(8,128)(2,1)S(1)}, u32[]{:S(2)}, u32[]{:S(2)}) collective-permute-start(bf16[32,32,128]{2,1,0:T(8,128)(2,1)S(1)} %get-tuple-element.41), channel_id=1, source_target_pairs={{0,8},{8,0},{1,9},{9,1},{2,10},{10,2},{3,11},{11,3},{4,12},{12,4},... | collective-permute-start | bytes 786440 | tf_op jit(solution)/shard_map/ppermute | solution.py:240
  131.6 3.6 %collective-permute-start.6 = (bf16[32,16,128]{2,1,0:T(8,128)(2,1)S(1)}, bf16[32,16,128]{2,1,0:T(8,128)(2,1)S(1)}, u32[]{:S(2)}, u32[]{:S(2)}) collective-permute-start(bf16[32,16,128]{2,1,0:T(8,128)(2,1)S(1)} %get-tuple-element.44), channel_id=1, source_target_pairs={{0,2},{1,3},{2,0},{3,1},{4,6},{5,7},{6,4},{7,5},{8,10},{9,11},{10,... | collective-permute-start | bytes 393224 | tf_op jit(solution)/shard_map/ppermute | solution.py:244
  135.2 0.0 collective-permute-done.10.refs_6_
  135.2 2.7 %collective-permute-start.7 = (bf16[32,16,128]{2,1,0:T(8,128)(2,1)S(1)}, bf16[32,16,128]{2,1,0:T(8,128)(2,1)S(1)}, u32[]{:S(2)}, u32[]{:S(2)}) collective-permute-start(bf16[32,16,128]{2,1,0:T(8,128)(2,1)S(1)} %get-tuple-element.45), channel_id=1, source_target_pairs={{0,3},{1,2},{2,1},{3,0},{4,7},{5,6},{6,5},{7,4},{8,11},{9,10},{10,... | collective-permute-start | bytes 393224 | tf_op jit(solution)/shard_map/ppermute | solution.py:244
  137.9 0.0 collective-permute-done.11.refs_7_
  137.9 7.2 %collective-permute-start.8 = (bf16[32,16,128]{2,1,0:T(8,128)(2,1)S(1)}, bf16[32,16,128]{2,1,0:T(8,128)(2,1)S(1)}, u32[]{:S(2)}, u32[]{:S(2)}) collective-permute-start(bf16[32,16,128]{2,1,0:T(8,128)(2,1)S(1)} %get-tuple-element.46), channel_id=1, source_target_pairs={{0,4},{1,5},{2,6},{3,7},{4,0},{5,1},{6,2},{7,3},{8,12},{9,13},{10,... | collective-permute-start | bytes 393224 | tf_op jit(solution)/shard_map/ppermute | solution.py:244
  145.1 2.1 %collective-permute-start.9 = (bf16[32,16,128]{2,1,0:T(8,128)(2,1)S(1)}, bf16[32,16,128]{2,1,0:T(8,128)(2,1)S(1)}, u32[]{:S(2)}, u32[]{:S(2)}) collective-permute-start(bf16[32,16,128]{2,1,0:T(8,128)(2,1)S(1)} %get-tuple-element.47), channel_id=1, source_target_pairs={{0,5},{1,4},{2,7},{3,6},{4,1},{5,0},{6,3},{7,2},{8,13},{9,12},{10,... | collective-permute-start | bytes 393224 | tf_op jit(solution)/shard_map/ppermute | solution.py:244
  147.2 0.0 collective-permute-done.7.refs_3_
  147.3 2.5 %collective-permute-done.8.refs_4_ = bf16[32,16,128]{2,1,0:T(8,128)(2,1)S(1)} collective-permute-done((bf16[32,16,128]{2,1,0:T(8,128)(2,1)S(1)}, bf16[32,16,128]{2,1,0:T(8,128)(2,1)S(1)}, u32[]{:S(2)}, u32[]{:S(2)}) %collective-permute-start.8) | collective-permute-done | bytes 131104 | tf_op jit(solution)/shard_map/ppermute | solution.py:244
  149.7 12.5 %collective-permute-done.9.refs_5_ = bf16[32,16,128]{2,1,0:T(8,128)(2,1)S(1)} collective-permute-done((bf16[32,16,128]{2,1,0:T(8,128)(2,1)S(1)}, bf16[32,16,128]{2,1,0:T(8,128)(2,1)S(1)}, u32[]{:S(2)}, u32[]{:S(2)}) %collective-permute-start.9) | collective-permute-done | bytes 131104 | tf_op jit(solution)/shard_map/ppermute | solution.py:244
  162.3 1.0 shard_map.92
  163.3 9.8 %all-to-all-start.3 = ((bf16[32,48,128]{2,1,0:T(8,128)(2,1)}), bf16[32,48,128]{2,1,0:T(8,128)(2,1)S(1)}, u32[]{:S(2)}, u32[]{:S(2)}) async-start(bf16[32,48,128]{2,1,0:T(8,128)(2,1)} %shard_map.92), calls=%async_computation.3 | async-start | bytes 786432 | tf_op jit(solution)/shard_map/all_to_all | solution.py:248
  173.1 1.6 copy.9
  174.7 1.3 copy.10
  176.0 12.3 %all-to-all-done.3.got_ref = bf16[32,48,128]{2,1,0:T(8,128)(2,1)S(1)} async-done(((bf16[32,48,128]{2,1,0:T(8,128)(2,1)}), bf16[32,48,128]{2,1,0:T(8,128)(2,1)S(1)}, u32[]{:S(2)}, u32[]{:S(2)}) %all-to-all-start.3) | async-done | bytes 393248 | tf_op jit(solution)/shard_map/all_to_all | solution.py:248
  188.3 0.8 shard_map.93
  (16 shorter events, 0.0 us)
Async XLA Ops:
  0.6 7.2 %copy-start.2 = (bf16[128,4096]{1,0:T(8,128)(2,1)S(1)}, bf16[128,4096]{1,0:T(8,128)(2,1)}, u32[]{:S(2)}) copy-start(bf16[128,4096]{1,0:T(8,128)(2,1)} %table_ref.1) | copy-start | bytes 3145732
  0.6 0.8 copy-start.4
  1.4 0.7 copy-start.5
  2.2 0.7 copy-start.6
  3.5 4.4 %collective-permute-start = (bf16[3,32,128]{2,1,0:T(8,128)(2,1)S(1)}, bf16[3,32,128]{2,1,0:T(8,128)(2,1)S(1)}, u32[]{:S(2)}, u32[]{:S(2)}) collective-permute-start(bf16[3,32,128]{2,1,0:T(8,128)(2,1)S(1)} %get-tuple-element.29), channel_id=1, source_target_pairs={{0,8},{8,0},{1,9},{9,1},{2,10},{10,2},{3,11},{11,3},{4,12},{12,4},... | collective-permute-start | bytes 73736 | tf_op jit(solution)/shard_map/ppermute | solution.py:240
  5.4 1.2 copy-start.3
  56.6 17.9 %collective-permute-start.1 = (bf16[32,64,128]{2,1,0:T(8,128)(2,1)}, bf16[32,64,128]{2,1,0:T(8,128)(2,1)S(1)}, u32[]{:S(2)}, u32[]{:S(2)}) collective-permute-start(bf16[32,64,128]{2,1,0:T(8,128)(2,1)} %slice.4), channel_id=1, source_target_pairs={{0,1},{1,0},{2,3},{3,2},{4,5},{5,4},{6,7},{7,6},{8,9},{9,8},{10,11... | collective-permute-start | bytes 1572872 | tf_op jit(solution)/shard_map/ppermute | solution.py:244
  60.1 32.9 %all-to-all-start.1 = ((bf16[32,128,128]{2,1,0:T(8,128)(2,1)}), bf16[32,128,128]{2,1,0:T(8,128)(2,1)S(1)}, u32[]{:S(2)}, u32[]{:S(2)}) async-start(bf16[32,128,128]{2,1,0:T(8,128)(2,1)} %shard_map.86), calls=%async_computation.1 | async-start | bytes 2097152 | tf_op jit(solution)/shard_map/all_to_all | solution.py:248
  64.8 1.1 copy-start.7
  74.5 4.5 %copy-start = (bf16[32,512,128]{2,1,0:T(8,128)(2,1)}, bf16[32,512,128]{2,1,0:T(8,128)(2,1)S(1)}, u32[]{:S(2)}) copy-start(bf16[32,512,128]{2,1,0:T(8,128)(2,1)S(1)} %get-tuple-element.39.pick_ref) | copy-start | bytes 12582916
  79.1 2.0 %copy-start.8 = (bf16[32,512,128]{2,1,0:T(8,128)(2,1)}, bf16[32,512,128]{2,1,0:T(8,128)(2,1)S(1)}, u32[]{:S(2)}) copy-start(bf16[32,512,128]{2,1,0:T(8,128)(2,1)S(1)} %get-tuple-element.31.mix_ref) | copy-start | bytes 12582916
  81.1 4.5 %collective-permute-start.2 = (bf16[32,128,128]{2,1,0:T(8,128)(2,1)S(1)}, bf16[32,128,128]{2,1,0:T(8,128)(2,1)S(1)}, u32[]{:S(2)}, u32[]{:S(2)}) collective-permute-start(bf16[32,128,128]{2,1,0:T(8,128)(2,1)S(1)} %get-tuple-element.34), channel_id=1, source_target_pairs={{0,8},{8,0},{1,9},{9,1},{2,10},{10,2},{3,11},{11,3},{4,12},{12,4},... | collective-permute-start | bytes 3145736 | tf_op jit(solution)/shard_map/ppermute | solution.py:240
  93.0 70.3 %all-to-all-start.2 = ((bf16[32,128,128]{2,1,0:T(8,128)(2,1)}), bf16[32,128,128]{2,1,0:T(8,128)(2,1)}, u32[]{:S(2)}, u32[]{:S(2)}) async-start(bf16[32,128,128]{2,1,0:T(8,128)(2,1)} %add_convert_fusion), calls=%async_computation.2 | async-start | bytes 2097152 | tf_op jit(solution)/shard_map/all_to_all | solution.py:248
  98.2 23.5 %copy-start.1 = (bf16[32,512,128]{2,1,0:T(8,128)(2,1)S(1)}, bf16[32,512,128]{2,1,0:T(8,128)(2,1)}, u32[]{:S(2)}) copy-start(bf16[32,512,128]{2,1,0:T(8,128)(2,1)} %copy-done) | copy-start | bytes 12582916
  98.2 4.8 %collective-permute-start.3 = (bf16[32,128,128]{2,1,0:T(8,128)(2,1)S(1)}, bf16[32,128,128]{2,1,0:T(8,128)(2,1)S(1)}, u32[]{:S(2)}, u32[]{:S(2)}) collective-permute-start(bf16[32,128,128]{2,1,0:T(8,128)(2,1)S(1)} %all-to-all-done.1.near_ref), channel_id=1, source_target_pairs={{0,8},{8,0},{1,9},{9,1},{2,10},{10,2},{3,11},{11,3},{4,12},{12,4},... | collective-permute-start | bytes 3145736 | tf_op jit(solution)/shard_map/ppermute | solution.py:240
  103.1 2.2 %copy-start.9 = (bf16[32,512,128]{2,1,0:T(8,128)(2,1)S(1)}, bf16[32,512,128]{2,1,0:T(8,128)(2,1)}, u32[]{:S(2)}) copy-start(bf16[32,512,128]{2,1,0:T(8,128)(2,1)} %copy-done.8) | copy-start | bytes 12582916
  110.4 24.8 %collective-permute-start.10 = (bf16[32,16,128]{2,1,0:T(8,128)(2,1)S(1)}, bf16[32,16,128]{2,1,0:T(8,128)(2,1)S(1)}, u32[]{:S(2)}, u32[]{:S(2)}) collective-permute-start(bf16[32,16,128]{2,1,0:T(8,128)(2,1)S(1)} %get-tuple-element.48), channel_id=1, source_target_pairs={{0,6},{1,7},{2,4},{3,5},{4,2},{5,3},{6,0},{7,1},{8,14},{9,15},{10,... | collective-permute-start | bytes 393224 | tf_op jit(solution)/shard_map/ppermute | solution.py:244
  115.6 22.3 %collective-permute-start.11 = (bf16[32,16,128]{2,1,0:T(8,128)(2,1)S(1)}, bf16[32,16,128]{2,1,0:T(8,128)(2,1)S(1)}, u32[]{:S(2)}, u32[]{:S(2)}) collective-permute-start(bf16[32,16,128]{2,1,0:T(8,128)(2,1)S(1)} %get-tuple-element.49), channel_id=1, source_target_pairs={{0,7},{1,6},{2,5},{3,4},{4,3},{5,2},{6,1},{7,0},{8,15},{9,14},{10,... | collective-permute-start | bytes 393224 | tf_op jit(solution)/shard_map/ppermute | solution.py:244
  117.6 27.5 %collective-permute-start.5 = (bf16[32,16,128]{2,1,0:T(8,128)(2,1)S(1)}, bf16[32,16,128]{2,1,0:T(8,128)(2,1)S(1)}, u32[]{:S(2)}, u32[]{:S(2)}) collective-permute-start(bf16[32,16,128]{2,1,0:T(8,128)(2,1)S(1)} %get-tuple-element.43), channel_id=1, source_target_pairs={{0,1},{1,0},{2,3},{3,2},{4,5},{5,4},{6,7},{7,6},{8,9},{9,8},{10,11... | collective-permute-start | bytes 393224 | tf_op jit(solution)/shard_map/ppermute | solution.py:244
  129.6 32.6 %collective-permute-start.4 = (bf16[32,32,128]{2,1,0:T(8,128)(2,1)S(1)}, bf16[32,32,128]{2,1,0:T(8,128)(2,1)S(1)}, u32[]{:S(2)}, u32[]{:S(2)}) collective-permute-start(bf16[32,32,128]{2,1,0:T(8,128)(2,1)S(1)} %get-tuple-element.41), channel_id=1, source_target_pairs={{0,8},{8,0},{1,9},{9,1},{2,10},{10,2},{3,11},{11,3},{4,12},{12,4},... | collective-permute-start | bytes 786440 | tf_op jit(solution)/shard_map/ppermute | solution.py:240
  131.6 15.7 %collective-permute-start.6 = (bf16[32,16,128]{2,1,0:T(8,128)(2,1)S(1)}, bf16[32,16,128]{2,1,0:T(8,128)(2,1)S(1)}, u32[]{:S(2)}, u32[]{:S(2)}) collective-permute-start(bf16[32,16,128]{2,1,0:T(8,128)(2,1)S(1)} %get-tuple-element.44), channel_id=1, source_target_pairs={{0,2},{1,3},{2,0},{3,1},{4,6},{5,7},{6,4},{7,5},{8,10},{9,11},{10,... | collective-permute-start | bytes 393224 | tf_op jit(solution)/shard_map/ppermute | solution.py:244
  135.2 12.0 %collective-permute-start.7 = (bf16[32,16,128]{2,1,0:T(8,128)(2,1)S(1)}, bf16[32,16,128]{2,1,0:T(8,128)(2,1)S(1)}, u32[]{:S(2)}, u32[]{:S(2)}) collective-permute-start(bf16[32,16,128]{2,1,0:T(8,128)(2,1)S(1)} %get-tuple-element.45), channel_id=1, source_target_pairs={{0,3},{1,2},{2,1},{3,0},{4,7},{5,6},{6,5},{7,4},{8,11},{9,10},{10,... | collective-permute-start | bytes 393224 | tf_op jit(solution)/shard_map/ppermute | solution.py:244
  137.9 11.8 %collective-permute-start.8 = (bf16[32,16,128]{2,1,0:T(8,128)(2,1)S(1)}, bf16[32,16,128]{2,1,0:T(8,128)(2,1)S(1)}, u32[]{:S(2)}, u32[]{:S(2)}) collective-permute-start(bf16[32,16,128]{2,1,0:T(8,128)(2,1)S(1)} %get-tuple-element.46), channel_id=1, source_target_pairs={{0,4},{1,5},{2,6},{3,7},{4,0},{5,1},{6,2},{7,3},{8,12},{9,13},{10,... | collective-permute-start | bytes 393224 | tf_op jit(solution)/shard_map/ppermute | solution.py:244
  145.1 17.2 %collective-permute-start.9 = (bf16[32,16,128]{2,1,0:T(8,128)(2,1)S(1)}, bf16[32,16,128]{2,1,0:T(8,128)(2,1)S(1)}, u32[]{:S(2)}, u32[]{:S(2)}) collective-permute-start(bf16[32,16,128]{2,1,0:T(8,128)(2,1)S(1)} %get-tuple-element.47), channel_id=1, source_target_pairs={{0,5},{1,4},{2,7},{3,6},{4,1},{5,0},{6,3},{7,2},{8,13},{9,12},{10,... | collective-permute-start | bytes 393224 | tf_op jit(solution)/shard_map/ppermute | solution.py:244
  163.3 25.1 %all-to-all-start.3 = ((bf16[32,48,128]{2,1,0:T(8,128)(2,1)}), bf16[32,48,128]{2,1,0:T(8,128)(2,1)S(1)}, u32[]{:S(2)}, u32[]{:S(2)}) async-start(bf16[32,48,128]{2,1,0:T(8,128)(2,1)} %shard_map.92), calls=%async_computation.3 | async-start | bytes 786432 | tf_op jit(solution)/shard_map/all_to_all | solution.py:248

commit v3 on v2

v3 whole, which is shorter than its diff:
```python
import jax
import jax.numpy as jnp
from jax import lax
from jax.experimental import pallas as pl
from jax.experimental.pallas import tpu as pltpu
from jax.sharding import Mesh
from jax.sharding import PartitionSpec as P

CAP = 5
CHIPS = 32
GROUP_SLOTS = 512
TAGS = 384
BF16 = jnp.bfloat16
F32 = jnp.float32


def iota(shape, dim):
    return lax.broadcasted_iota(jnp.int32, shape, dim)


def contract(a, b, da, db):
    return lax.dot_general(a, b, (((da,), (db,)), ((), ())), preferred_element_type=F32)


def prepare_kernel(
    blocks_any,
    rows_any,
    weights_any,
    table_any,
    grads_any,
    own_ref,
    other_ref,
    half_ref,
    out_ref,
    blocks_ref,
    rows_ref,
    weights_ref,
    table_ref,
    grads_ref,
    sems,
):
    anys = (blocks_any, rows_any, weights_any, grads_any, table_any)
    refs = (blocks_ref, rows_ref, weights_ref, grads_ref, table_ref)
    copies = [pltpu.make_async_copy(a, r, sems.at[i]) for i, (a, r) in enumerate(zip(anys, refs))]
    for copy in copies:
        copy.start()
    for copy in copies[:3]:
        copy.wait()
    tags(blocks_ref, rows_ref, weights_ref, own_ref, other_ref)
    copies[3].wait()
    for j in range(CHIPS):
        out_ref[j] = grads_ref[:, 128 * j : 128 * (j + 1)]
    copies[4].wait()
    y = lax.axis_index("y")
    for i in range(4):
        block = (((y >> 1) ^ i) << 1) | (y & 1)
        rows = pl.ds(pl.multiple_of(block * 16, 16), 16)
        for j in range(CHIPS):
            half_ref[j, 16 * i : 16 * (i + 1), :] = table_ref[rows, 128 * j : 128 * (j + 1)]


def tags(blocks_ref, rows_ref, weights_ref, own_ref, other_ref):
    core = lax.axis_index("core")
    n = 256
    owner = jnp.concatenate([blocks_ref[0:1, :], blocks_ref[1:2, :]], axis=1)
    hot = (owner == iota((64, n), 0)).astype(F32)
    upper = (iota((n, n), 0) < iota((n, n), 1)).astype(BF16)
    before = contract(hot.astype(BF16), upper, 1, 0)
    rank = jnp.sum(before * hot, axis=0, keepdims=True).astype(jnp.int32)
    half = owner & 1
    chip = owner >> 1
    rows = rows_ref[...].astype(F32).astype(BF16)
    rows = jnp.concatenate([rows[:16], rows[16:]], axis=1)
    weights = weights_ref[...].astype(BF16)
    weights = jnp.concatenate([weights[:16], weights[16:]], axis=1)
    entry = iota((CHIPS, n), 1) + 1
    lanes = iota((TAGS, n), 0)
    token_place = (lanes == 2 * CHIPS * CAP + core * CAP + rank).astype(F32).astype(BF16)
    for out, mine in ((own_ref, core), (other_ref, 1 - core)):
        slot = jnp.where(half == mine, core * (CHIPS * CAP) + chip * CAP + rank, -1)
        hits = (lanes == slot).astype(F32).astype(BF16)
        tokens = jnp.where(jnp.where(half == mine, chip, -1) == iota((CHIPS, n), 0), entry, 0)
        tokens = tokens.astype(F32).astype(BF16)
        out_tags = jnp.concatenate([contract(rows, hits, 1, 1), contract(weights, hits, 1, 1)], axis=0)
        out_tags = (out_tags + contract(tokens, token_place, 1, 1)).astype(BF16)
        for i in range(3):
            out[i] = out_tags[:, 128 * i : 128 * (i + 1)]


def first_kernel(own_ref, other_ref, half_ref, out_ref):
    tags = own_ref[...].reshape(96, 128) + other_ref[...].reshape(96, 128)
    for j in range(CHIPS):
        out_ref[j, 0:96, :] = tags
        out_ref[j, 96:160, :] = half_ref[j]


def widen(got_ref, tags_ref, wide_ref):
    for g in range(CHIPS):
        for i in range(3):
            tags_ref[g * 32 : (g + 1) * 32, 128 * i : 128 * (i + 1)] = got_ref[g, 32 * i : 32 * (i + 1), :]
    slot = iota((1, GROUP_SLOTS), 1)
    sender, rank = (slot >> 3) & 1, slot & 7
    used = rank < CAP
    lane = jnp.where(used, sender * (CHIPS * CAP) + (slot >> 4) * CAP + rank, -1)
    spread = (iota((TAGS, GROUP_SLOTS), 0) == lane).astype(F32).astype(BF16)
    lane = jnp.where(used, 2 * CHIPS * CAP - 256 + sender * CAP + rank, -1)
    spread_tokens = (iota((128, GROUP_SLOTS), 0) == lane).astype(F32).astype(BF16)
    for i in range(4):
        rows = slice(256 * i, 256 * (i + 1))
        wide_ref[rows, 0:GROUP_SLOTS] = contract(tags_ref[rows, :], spread, 1, 0)
        wide_ref[rows, GROUP_SLOTS : 2 * GROUP_SLOTS] = contract(
            tags_ref[rows, 256:384], spread_tokens, 1, 0
        )


def token_tags(wide_ref, g, shard_of):
    tokens = wide_ref[pl.ds(pl.multiple_of(g * 32, 32), 32), GROUP_SLOTS : 2 * GROUP_SLOTS]
    tag = jnp.sum(jnp.where(shard_of, tokens, 0.0), axis=0, keepdims=True)
    valid = tag > 0.5
    second_block = (tag > 128.5).astype(F32)
    return valid, tag - 1.0 - 128.0 * second_block, second_block


def slot_rows(wide_ref, g):
    rows = wide_ref[pl.ds(pl.multiple_of(g * 32, 32), 16), 0:GROUP_SLOTS]
    return (rows.astype(jnp.int32) ^ (lax.axis_index("y") * 16)).astype(F32)


def slot_masks():
    core = lax.axis_index("core")
    shard_of = iota((CHIPS, GROUP_SLOTS), 1) // 16 == iota((CHIPS, GROUP_SLOTS), 0)
    second = (iota((1, GROUP_SLOTS), 1) & 8) != 0
    return shard_of, jnp.where(second, 1 - core, core).astype(F32)


def mix_kernel(got_ref, mix_ref, pick_ref, token_ref, tags_ref, wide_ref):
    widen(got_ref, tags_ref, wide_ref)
    shard_of, far = slot_masks()
    position = iota((128, GROUP_SLOTS), 0).astype(F32).astype(BF16)

    def group(g, _):
        valid, token, second_block = token_tags(wide_ref, g, shard_of)
        quarter = (
            (token > 31.5).astype(F32) + (token > 63.5).astype(F32) + (token > 95.5).astype(F32)
        )
        token_ref[g, 0:1, :] = jnp.where(valid, far * 128.0 + token, -1.0)
        token_ref[g, 1:2, :] = jnp.where(valid, far * 32.0 + token - 32.0 * quarter, -1.0)
        part = jnp.where(valid, quarter * 2.0 + second_block, -1.0)
        rows = slot_rows(wide_ref, g)
        picks = jnp.concatenate([jnp.where(part == float(i), rows, -1.0) for i in range(8)], axis=0)
        rows = rows.astype(BF16)
        at = pl.multiple_of(g * 32 + 16, 16)
        weights = wide_ref[pl.ds(at, 16), 0:GROUP_SLOTS].astype(BF16)
        mix = jnp.zeros((128, GROUP_SLOTS), BF16)
        for k in range(16):
            mix = jnp.where(rows[k : k + 1, :] == position, weights[k : k + 1, :], mix)
        here = pl.ds(pl.multiple_of(g * 16, 16), 16)
        mix_ref[:, here, :] = mix.T.reshape(CHIPS, 16, 128)
        pick_ref[:, here, :] = picks.astype(BF16).T.reshape(CHIPS, 16, 128)
        return 0

    lax.fori_loop(0, CHIPS, group, 0, unroll=4)


def table_of(got_ref, table_ref, o):
    pieces = []
    for i in range(4):
        pieces += [got_ref[o, 96 + 16 * i : 112 + 16 * i, :], table_ref[o, 16 * i : 16 * (i + 1), :]]
    return jnp.concatenate(pieces, axis=0)


def add_kernel(near_ref, far_ref, out_ref):
    for j in range(CHIPS):
        out_ref[j] = (near_ref[j].astype(F32) + far_ref[j].astype(F32)).astype(BF16)


def value_kernel(mix_ref, token_ref, got_ref, table_ref, near_ref, far_ref, sums_ref):
    def shard(o, _):
        sums_ref[o] = contract(mix_ref[o], table_of(got_ref, table_ref, o), 1, 0).astype(BF16)
        return 0

    lax.fori_loop(0, CHIPS, shard, 0, unroll=8)
    token_rows = iota((256, GROUP_SLOTS), 0).astype(F32).astype(BF16)

    def group(g, _):
        sums = sums_ref[:, pl.ds(pl.multiple_of(g * 16, 16), 16), :].reshape(GROUP_SLOTS, 128)
        place = token_ref[g, 0:1, :].astype(BF16)
        hits = jnp.where(place == token_rows, jnp.ones((), BF16), jnp.zeros((), BF16))
        out = contract(hits, sums, 1, 0).astype(BF16)
        near_ref[g] = out[:128]
        far_ref[g] = out[128:]
        return 0

    lax.fori_loop(0, CHIPS, group, 0, unroll=8)


def gather_kernel(token_ref, near_ref, far_ref, rows_ref):
    token_rows = iota((256, GROUP_SLOTS), 0).astype(F32).astype(BF16)

    def gather(g, _):
        place = token_ref[g, 0:1, :].astype(BF16)
        hits = jnp.where(place == token_rows, jnp.ones((), BF16), jnp.zeros((), BF16))
        grads = jnp.concatenate([near_ref[g], far_ref[g]], axis=0)
        rows = contract(hits, grads, 0, 0).astype(BF16)
        rows_ref[:, pl.ds(pl.multiple_of(g * 16, 16), 16), :] = rows.reshape(CHIPS, 16, 128)
        return 0

    lax.fori_loop(0, CHIPS, gather, 0, unroll=8)


def table_grad_kernel(mix_ref, rows_ref, keep_ref, send_ref):
    def shard(o, _):
        grad = contract(mix_ref[o], rows_ref[o], 0, 0).astype(BF16)
        for m in range(8):
            (send_ref if m & 1 else keep_ref)[m >> 1, o] = grad[16 * m : 16 * (m + 1)]
        return 0

    lax.fori_loop(0, CHIPS, shard, 0, unroll=8)


def fold_kernel(keep_ref, got_ref, *out_refs):
    for i, out_ref in enumerate(out_refs):
        for j in range(CHIPS):
            out_ref[j] = (keep_ref[i, j].astype(F32) + got_ref[i, j].astype(F32)).astype(BF16)


def weight_grad_kernel(rows_ref, pick_ref, token_ref, got_ref, table_ref, near_ref, far_ref, found_ref):
    def shard(o, _):
        scores = contract(rows_ref[o], table_of(got_ref, table_ref, o), 1, 1)
        picks = pick_ref[o].astype(F32).astype(jnp.int32)
        found = jnp.take_along_axis(scores, jnp.maximum(picks, 0), axis=1, mode="promise_in_bounds")
        found_ref[o] = jnp.where(picks >= 0, found, 0.0).astype(BF16)
        return 0

    lax.fori_loop(0, CHIPS, shard, 0, unroll=8)
    fold_rows = iota((64, GROUP_SLOTS), 0).astype(F32).astype(BF16)

    def group(g, _):
        found = found_ref[:, pl.ds(pl.multiple_of(g * 16, 16), 16), :].reshape(GROUP_SLOTS, 128)
        place = token_ref[g, 1:2, :].astype(BF16)
        hits = jnp.where(place == fold_rows, jnp.ones((), BF16), jnp.zeros((), BF16))
        out = contract(hits, found, 1, 0).astype(BF16)
        near_ref[g] = out[:32]
        far_ref[g] = out[32:]
        return 0

    lax.fori_loop(0, CHIPS, group, 0, unroll=8)


def last_kernel(near_ref, far_ref, *refs):
    out_ref = refs[-1]
    for j in range(CHIPS):
        out_ref[j, 0:32, :] = (near_ref[j].astype(F32) + far_ref[j].astype(F32)).astype(BF16)
        total = refs[0][j].astype(F32)
        for ref in refs[1:-1]:
            total += ref[j].astype(F32)
        out_ref[j, 32:48, :] = total.astype(BF16)


def finish_kernel(got_ref, weight_ref, table_ref):
    def add(j, total):
        return total + got_ref[j, 0:32, :].astype(F32)

    total = lax.fori_loop(0, CHIPS, add, jnp.zeros((32, 128), F32), unroll=8)
    total = jnp.concatenate([total[:, 32 * i : 32 * (i + 1)] for i in range(4)], axis=0)
    weight_ref[...] = total.T.astype(BF16)
    for j in range(CHIPS):
        table_ref[:, 128 * j : 128 * (j + 1)] = got_ref[j, 32:48, :]


def call(kernel, out_shapes, *operands, us=1, scratch=(), limit=16, spaces=()):
    vmem = pl.BlockSpec(memory_space=pltpu.VMEM)
    outs = tuple(s if isinstance(s, jax.ShapeDtypeStruct) else jax.ShapeDtypeStruct(s, BF16) for s in out_shapes)
    return pl.pallas_call(
        kernel,
        out_shape=outs,
        in_specs=[pl.BlockSpec(memory_space=s) for s in spaces] + [vmem] * (len(operands) - len(spaces)),
        out_specs=tuple(vmem for _ in outs),
        scratch_shapes=scratch,
        compiler_params=pltpu.CompilerParams(vmem_limit_bytes=limit * 2**20),
        cost_estimate=pl.CostEstimate(
            flops=0, bytes_accessed=int(us * 3.3e6), transcendentals=0
        ),
    )(*operands)


def swap_cores(v):
    return lax.ppermute(v, "core", [(0, 1), (1, 0)])


def across(v, bits):
    return lax.ppermute(v, "y", [(i, i ^ bits) for i in range(8)])


def exchange(v):
    return lax.all_to_all(v, ("x", "z"), split_axis=0, concat_axis=0, tiled=True)


def after(v, *others):
    return lax.optimization_barrier((v, *others))[0]


def on_device(key_blocks, key_rows, weights, value_table, cotangent):
    own, other, half, grads = call(
        prepare_kernel,
        [(3, 32, 128)] * 2 + [(CHIPS, 64, 128), (CHIPS, 128, 128)],
        key_blocks.T,
        key_rows.T,
        weights.T,
        value_table,
        cotangent,
        us=2,
        scratch=[
            pltpu.VMEM((2, 128), jnp.int32),
            pltpu.VMEM((32, 128), jnp.int32),
            pltpu.VMEM((32, 128), F32),
            pltpu.VMEM((128, 4096), BF16),
            pltpu.VMEM((128, 4096), BF16),
            pltpu.SemaphoreType.DMA((5,)),
        ],
        limit=60,
        spaces=[pl.ANY] * 5,
    )
    other = swap_cores(other)
    (first,) = call(first_kernel, [(CHIPS, 160, 128)], own, other, half, us=0.4)
    got = exchange(first)
    near_grads = exchange(after(grads, got))

    table = across(got[:, 96:, :], 1)
    mix, picks, tokens = call(
        mix_kernel,
        [(CHIPS, GROUP_SLOTS, 128)] * 2 + [jax.ShapeDtypeStruct((CHIPS, 8, GROUP_SLOTS), F32)],
        got,
        us=8.5,
        scratch=[
            pltpu.VMEM((CHIPS * 32, TAGS), BF16),
            pltpu.VMEM((CHIPS * 32, 2 * GROUP_SLOTS), F32),
        ],
    )
    near, far = call(
        value_kernel,
        [(CHIPS, 128, 128)] * 2,
        mix,
        tokens,
        got,
        table,
        us=4.5,
        scratch=[pltpu.VMEM((CHIPS, GROUP_SLOTS, 128), BF16)],
    )
    (out,) = call(add_kernel, [(CHIPS, 128, 128)], near, swap_cores(far), us=0.3)
    got_out = exchange(after(out, near_grads))

    (rows,) = call(
        gather_kernel,
        [(CHIPS, GROUP_SLOTS, 128)],
        tokens,
        near_grads,
        swap_cores(near_grads),
        us=3,
    )
    keep, send = call(table_grad_kernel, [(4, CHIPS, 16, 128)] * 2, mix, rows, us=2.5)
    near, far = call(
        weight_grad_kernel,
        [(CHIPS, 32, 128)] * 2,
        rows,
        picks,
        tokens,
        got,
        table,
        us=8,
        scratch=[pltpu.VMEM((CHIPS, GROUP_SLOTS, 128), BF16)],
    )
    halves = call(fold_kernel, [(CHIPS, 16, 128)] * 4, keep, across(send, 1), us=0.3)
    parts = [halves[0]] + [across(halves[i], 2 * i) for i in (2, 1, 3)]
    (last,) = call(last_kernel, [(CHIPS, 48, 128)], near, swap_cores(far), *parts, us=0.8)
    got_last = exchange(after(last, got_out))
    memory_out = jnp.transpose(got_out, (1, 0, 2)).reshape(128, 4096)
    weight_out, table_out = call(finish_kernel, [(32, 128), (16, 4096)], got_last)
    return memory_out, weight_out.T, table_out


def solution(mesh):
    fine = Mesh(mesh.devices.reshape(4, 8, 2, 8), ("x", "z", "core", "y"))
    tokens = P(("x", "z", "core", "y"), None)
    return jax.shard_map(
        on_device,
        mesh=fine,
        in_specs=(tokens, tokens, tokens, P(("x", "z", "core"), None), tokens),
        out_specs=(tokens, tokens, tokens),
        check_vma=False,
    )
```

time: 190 us -> 171 us (0.900)
  waiting for transfers between devices: 38.6 us -> 30.8 us
  starting transfers between devices: 58 us -> 50.3 us
  local copies, waits for them, and re-layouts: 12.6 us -> 8.73 us
  Pallas kernels: 29.9 us -> 31.9 us
    ppermute x8 -> x5, starting transfers between devices: 30.4 us -> 19.3 us  [across(): return lax.ppermute(v, 'y', [(i, i ^ bits) for i in range(8)])]
    all_to_all x3, waiting for transfers between devices: 18.3 us -> 11.8 us  [exchange(): lax.all_to_all(v, ('x', 'z'), split_axis=0, concat_axis=0, tiled=True)]
    all_to_all x3, starting transfers between devices: 19.6 us -> 23.1 us  [exchange(): lax.all_to_all(v, ('x', 'z'), split_axis=0, concat_axis=0, tiled=True)]
    unnamed x21 -> x13, local copies, waits for them, and re-layouts: 10.1 us -> 7.05 us
    ppermute x8 -> x5, waiting for transfers between devices: 15 us -> 12.4 us  [across(): return lax.ppermute(v, 'y', [(i, i ^ bits) for i in range(8)])]
    pallas_call x9 -> x11, Pallas kernels: 29.9 us -> 31.9 us  [call(): pl.pallas_call(kernel, out_shape=outs, in_specs=[pl.BlockSpec(memory_spac...]
  transfers between devices with their start and end apart: 15 -> 12, of which waited for: 6 -> 10; matrix products, arithmetic and copies ran while one was open for 2% -> 2% of each run, Pallas kernels for 15% -> 17%
where the time goes in v3:
time: 171 us; the launch traced here: 170 us
  starting transfers between devices  50.3 us (29%)
  blocking collectives  47.5 us (28%)
  Pallas kernels  31.9 us (19%)
  waiting for transfers between devices  30.8 us (18%)
  local copies, waits for them, and re-layouts  8.73 us (5%)
    all_to_all x1, blocking collectives, exchange(): lax.all_to_all(v, ('x', 'z'), split_axis=0, concat_axis=0, tiled=True)  47.5 us
    pallas_call x11, Pallas kernels, call(): pl.pallas_call(kernel, out_shape=outs, in_specs=[pl.BlockSpec(memory_spac...  31.9 us
    all_to_all x3, starting transfers between devices, exchange(): lax.all_to_all(v, ('x', 'z'), split_axis=0, concat_axis=0, tiled=True)  23.1 us
    ppermute x5, starting transfers between devices, across(): return lax.ppermute(v, 'y', [(i, i ^ bits) for i in range(8)])  19.3 us
    ppermute x5, waiting for transfers between devices, across(): return lax.ppermute(v, 'y', [(i, i ^ bits) for i in range(8)])  12.4 us
    all_to_all x3, waiting for transfers between devices, exchange(): lax.all_to_all(v, ('x', 'z'), split_axis=0, concat_axis=0, tiled=True)  11.8 us
    ppermute x4, starting transfers between devices, swap_cores(): return lax.ppermute(v, 'core', [(0, 1), (1, 0)])  7.93 us
    unnamed x13, local copies, waits for them, and re-layouts  7.05 us
  transfers between devices with their start and end apart: 12, of which 10 were waited for; matrix products, arithmetic and copies ran while one was open for 2% of the time, Pallas kernels for 17%

profile of v3, /device:TPU:64, one launch (start us, length us, event | category | flops | bytes accessed | tf_op | source)
XLA Modules:
  0.0 170.1 jit_solution(18431104654681564088)
XLA Ops:
  0.6 2.9 %shard_map.76 = (bf16[3,32,128]{2,1,0:T(8,128)(2,1)}, bf16[3,32,128]{2,1,0:T(8,128)(2,1)}, bf16[32,64,128]{2,1,0:T(8,128)(2,1)}, bf16[32,128,128]{2,1,0:T(8,128)(2,1)}) custom-call(s32[2,128]{1,0:T(2,128)} %bitcast.9, s32[32,128]{1,0:T(8,128)} %bitcast.7, f32[32,128]{1,0:T(8,128)} %bitcast.8, bf16[128,4096]{1,0:T(8,128)(2,1)} %table_any.1, ...), custom_call_target="tpu_custom_call" | custom-call | bytes 6600000 | tf_op jit(solution)/shard_map/pallas_call | solution.py:274
  3.5 1.9 %collective-permute-start = (bf16[3,32,128]{2,1,0:T(8,128)(2,1)}, bf16[3,32,128]{2,1,0:T(8,128)(2,1)S(1)}, u32[]{:S(2)}, u32[]{:S(2)}) collective-permute-start(bf16[3,32,128]{2,1,0:T(8,128)(2,1)} %get-tuple-element.26), channel_id=1, source_target_pairs={{0,8},{8,0},{1,9},{9,1},{2,10},{10,2},{3,11},{11,3},{4,12},{12,4},... | collective-permute-start | bytes 73736 | tf_op jit(solution)/shard_map/ppermute | solution.py:288
  5.5 1.4 collective-permute-done.other_ref
  6.8 1.0 copy-done.4
  7.9 0.7 copy-done.5
  8.6 0.1 shard_map.77
  8.7 47.5 %all_to_all.20.got_ref = bf16[32,160,128]{2,1,0:T(8,128)(2,1)S(1)} all-to-all(bf16[32,160,128]{2,1,0:T(8,128)(2,1)S(1)} %shard_map.77), channel_id=1, replica_groups=mesh['x'=4,'z'=8,'core'=2,'y'=8] {'x','z'}, dimensions={0} | all-to-all | bytes 2621440 | tf_op jit(solution)/shard_map/all_to_all | solution.py:296
  56.2 4.6 %all-to-all-start.1 = ((bf16[32,128,128]{2,1,0:T(8,128)(2,1)}), bf16[32,128,128]{2,1,0:T(8,128)(2,1)S(1)}, u32[]{:S(2)}, u32[]{:S(2)}) async-start(bf16[32,128,128]{2,1,0:T(8,128)(2,1)} %get-tuple-element.33), calls=%async_computation.1 | async-start | bytes 2097152 | tf_op jit(solution)/shard_map/all_to_all | solution.py:296
  60.8 0.1 slice.4
  60.8 3.5 %collective-permute-start.1 = (bf16[32,64,128]{2,1,0:T(8,128)(2,1)S(1)}, bf16[32,64,128]{2,1,0:T(8,128)(2,1)S(1)}, u32[]{:S(2)}, u32[]{:S(2)}) collective-permute-start(bf16[32,64,128]{2,1,0:T(8,128)(2,1)S(1)} %slice.4), channel_id=1, source_target_pairs={{0,1},{1,0},{2,3},{3,2},{4,5},{5,4},{6,7},{7,6},{8,9},{9,8},{10,11... | collective-permute-start | bytes 1572872 | tf_op jit(solution)/shard_map/ppermute | solution.py:292
  64.3 8.4 %shard_map.78 = (bf16[32,512,128]{2,1,0:T(8,128)(2,1)S(1)}, bf16[32,512,128]{2,1,0:T(8,128)(2,1)S(1)}, f32[32,8,512]{2,1,0:T(8,128)S(1)}) custom-call(bf16[32,160,128]{2,1,0:T(8,128)(2,1)S(1)} %all_to_all.20.got_ref), custom_call_target="tpu_custom_call" | custom-call | bytes 28050000 | tf_op jit(solution)/shard_map/pallas_call | solution.py:274
  72.7 0.0 copy-start.2
  72.7 1.9 %copy-done.2 = bf16[32,512,128]{2,1,0:T(8,128)(2,1)} copy-done((bf16[32,512,128]{2,1,0:T(8,128)(2,1)}, bf16[32,512,128]{2,1,0:T(8,128)(2,1)S(1)}, u32[]{:S(2)}) %copy-start.2) | copy-done | bytes 4194328
  74.7 1.0 collective-permute-done.1.table_ref
  75.6 4.5 %shard_map.79 = (bf16[32,128,128]{2,1,0:T(8,128)(2,1)S(1)}, bf16[32,128,128]{2,1,0:T(8,128)(2,1)S(1)}) custom-call(bf16[32,512,128]{2,1,0:T(8,128)(2,1)S(1)} %get-tuple-element.28.mix_ref, f32[32,8,512]{2,1,0:T(8,128)S(1)} %get-tuple-element.29.token_ref, bf16[32,160,128]{2,1,0:T(8,128)(2,1)S(1)} %all_to_all.20.got_ref, ...), custom_call_target="tpu_custom_call" | custom-call | bytes 14850000 | tf_op jit(solution)/shard_map/pallas_call | solution.py:274
  80.1 0.0 copy-start
  80.1 2.0 %copy-done = bf16[32,512,128]{2,1,0:T(8,128)(2,1)} copy-done((bf16[32,512,128]{2,1,0:T(8,128)(2,1)}, bf16[32,512,128]{2,1,0:T(8,128)(2,1)S(1)}, u32[]{:S(2)}) %copy-start) | copy-done | bytes 4194328
  82.1 1.9 %collective-permute-start.2 = (bf16[32,128,128]{2,1,0:T(8,128)(2,1)S(1)}, bf16[32,128,128]{2,1,0:T(8,128)(2,1)S(1)}, u32[]{:S(2)}, u32[]{:S(2)}) collective-permute-start(bf16[32,128,128]{2,1,0:T(8,128)(2,1)S(1)} %get-tuple-element.31), channel_id=1, source_target_pairs={{0,8},{8,0},{1,9},{9,1},{2,10},{10,2},{3,11},{11,3},{4,12},{12,4},... | collective-permute-start | bytes 3145736 | tf_op jit(solution)/shard_map/ppermute | solution.py:288
  84.1 2.6 %collective-permute-done.2.far_ref = bf16[32,128,128]{2,1,0:T(8,128)(2,1)S(1)} collective-permute-done((bf16[32,128,128]{2,1,0:T(8,128)(2,1)S(1)}, bf16[32,128,128]{2,1,0:T(8,128)(2,1)S(1)}, u32[]{:S(2)}, u32[]{:S(2)}) %collective-permute-start.2) | collective-permute-done | bytes 1048608 | tf_op jit(solution)/shard_map/ppermute | solution.py:288
  86.7 1.2 shard_map.80
  87.9 1.2 all-to-all-done.1.near_ref
  89.1 8.7 %all-to-all-start.2 = ((bf16[32,128,128]{2,1,0:T(8,128)(2,1)}), bf16[32,128,128]{2,1,0:T(8,128)(2,1)}, u32[]{:S(2)}, u32[]{:S(2)}) async-start(bf16[32,128,128]{2,1,0:T(8,128)(2,1)} %shard_map.80), calls=%async_computation.2 | async-start | bytes 2097152 | tf_op jit(solution)/shard_map/all_to_all | solution.py:296
  97.8 0.0 copy-start.1
  97.8 2.2 %collective-permute-start.3 = (bf16[32,128,128]{2,1,0:T(8,128)(2,1)S(1)}, bf16[32,128,128]{2,1,0:T(8,128)(2,1)S(1)}, u32[]{:S(2)}, u32[]{:S(2)}) collective-permute-start(bf16[32,128,128]{2,1,0:T(8,128)(2,1)S(1)} %all-to-all-done.1.near_ref), channel_id=1, source_target_pairs={{0,8},{8,0},{1,9},{9,1},{2,10},{10,2},{3,11},{11,3},{4,12},{12,4},... | collective-permute-start | bytes 3145736 | tf_op jit(solution)/shard_map/ppermute | solution.py:288
  100.0 2.6 %collective-permute-done.3.far_ref = bf16[32,128,128]{2,1,0:T(8,128)(2,1)S(1)} collective-permute-done((bf16[32,128,128]{2,1,0:T(8,128)(2,1)S(1)}, bf16[32,128,128]{2,1,0:T(8,128)(2,1)S(1)}, u32[]{:S(2)}, u32[]{:S(2)}) %collective-permute-start.3) | collective-permute-done | bytes 1048608 | tf_op jit(solution)/shard_map/ppermute | solution.py:288
  102.6 3.1 %shard_map.81.rows_ref = bf16[32,512,128]{2,1,0:T(8,128)(2,1)S(1)} custom-call(f32[32,8,512]{2,1,0:T(8,128)S(1)} %get-tuple-element.29.token_ref, bf16[32,128,128]{2,1,0:T(8,128)(2,1)S(1)} %all-to-all-done.1.near_ref, bf16[32,128,128]{2,1,0:T(8,128)(2,1)S(1)} %collective-permute-done.3.far_ref), custom_call_target="tpu_custom_call" | custom-call | bytes 9900000 | tf_op jit(solution)/shard_map/pallas_call | solution.py:274
  105.8 0.0 copy-done.1
  105.8 0.0 copy-start.3
  105.8 1.9 %shard_map.83 = (bf16[4,32,16,128]{3,2,1,0:T(8,128)(2,1)S(1)}, bf16[4,32,16,128]{3,2,1,0:T(8,128)(2,1)S(1)}) custom-call(bf16[32,512,128]{2,1,0:T(8,128)(2,1)S(1)} %copy-done.1, bf16[32,512,128]{2,1,0:T(8,128)(2,1)S(1)} %shard_map.81.rows_ref), custom_call_target="tpu_custom_call" | custom-call | bytes 8250000 | tf_op jit(solution)/shard_map/pallas_call | solution.py:274
  107.7 3.5 %collective-permute-start.5 = (bf16[4,32,16,128]{3,2,1,0:T(8,128)(2,1)S(1)}, bf16[4,32,16,128]{3,2,1,0:T(8,128)(2,1)S(1)}, u32[]{:S(2)}, u32[]{:S(2)}) collective-permute-start(bf16[4,32,16,128]{3,2,1,0:T(8,128)(2,1)S(1)} %get-tuple-element.39), channel_id=1, source_target_pairs={{0,1},{1,0},{2,3},{3,2},{4,5},{5,4},{6,7},{7,6},{8,9},{9,8},{10,11... | collective-permute-start | bytes 1572872 | tf_op jit(solution)/shard_map/ppermute | solution.py:292
  111.2 7.9 %shard_map.82 = (bf16[32,32,128]{2,1,0:T(8,128)(2,1)S(1)}, bf16[32,32,128]{2,1,0:T(8,128)(2,1)S(1)}) custom-call(bf16[32,512,128]{2,1,0:T(8,128)(2,1)S(1)} %shard_map.81.rows_ref, bf16[32,512,128]{2,1,0:T(8,128)(2,1)S(1)} %copy-done.3, f32[32,8,512]{2,1,0:T(8,128)S(1)} %get-tuple-element.29.token_ref, bf16[32,160,128]{2,1,0:T(8,128)(2,1)S(1)} %all_to_all.20.got_ref, ...), custom_call_target="tpu_custom_call" | custom-call | bytes 26400000 | tf_op jit(solution)/shard_map/pallas_call | solution.py:274
  119.2 1.9 %collective-permute-start.4 = (bf16[32,32,128]{2,1,0:T(8,128)(2,1)S(1)}, bf16[32,32,128]{2,1,0:T(8,128)(2,1)S(1)}, u32[]{:S(2)}, u32[]{:S(2)}) collective-permute-start(bf16[32,32,128]{2,1,0:T(8,128)(2,1)S(1)} %get-tuple-element.37), channel_id=1, source_target_pairs={{0,8},{8,0},{1,9},{9,1},{2,10},{10,2},{3,11},{11,3},{4,12},{12,4},... | collective-permute-start | bytes 786440 | tf_op jit(solution)/shard_map/ppermute | solution.py:288
  121.1 2.5 %collective-permute-done.5.got_ref = bf16[4,32,16,128]{3,2,1,0:T(8,128)(2,1)S(1)} collective-permute-done((bf16[4,32,16,128]{3,2,1,0:T(8,128)(2,1)S(1)}, bf16[4,32,16,128]{3,2,1,0:T(8,128)(2,1)S(1)}, u32[]{:S(2)}, u32[]{:S(2)}) %collective-permute-start.5) | collective-permute-done | bytes 524320 | tf_op jit(solution)/shard_map/ppermute | solution.py:292
  123.6 0.1 shard_map.84
  123.7 7.7 %collective-permute-start.6 = (bf16[32,16,128]{2,1,0:T(8,128)(2,1)S(1)}, bf16[32,16,128]{2,1,0:T(8,128)(2,1)S(1)}, u32[]{:S(2)}, u32[]{:S(2)}) collective-permute-start(bf16[32,16,128]{2,1,0:T(8,128)(2,1)S(1)} %get-tuple-element.41), channel_id=1, source_target_pairs={{0,4},{1,5},{2,6},{3,7},{4,0},{5,1},{6,2},{7,3},{8,12},{9,13},{10,... | collective-permute-start | bytes 393224 | tf_op jit(solution)/shard_map/ppermute | solution.py:292
  131.5 2.7 %collective-permute-start.7 = (bf16[32,16,128]{2,1,0:T(8,128)(2,1)S(1)}, bf16[32,16,128]{2,1,0:T(8,128)(2,1)S(1)}, u32[]{:S(2)}, u32[]{:S(2)}) collective-permute-start(bf16[32,16,128]{2,1,0:T(8,128)(2,1)S(1)} %get-tuple-element.42), channel_id=1, source_target_pairs={{0,2},{1,3},{2,0},{3,1},{4,6},{5,7},{6,4},{7,5},{8,10},{9,11},{10,... | collective-permute-start | bytes 393224 | tf_op jit(solution)/shard_map/ppermute | solution.py:292
  134.2 1.9 %collective-permute-start.8 = (bf16[32,16,128]{2,1,0:T(8,128)(2,1)S(1)}, bf16[32,16,128]{2,1,0:T(8,128)(2,1)S(1)}, u32[]{:S(2)}, u32[]{:S(2)}) collective-permute-start(bf16[32,16,128]{2,1,0:T(8,128)(2,1)S(1)} %get-tuple-element.43), channel_id=1, source_target_pairs={{0,6},{1,7},{2,4},{3,5},{4,2},{5,3},{6,0},{7,1},{8,14},{9,15},{10,... | collective-permute-start | bytes 393224 | tf_op jit(solution)/shard_map/ppermute | solution.py:292
  136.1 0.0 collective-permute-done.4.far_ref
  136.1 1.2 collective-permute-done.6.refs_1_
  137.3 6.1 %collective-permute-done.7.refs_2_ = bf16[32,16,128]{2,1,0:T(8,128)(2,1)S(1)} collective-permute-done((bf16[32,16,128]{2,1,0:T(8,128)(2,1)S(1)}, bf16[32,16,128]{2,1,0:T(8,128)(2,1)S(1)}, u32[]{:S(2)}, u32[]{:S(2)}) %collective-permute-start.7) | collective-permute-done | bytes 131104 | tf_op jit(solution)/shard_map/ppermute | solution.py:292
  143.5 1.6 collective-permute-done.8.refs_3_
  145.1 0.9 shard_map.85
  146.0 0.0 all-to-all-done.2
  146.0 9.8 %all-to-all-start.3 = ((bf16[32,48,128]{2,1,0:T(8,128)(2,1)}), bf16[32,48,128]{2,1,0:T(8,128)(2,1)S(1)}, u32[]{:S(2)}, u32[]{:S(2)}) async-start(bf16[32,48,128]{2,1,0:T(8,128)(2,1)} %shard_map.85), calls=%async_computation.3 | async-start | bytes 786432 | tf_op jit(solution)/shard_map/all_to_all | solution.py:296
  155.8 1.6 copy.8
  157.4 1.3 copy.9
  158.7 10.6 %all-to-all-done.3.got_ref = bf16[32,48,128]{2,1,0:T(8,128)(2,1)S(1)} async-done(((bf16[32,48,128]{2,1,0:T(8,128)(2,1)}), bf16[32,48,128]{2,1,0:T(8,128)(2,1)S(1)}, u32[]{:S(2)}, u32[]{:S(2)}) %all-to-all-start.3) | async-done | bytes 393248 | tf_op jit(solution)/shard_map/all_to_all | solution.py:296
  169.3 0.8 shard_map.86
  (3 shorter events, 0.0 us)
Async XLA Ops:
  3.5 3.3 %collective-permute-start = (bf16[3,32,128]{2,1,0:T(8,128)(2,1)}, bf16[3,32,128]{2,1,0:T(8,128)(2,1)S(1)}, u32[]{:S(2)}, u32[]{:S(2)}) collective-permute-start(bf16[3,32,128]{2,1,0:T(8,128)(2,1)} %get-tuple-element.26), channel_id=1, source_target_pairs={{0,8},{8,0},{1,9},{9,1},{2,10},{10,2},{3,11},{11,3},{4,12},{12,4},... | collective-permute-start | bytes 73736 | tf_op jit(solution)/shard_map/ppermute | solution.py:288
  6.8 1.0 copy-start.4
  7.9 0.7 copy-start.5
  56.2 32.9 %all-to-all-start.1 = ((bf16[32,128,128]{2,1,0:T(8,128)(2,1)}), bf16[32,128,128]{2,1,0:T(8,128)(2,1)S(1)}, u32[]{:S(2)}, u32[]{:S(2)}) async-start(bf16[32,128,128]{2,1,0:T(8,128)(2,1)} %get-tuple-element.33), calls=%async_computation.1 | async-start | bytes 2097152 | tf_op jit(solution)/shard_map/all_to_all | solution.py:296
  60.8 14.8 %collective-permute-start.1 = (bf16[32,64,128]{2,1,0:T(8,128)(2,1)S(1)}, bf16[32,64,128]{2,1,0:T(8,128)(2,1)S(1)}, u32[]{:S(2)}, u32[]{:S(2)}) collective-permute-start(bf16[32,64,128]{2,1,0:T(8,128)(2,1)S(1)} %slice.4), channel_id=1, source_target_pairs={{0,1},{1,0},{2,3},{3,2},{4,5},{5,4},{6,7},{7,6},{8,9},{9,8},{10,11... | collective-permute-start | bytes 1572872 | tf_op jit(solution)/shard_map/ppermute | solution.py:292
  72.7 2.0 %copy-start.2 = (bf16[32,512,128]{2,1,0:T(8,128)(2,1)}, bf16[32,512,128]{2,1,0:T(8,128)(2,1)S(1)}, u32[]{:S(2)}) copy-start(bf16[32,512,128]{2,1,0:T(8,128)(2,1)S(1)} %get-tuple-element.35.pick_ref) | copy-start | bytes 12582916
  80.1 2.0 %copy-start = (bf16[32,512,128]{2,1,0:T(8,128)(2,1)}, bf16[32,512,128]{2,1,0:T(8,128)(2,1)S(1)}, u32[]{:S(2)}) copy-start(bf16[32,512,128]{2,1,0:T(8,128)(2,1)S(1)} %get-tuple-element.28.mix_ref) | copy-start | bytes 12582916
  82.1 4.5 %collective-permute-start.2 = (bf16[32,128,128]{2,1,0:T(8,128)(2,1)S(1)}, bf16[32,128,128]{2,1,0:T(8,128)(2,1)S(1)}, u32[]{:S(2)}, u32[]{:S(2)}) collective-permute-start(bf16[32,128,128]{2,1,0:T(8,128)(2,1)S(1)} %get-tuple-element.31), channel_id=1, source_target_pairs={{0,8},{8,0},{1,9},{9,1},{2,10},{10,2},{3,11},{11,3},{4,12},{12,4},... | collective-permute-start | bytes 3145736 | tf_op jit(solution)/shard_map/ppermute | solution.py:288
  89.1 56.9 %all-to-all-start.2 = ((bf16[32,128,128]{2,1,0:T(8,128)(2,1)}), bf16[32,128,128]{2,1,0:T(8,128)(2,1)}, u32[]{:S(2)}, u32[]{:S(2)}) async-start(bf16[32,128,128]{2,1,0:T(8,128)(2,1)} %shard_map.80), calls=%async_computation.2 | async-start | bytes 2097152 | tf_op jit(solution)/shard_map/all_to_all | solution.py:296
  97.8 8.0 %copy-start.1 = (bf16[32,512,128]{2,1,0:T(8,128)(2,1)S(1)}, bf16[32,512,128]{2,1,0:T(8,128)(2,1)}, u32[]{:S(2)}) copy-start(bf16[32,512,128]{2,1,0:T(8,128)(2,1)} %copy-done) | copy-start | bytes 12582916
  97.8 4.8 %collective-permute-start.3 = (bf16[32,128,128]{2,1,0:T(8,128)(2,1)S(1)}, bf16[32,128,128]{2,1,0:T(8,128)(2,1)S(1)}, u32[]{:S(2)}, u32[]{:S(2)}) collective-permute-start(bf16[32,128,128]{2,1,0:T(8,128)(2,1)S(1)} %all-to-all-done.1.near_ref), channel_id=1, source_target_pairs={{0,8},{8,0},{1,9},{9,1},{2,10},{10,2},{3,11},{11,3},{4,12},{12,4},... | collective-permute-start | bytes 3145736 | tf_op jit(solution)/shard_map/ppermute | solution.py:288
  105.8 5.5 %copy-start.3 = (bf16[32,512,128]{2,1,0:T(8,128)(2,1)S(1)}, bf16[32,512,128]{2,1,0:T(8,128)(2,1)}, u32[]{:S(2)}) copy-start(bf16[32,512,128]{2,1,0:T(8,128)(2,1)} %copy-done.2) | copy-start | bytes 12582916
  107.7 15.9 %collective-permute-start.5 = (bf16[4,32,16,128]{3,2,1,0:T(8,128)(2,1)S(1)}, bf16[4,32,16,128]{3,2,1,0:T(8,128)(2,1)S(1)}, u32[]{:S(2)}, u32[]{:S(2)}) collective-permute-start(bf16[4,32,16,128]{3,2,1,0:T(8,128)(2,1)S(1)} %get-tuple-element.39), channel_id=1, source_target_pairs={{0,1},{1,0},{2,3},{3,2},{4,5},{5,4},{6,7},{7,6},{8,9},{9,8},{10,11... | collective-permute-start | bytes 1572872 | tf_op jit(solution)/shard_map/ppermute | solution.py:292
  119.2 16.9 %collective-permute-start.4 = (bf16[32,32,128]{2,1,0:T(8,128)(2,1)S(1)}, bf16[32,32,128]{2,1,0:T(8,128)(2,1)S(1)}, u32[]{:S(2)}, u32[]{:S(2)}) collective-permute-start(bf16[32,32,128]{2,1,0:T(8,128)(2,1)S(1)} %get-tuple-element.37), channel_id=1, source_target_pairs={{0,8},{8,0},{1,9},{9,1},{2,10},{10,2},{3,11},{11,3},{4,12},{12,4},... | collective-permute-start | bytes 786440 | tf_op jit(solution)/shard_map/ppermute | solution.py:288
  123.7 13.6 %collective-permute-start.6 = (bf16[32,16,128]{2,1,0:T(8,128)(2,1)S(1)}, bf16[32,16,128]{2,1,0:T(8,128)(2,1)S(1)}, u32[]{:S(2)}, u32[]{:S(2)}) collective-permute-start(bf16[32,16,128]{2,1,0:T(8,128)(2,1)S(1)} %get-tuple-element.41), channel_id=1, source_target_pairs={{0,4},{1,5},{2,6},{3,7},{4,0},{5,1},{6,2},{7,3},{8,12},{9,13},{10,... | collective-permute-start | bytes 393224 | tf_op jit(solution)/shard_map/ppermute | solution.py:292
  131.5 12.0 %collective-permute-start.7 = (bf16[32,16,128]{2,1,0:T(8,128)(2,1)S(1)}, bf16[32,16,128]{2,1,0:T(8,128)(2,1)S(1)}, u32[]{:S(2)}, u32[]{:S(2)}) collective-permute-start(bf16[32,16,128]{2,1,0:T(8,128)(2,1)S(1)} %get-tuple-element.42), channel_id=1, source_target_pairs={{0,2},{1,3},{2,0},{3,1},{4,6},{5,7},{6,4},{7,5},{8,10},{9,11},{10,... | collective-permute-start | bytes 393224 | tf_op jit(solution)/shard_map/ppermute | solution.py:292
  134.2 10.9 %collective-permute-start.8 = (bf16[32,16,128]{2,1,0:T(8,128)(2,1)S(1)}, bf16[32,16,128]{2,1,0:T(8,128)(2,1)S(1)}, u32[]{:S(2)}, u32[]{:S(2)}) collective-permute-start(bf16[32,16,128]{2,1,0:T(8,128)(2,1)S(1)} %get-tuple-element.43), channel_id=1, source_target_pairs={{0,6},{1,7},{2,4},{3,5},{4,2},{5,3},{6,0},{7,1},{8,14},{9,15},{10,... | collective-permute-start | bytes 393224 | tf_op jit(solution)/shard_map/ppermute | solution.py:292
  146.0 23.4 %all-to-all-start.3 = ((bf16[32,48,128]{2,1,0:T(8,128)(2,1)}), bf16[32,48,128]{2,1,0:T(8,128)(2,1)S(1)}, u32[]{:S(2)}, u32[]{:S(2)}) async-start(bf16[32,48,128]{2,1,0:T(8,128)(2,1)} %shard_map.85), calls=%async_computation.3 | async-start | bytes 786432 | tf_op jit(solution)/shard_map/all_to_all | solution.py:296

commit v4 on v3

--- a/solution.py
+++ b/solution.py
@@ -279,7 +279,7 @@
         scratch_shapes=scratch,
         compiler_params=pltpu.CompilerParams(vmem_limit_bytes=limit * 2**20),
         cost_estimate=pl.CostEstimate(
-            flops=0, bytes_accessed=int(us * 3.3e6), transcendentals=0
+            flops=int(us * 1e9), bytes_accessed=int(us * 3.3e6), transcendentals=0
         ),
     )(*operands)
 

time: 171 us -> 168 us (0.982)
  starting transfers between devices: 50.3 us -> 46.6 us
  Pallas kernels: 31.9 us -> 34.6 us
  local copies, waits for them, and re-layouts: 8.73 us -> 6.98 us
    all_to_all x3, waiting for transfers between devices: 11.8 us -> 17.7 us  [exchange(): lax.all_to_all(v, ('x', 'z'), split_axis=0, concat_axis=0, tiled=True)]
    ppermute x4, waiting for transfers between devices: 6.63 us -> 1.38 us  [swap_cores(): return lax.ppermute(v, 'core', [(0, 1), (1, 0)])]
    all_to_all x3, starting transfers between devices: 23.1 us -> 19.6 us  [exchange(): lax.all_to_all(v, ('x', 'z'), split_axis=0, concat_axis=0, tiled=True)]
    pallas_call x11, Pallas kernels: 31.9 us -> 34.6 us  [call(): pl.pallas_call(kernel, out_shape=outs, in_specs=[pl.BlockSpec(memory_spac...]
    unnamed x13 -> x23, local copies, waits for them, and re-layouts: 7.05 us -> 6.26 us
  transfers between devices with their start and end apart: 12 -> 12, of which waited for: 10 -> 8; matrix products, arithmetic and copies ran while one was open for 2% -> 1% of each run, Pallas kernels for 17% -> 18%
where the time goes in v4:
time: 168 us
  blocking collectives  47.5 us (28%)
  starting transfers between devices  46.6 us (28%)
  Pallas kernels  34.6 us (21%)
  waiting for transfers between devices  31 us (18%)
  local copies, waits for them, and re-layouts  6.98 us (4%)
    all_to_all x1, blocking collectives, exchange(): lax.all_to_all(v, ('x', 'z'), split_axis=0, concat_axis=0, tiled=True)  47.5 us
    pallas_call x11, Pallas kernels, call(): pl.pallas_call(kernel, out_shape=outs, in_specs=[pl.BlockSpec(memory_spac...  34.6 us
    all_to_all x3, starting transfers between devices, exchange(): lax.all_to_all(v, ('x', 'z'), split_axis=0, concat_axis=0, tiled=True)  19.6 us
    ppermute x5, starting transfers between devices, across(): return lax.ppermute(v, 'y', [(i, i ^ bits) for i in range(8)])  19.3 us
    all_to_all x3, waiting for transfers between devices, exchange(): lax.all_to_all(v, ('x', 'z'), split_axis=0, concat_axis=0, tiled=True)  17.7 us
    ppermute x5, waiting for transfers between devices, across(): return lax.ppermute(v, 'y', [(i, i ^ bits) for i in range(8)])  12 us
    ppermute x4, starting transfers between devices, swap_cores(): return lax.ppermute(v, 'core', [(0, 1), (1, 0)])  7.67 us
    unnamed x23, local copies, waits for them, and re-layouts  6.26 us
  transfers between devices with their start and end apart: 12, of which 8 were waited for; matrix products, arithmetic and copies ran while one was open for 1% of the time, Pallas kernels for 18%

profile of v4, /device:TPU:64, one launch (start us, length us, event | category | flops | bytes accessed | tf_op | source)
XLA Modules:
  0.0 167.6 jit_solution(1728336571084405559)
XLA Ops:
  0.6 2.9 %shard_map.76 = (bf16[3,32,128]{2,1,0:T(8,128)(2,1)}, bf16[3,32,128]{2,1,0:T(8,128)(2,1)}, bf16[32,64,128]{2,1,0:T(8,128)(2,1)}, bf16[32,128,128]{2,1,0:T(8,128)(2,1)}) custom-call(s32[2,128]{1,0:T(2,128)} %bitcast.10, s32[32,128]{1,0:T(8,128)} %bitcast.8, f32[32,128]{1,0:T(8,128)} %bitcast.9, bf16[128,4096]{1,0:T(8,128)(2,1)} %table_any.1, ...), custom_call_target="tpu_custom_call" | custom-call | flops 2000000000 | bytes 6600000 | tf_op jit(solution)/shard_map/pallas_call | solution.py:274
  3.5 1.9 %collective-permute-start = (bf16[3,32,128]{2,1,0:T(8,128)(2,1)}, bf16[3,32,128]{2,1,0:T(8,128)(2,1)S(1)}, u32[]{:S(2)}, u32[]{:S(2)}) collective-permute-start(bf16[3,32,128]{2,1,0:T(8,128)(2,1)} %get-tuple-element.26), channel_id=1, source_target_pairs={{0,8},{8,0},{1,9},{9,1},{2,10},{10,2},{3,11},{11,3},{4,12},{12,4},... | collective-permute-start | bytes 73736 | tf_op jit(solution)/shard_map/ppermute | solution.py:288
  5.5 1.4 collective-permute-done.other_ref
  6.8 1.0 copy-done
  7.9 0.7 copy-done.1
  8.6 0.1 shard_map.77
  8.7 47.5 %all_to_all.20.got_ref = bf16[32,160,128]{2,1,0:T(8,128)(2,1)S(1)} all-to-all(bf16[32,160,128]{2,1,0:T(8,128)(2,1)S(1)} %shard_map.77), channel_id=1, replica_groups=mesh['x'=4,'z'=8,'core'=2,'y'=8] {'x','z'}, dimensions={0} | all-to-all | bytes 2621440 | tf_op jit(solution)/shard_map/all_to_all | solution.py:296
  56.2 4.6 %all-to-all-start.1 = ((bf16[32,128,128]{2,1,0:T(8,128)(2,1)}), bf16[32,128,128]{2,1,0:T(8,128)(2,1)}, u32[]{:S(2)}, u32[]{:S(2)}) async-start(bf16[32,128,128]{2,1,0:T(8,128)(2,1)} %get-tuple-element.33), calls=%async_computation.1 | async-start | bytes 2097152 | tf_op jit(solution)/shard_map/all_to_all | solution.py:296
  60.8 0.1 slice.4
  60.9 3.5 %collective-permute-start.1 = (bf16[32,64,128]{2,1,0:T(8,128)(2,1)S(1)}, bf16[32,64,128]{2,1,0:T(8,128)(2,1)S(1)}, u32[]{:S(2)}, u32[]{:S(2)}) collective-permute-start(bf16[32,64,128]{2,1,0:T(8,128)(2,1)S(1)} %slice.4), channel_id=1, source_target_pairs={{0,1},{1,0},{2,3},{3,2},{4,5},{5,4},{6,7},{7,6},{8,9},{9,8},{10,11... | collective-permute-start | bytes 1572872 | tf_op jit(solution)/shard_map/ppermute | solution.py:292
  64.4 8.4 %shard_map.78 = (bf16[32,512,128]{2,1,0:T(8,128)(2,1)S(1)}, bf16[32,512,128]{2,1,0:T(8,128)(2,1)S(1)}, f32[32,8,512]{2,1,0:T(8,128)S(1)}) custom-call(bf16[32,160,128]{2,1,0:T(8,128)(2,1)S(1)} %all_to_all.20.got_ref), custom_call_target="tpu_custom_call" | custom-call | flops 8499999744 | bytes 28050000 | tf_op jit(solution)/shard_map/pallas_call | solution.py:274
  72.8 0.0 copy-start.9
  72.8 2.0 %copy-done.9 = bf16[32,512,128]{2,1,0:T(8,128)(2,1)} copy-done((bf16[32,512,128]{2,1,0:T(8,128)(2,1)}, bf16[32,512,128]{2,1,0:T(8,128)(2,1)S(1)}, u32[]{:S(2)}) %copy-start.9) | copy-done | bytes 4194328
  74.7 1.0 collective-permute-done.1.table_ref
  75.7 5.5 %shard_map.79 = (bf16[32,128,128]{2,1,0:T(8,128)(2,1)S(1)}, bf16[32,128,128]{2,1,0:T(8,128)(2,1)}) custom-call(bf16[32,512,128]{2,1,0:T(8,128)(2,1)S(1)} %get-tuple-element.28.mix_ref, f32[32,8,512]{2,1,0:T(8,128)S(1)} %get-tuple-element.29.token_ref, bf16[32,160,128]{2,1,0:T(8,128)(2,1)S(1)} %all_to_all.20.got_ref, ...), custom_call_target="tpu_custom_call" | custom-call | flops 4499999744 | bytes 14850000 | tf_op jit(solution)/shard_map/pallas_call | solution.py:274
  81.2 0.0 copy-done.4
  81.2 0.0 copy-done.6
  81.2 0.0 copy-done.2
  81.2 1.9 %collective-permute-start.2 = (bf16[32,128,128]{2,1,0:T(8,128)(2,1)}, bf16[32,128,128]{2,1,0:T(8,128)(2,1)S(1)}, u32[]{:S(2)}, u32[]{:S(2)}) collective-permute-start(bf16[32,128,128]{2,1,0:T(8,128)(2,1)} %get-tuple-element.31), channel_id=1, source_target_pairs={{0,8},{8,0},{1,9},{9,1},{2,10},{10,2},{3,11},{11,3},{4,12},{12,4},... | collective-permute-start | bytes 3145736 | tf_op jit(solution)/shard_map/ppermute | solution.py:288
  83.1 6.1 %all-to-all-done.1.near_ref = bf16[32,128,128]{2,1,0:T(8,128)(2,1)} async-done(((bf16[32,128,128]{2,1,0:T(8,128)(2,1)}), bf16[32,128,128]{2,1,0:T(8,128)(2,1)}, u32[]{:S(2)}, u32[]{:S(2)}) %all-to-all-start.1) | async-done | bytes 1048608 | tf_op jit(solution)/shard_map/all_to_all | solution.py:296
  89.2 1.9 %collective-permute-start.3 = (bf16[32,128,128]{2,1,0:T(8,128)(2,1)}, bf16[32,128,128]{2,1,0:T(8,128)(2,1)}, u32[]{:S(2)}, u32[]{:S(2)}) collective-permute-start(bf16[32,128,128]{2,1,0:T(8,128)(2,1)} %all-to-all-done.1.near_ref), channel_id=1, source_target_pairs={{0,8},{8,0},{1,9},{9,1},{2,10},{10,2},{3,11},{11,3},{4,12},{12,4},... | collective-permute-start | bytes 3145736 | tf_op jit(solution)/shard_map/ppermute | solution.py:288
  91.1 0.0 collective-permute-done.2.far_ref
  91.1 1.2 shard_map.80
  92.3 5.2 %all-to-all-start.2 = ((bf16[32,128,128]{2,1,0:T(8,128)(2,1)}), bf16[32,128,128]{2,1,0:T(8,128)(2,1)S(1)}, u32[]{:S(2)}, u32[]{:S(2)}) async-start(bf16[32,128,128]{2,1,0:T(8,128)(2,1)} %shard_map.80), calls=%async_computation.2 | async-start | bytes 2097152 | tf_op jit(solution)/shard_map/all_to_all | solution.py:296
  97.5 0.0 copy-start.5
  97.5 0.0 collective-permute-done.3.far_ref
  97.6 1.2 copy-done.7
  98.7 4.9 %shard_map.81.rows_ref = bf16[32,512,128]{2,1,0:T(8,128)(2,1)S(1)} custom-call(f32[32,8,512]{2,1,0:T(8,128)S(1)} %copy-done.7, bf16[32,128,128]{2,1,0:T(8,128)(2,1)} %all-to-all-done.1.near_ref, bf16[32,128,128]{2,1,0:T(8,128)(2,1)} %collective-permute-done.3.far_ref), custom_call_target="tpu_custom_call" | custom-call | flops 3000000000 | bytes 9900000 | tf_op jit(solution)/shard_map/pallas_call | solution.py:274
  103.7 2.0 %shard_map.83 = (bf16[4,32,16,128]{3,2,1,0:T(8,128)(2,1)S(1)}, bf16[4,32,16,128]{3,2,1,0:T(8,128)(2,1)S(1)}) custom-call(bf16[32,512,128]{2,1,0:T(8,128)(2,1)S(1)} %copy-done.5, bf16[32,512,128]{2,1,0:T(8,128)(2,1)S(1)} %shard_map.81.rows_ref), custom_call_target="tpu_custom_call" | custom-call | flops 2500000000 | bytes 8250000 | tf_op jit(solution)/shard_map/pallas_call | solution.py:274
  105.6 3.5 %collective-permute-start.5 = (bf16[4,32,16,128]{3,2,1,0:T(8,128)(2,1)S(1)}, bf16[4,32,16,128]{3,2,1,0:T(8,128)(2,1)S(1)}, u32[]{:S(2)}, u32[]{:S(2)}) collective-permute-start(bf16[4,32,16,128]{3,2,1,0:T(8,128)(2,1)S(1)} %get-tuple-element.39), channel_id=1, source_target_pairs={{0,1},{1,0},{2,3},{3,2},{4,5},{5,4},{6,7},{7,6},{8,9},{9,8},{10,11... | collective-permute-start | bytes 1572872 | tf_op jit(solution)/shard_map/ppermute | solution.py:292
  109.2 7.9 %shard_map.82 = (bf16[32,32,128]{2,1,0:T(8,128)(2,1)S(1)}, bf16[32,32,128]{2,1,0:T(8,128)(2,1)S(1)}) custom-call(bf16[32,512,128]{2,1,0:T(8,128)(2,1)S(1)} %shard_map.81.rows_ref, bf16[32,512,128]{2,1,0:T(8,128)(2,1)S(1)} %copy-done.10, f32[32,8,512]{2,1,0:T(8,128)S(1)} %copy-done.8, bf16[32,160,128]{2,1,0:T(8,128)(2,1)S(1)} %all_to_all.20.got_ref, ...), custom_call_target="tpu_custom_call" | custom-call | flops 8000000000 | bytes 26400000 | tf_op jit(solution)/shard_map/pallas_call | solution.py:274
  117.1 1.9 %collective-permute-start.4 = (bf16[32,32,128]{2,1,0:T(8,128)(2,1)S(1)}, bf16[32,32,128]{2,1,0:T(8,128)(2,1)S(1)}, u32[]{:S(2)}, u32[]{:S(2)}) collective-permute-start(bf16[32,32,128]{2,1,0:T(8,128)(2,1)S(1)} %get-tuple-element.37), channel_id=1, source_target_pairs={{0,8},{8,0},{1,9},{9,1},{2,10},{10,2},{3,11},{11,3},{4,12},{12,4},... | collective-permute-start | bytes 786440 | tf_op jit(solution)/shard_map/ppermute | solution.py:288
  119.0 2.3 %collective-permute-done.5.got_ref = bf16[4,32,16,128]{3,2,1,0:T(8,128)(2,1)S(1)} collective-permute-done((bf16[4,32,16,128]{3,2,1,0:T(8,128)(2,1)S(1)}, bf16[4,32,16,128]{3,2,1,0:T(8,128)(2,1)S(1)}, u32[]{:S(2)}, u32[]{:S(2)}) %collective-permute-start.5) | collective-permute-done | bytes 524320 | tf_op jit(solution)/shard_map/ppermute | solution.py:292
  121.3 0.1 shard_map.84
  121.4 7.7 %collective-permute-start.6 = (bf16[32,16,128]{2,1,0:T(8,128)(2,1)S(1)}, bf16[32,16,128]{2,1,0:T(8,128)(2,1)S(1)}, u32[]{:S(2)}, u32[]{:S(2)}) collective-permute-start(bf16[32,16,128]{2,1,0:T(8,128)(2,1)S(1)} %get-tuple-element.41), channel_id=1, source_target_pairs={{0,4},{1,5},{2,6},{3,7},{4,0},{5,1},{6,2},{7,3},{8,12},{9,13},{10,... | collective-permute-start | bytes 393224 | tf_op jit(solution)/shard_map/ppermute | solution.py:292
  129.2 2.7 %collective-permute-start.7 = (bf16[32,16,128]{2,1,0:T(8,128)(2,1)S(1)}, bf16[32,16,128]{2,1,0:T(8,128)(2,1)S(1)}, u32[]{:S(2)}, u32[]{:S(2)}) collective-permute-start(bf16[32,16,128]{2,1,0:T(8,128)(2,1)S(1)} %get-tuple-element.42), channel_id=1, source_target_pairs={{0,2},{1,3},{2,0},{3,1},{4,6},{5,7},{6,4},{7,5},{8,10},{9,11},{10,... | collective-permute-start | bytes 393224 | tf_op jit(solution)/shard_map/ppermute | solution.py:292
  131.9 1.9 %collective-permute-start.8 = (bf16[32,16,128]{2,1,0:T(8,128)(2,1)S(1)}, bf16[32,16,128]{2,1,0:T(8,128)(2,1)S(1)}, u32[]{:S(2)}, u32[]{:S(2)}) collective-permute-start(bf16[32,16,128]{2,1,0:T(8,128)(2,1)S(1)} %get-tuple-element.43), channel_id=1, source_target_pairs={{0,6},{1,7},{2,4},{3,5},{4,2},{5,3},{6,0},{7,1},{8,14},{9,15},{10,... | collective-permute-start | bytes 393224 | tf_op jit(solution)/shard_map/ppermute | solution.py:292
  133.8 0.0 collective-permute-done.4.far_ref
  133.8 1.2 collective-permute-done.6.refs_1_
  135.0 5.9 %collective-permute-done.7.refs_2_ = bf16[32,16,128]{2,1,0:T(8,128)(2,1)S(1)} collective-permute-done((bf16[32,16,128]{2,1,0:T(8,128)(2,1)S(1)}, bf16[32,16,128]{2,1,0:T(8,128)(2,1)S(1)}, u32[]{:S(2)}, u32[]{:S(2)}) %collective-permute-start.7) | collective-permute-done | bytes 131104 | tf_op jit(solution)/shard_map/ppermute | solution.py:292
  140.9 1.6 collective-permute-done.8.refs_3_
  142.6 0.9 shard_map.85
  143.5 0.0 all-to-all-done.2
  143.5 9.8 %all-to-all-start.3 = ((bf16[32,48,128]{2,1,0:T(8,128)(2,1)}), bf16[32,48,128]{2,1,0:T(8,128)(2,1)S(1)}, u32[]{:S(2)}, u32[]{:S(2)}) async-start(bf16[32,48,128]{2,1,0:T(8,128)(2,1)} %shard_map.85), calls=%async_computation.3 | async-start | bytes 786432 | tf_op jit(solution)/shard_map/all_to_all | solution.py:296
  153.2 0.7 copy.8
  153.9 1.3 copy.9
  155.2 11.6 %all-to-all-done.3.got_ref = bf16[32,48,128]{2,1,0:T(8,128)(2,1)S(1)} async-done(((bf16[32,48,128]{2,1,0:T(8,128)(2,1)}), bf16[32,48,128]{2,1,0:T(8,128)(2,1)S(1)}, u32[]{:S(2)}, u32[]{:S(2)}) %all-to-all-start.3) | async-done | bytes 393248 | tf_op jit(solution)/shard_map/all_to_all | solution.py:296
  166.8 0.8 shard_map.86
  (13 shorter events, 0.0 us)
Async XLA Ops:
  3.5 3.3 %collective-permute-start = (bf16[3,32,128]{2,1,0:T(8,128)(2,1)}, bf16[3,32,128]{2,1,0:T(8,128)(2,1)S(1)}, u32[]{:S(2)}, u32[]{:S(2)}) collective-permute-start(bf16[3,32,128]{2,1,0:T(8,128)(2,1)} %get-tuple-element.26), channel_id=1, source_target_pairs={{0,8},{8,0},{1,9},{9,1},{2,10},{10,2},{3,11},{11,3},{4,12},{12,4},... | collective-permute-start | bytes 73736 | tf_op jit(solution)/shard_map/ppermute | solution.py:288
  6.8 1.0 copy-start
  7.9 0.7 copy-start.1
  56.2 33.0 %all-to-all-start.1 = ((bf16[32,128,128]{2,1,0:T(8,128)(2,1)}), bf16[32,128,128]{2,1,0:T(8,128)(2,1)}, u32[]{:S(2)}, u32[]{:S(2)}) async-start(bf16[32,128,128]{2,1,0:T(8,128)(2,1)} %get-tuple-element.33), calls=%async_computation.1 | async-start | bytes 2097152 | tf_op jit(solution)/shard_map/all_to_all | solution.py:296
  60.9 14.8 %collective-permute-start.1 = (bf16[32,64,128]{2,1,0:T(8,128)(2,1)S(1)}, bf16[32,64,128]{2,1,0:T(8,128)(2,1)S(1)}, u32[]{:S(2)}, u32[]{:S(2)}) collective-permute-start(bf16[32,64,128]{2,1,0:T(8,128)(2,1)S(1)} %slice.4), channel_id=1, source_target_pairs={{0,1},{1,0},{2,3},{3,2},{4,5},{5,4},{6,7},{7,6},{8,9},{9,8},{10,11... | collective-permute-start | bytes 1572872 | tf_op jit(solution)/shard_map/ppermute | solution.py:292
  72.8 2.0 %copy-start.9 = (bf16[32,512,128]{2,1,0:T(8,128)(2,1)}, bf16[32,512,128]{2,1,0:T(8,128)(2,1)S(1)}, u32[]{:S(2)}) copy-start(bf16[32,512,128]{2,1,0:T(8,128)(2,1)S(1)} %get-tuple-element.35.pick_ref) | copy-start | bytes 12582916
  74.7 6.5 %copy-start.4 = (bf16[32,512,128]{2,1,0:T(8,128)(2,1)}, bf16[32,512,128]{2,1,0:T(8,128)(2,1)S(1)}, u32[]{:S(2)}) copy-start(bf16[32,512,128]{2,1,0:T(8,128)(2,1)S(1)} %get-tuple-element.28.mix_ref) | copy-start | bytes 12582916
  74.7 6.5 %copy-start.6 = (f32[32,8,512]{2,1,0:T(8,128)}, f32[32,8,512]{2,1,0:T(8,128)S(1)}, u32[]{:S(2)}) copy-start(f32[32,8,512]{2,1,0:T(8,128)S(1)} %get-tuple-element.29.token_ref) | copy-start | bytes 1572868
  75.7 5.5 %copy-start.2 = (bf16[32,64,128]{2,1,0:T(8,128)(2,1)}, bf16[32,64,128]{2,1,0:T(8,128)(2,1)S(1)}, u32[]{:S(2)}) copy-start(bf16[32,64,128]{2,1,0:T(8,128)(2,1)S(1)} %collective-permute-done.1.table_ref) | copy-start | bytes 1572868
  81.2 9.9 %collective-permute-start.2 = (bf16[32,128,128]{2,1,0:T(8,128)(2,1)}, bf16[32,128,128]{2,1,0:T(8,128)(2,1)S(1)}, u32[]{:S(2)}, u32[]{:S(2)}) collective-permute-start(bf16[32,128,128]{2,1,0:T(8,128)(2,1)} %get-tuple-element.31), channel_id=1, source_target_pairs={{0,8},{8,0},{1,9},{9,1},{2,10},{10,2},{3,11},{11,3},{4,12},{12,4},... | collective-permute-start | bytes 3145736 | tf_op jit(solution)/shard_map/ppermute | solution.py:288
  89.2 8.3 %collective-permute-start.3 = (bf16[32,128,128]{2,1,0:T(8,128)(2,1)}, bf16[32,128,128]{2,1,0:T(8,128)(2,1)}, u32[]{:S(2)}, u32[]{:S(2)}) collective-permute-start(bf16[32,128,128]{2,1,0:T(8,128)(2,1)} %all-to-all-done.1.near_ref), channel_id=1, source_target_pairs={{0,8},{8,0},{1,9},{9,1},{2,10},{10,2},{3,11},{11,3},{4,12},{12,4},... | collective-permute-start | bytes 3145736 | tf_op jit(solution)/shard_map/ppermute | solution.py:288
  92.3 51.1 %all-to-all-start.2 = ((bf16[32,128,128]{2,1,0:T(8,128)(2,1)}), bf16[32,128,128]{2,1,0:T(8,128)(2,1)S(1)}, u32[]{:S(2)}, u32[]{:S(2)}) async-start(bf16[32,128,128]{2,1,0:T(8,128)(2,1)} %shard_map.80), calls=%async_computation.2 | async-start | bytes 2097152 | tf_op jit(solution)/shard_map/all_to_all | solution.py:296
  97.5 6.1 %copy-start.5 = (bf16[32,512,128]{2,1,0:T(8,128)(2,1)S(1)}, bf16[32,512,128]{2,1,0:T(8,128)(2,1)}, u32[]{:S(2)}) copy-start(bf16[32,512,128]{2,1,0:T(8,128)(2,1)} %copy-done.4) | copy-start | bytes 12582916
  97.5 1.2 copy-start.7
  103.6 5.5 %copy-start.3 = (bf16[32,64,128]{2,1,0:T(8,128)(2,1)S(1)}, bf16[32,64,128]{2,1,0:T(8,128)(2,1)}, u32[]{:S(2)}) copy-start(bf16[32,64,128]{2,1,0:T(8,128)(2,1)} %copy-done.2) | copy-start | bytes 1572868
  103.7 5.5 %copy-start.8 = (f32[32,8,512]{2,1,0:T(8,128)S(1)}, f32[32,8,512]{2,1,0:T(8,128)}, u32[]{:S(2)}) copy-start(f32[32,8,512]{2,1,0:T(8,128)} %copy-done.6) | copy-start | bytes 1572868
  103.7 5.5 %copy-start.10 = (bf16[32,512,128]{2,1,0:T(8,128)(2,1)S(1)}, bf16[32,512,128]{2,1,0:T(8,128)(2,1)}, u32[]{:S(2)}) copy-start(bf16[32,512,128]{2,1,0:T(8,128)(2,1)} %copy-done.9) | copy-start | bytes 12582916
  105.6 15.7 %collective-permute-start.5 = (bf16[4,32,16,128]{3,2,1,0:T(8,128)(2,1)S(1)}, bf16[4,32,16,128]{3,2,1,0:T(8,128)(2,1)S(1)}, u32[]{:S(2)}, u32[]{:S(2)}) collective-permute-start(bf16[4,32,16,128]{3,2,1,0:T(8,128)(2,1)S(1)} %get-tuple-element.39), channel_id=1, source_target_pairs={{0,1},{1,0},{2,3},{3,2},{4,5},{5,4},{6,7},{7,6},{8,9},{9,8},{10,11... | collective-permute-start | bytes 1572872 | tf_op jit(solution)/shard_map/ppermute | solution.py:292
  117.1 16.7 %collective-permute-start.4 = (bf16[32,32,128]{2,1,0:T(8,128)(2,1)S(1)}, bf16[32,32,128]{2,1,0:T(8,128)(2,1)S(1)}, u32[]{:S(2)}, u32[]{:S(2)}) collective-permute-start(bf16[32,32,128]{2,1,0:T(8,128)(2,1)S(1)} %get-tuple-element.37), channel_id=1, source_target_pairs={{0,8},{8,0},{1,9},{9,1},{2,10},{10,2},{3,11},{11,3},{4,12},{12,4},... | collective-permute-start | bytes 786440 | tf_op jit(solution)/shard_map/ppermute | solution.py:288
  121.4 13.6 %collective-permute-start.6 = (bf16[32,16,128]{2,1,0:T(8,128)(2,1)S(1)}, bf16[32,16,128]{2,1,0:T(8,128)(2,1)S(1)}, u32[]{:S(2)}, u32[]{:S(2)}) collective-permute-start(bf16[32,16,128]{2,1,0:T(8,128)(2,1)S(1)} %get-tuple-element.41), channel_id=1, source_target_pairs={{0,4},{1,5},{2,6},{3,7},{4,0},{5,1},{6,2},{7,3},{8,12},{9,13},{10,... | collective-permute-start | bytes 393224 | tf_op jit(solution)/shard_map/ppermute | solution.py:292
  129.2 11.8 %collective-permute-start.7 = (bf16[32,16,128]{2,1,0:T(8,128)(2,1)S(1)}, bf16[32,16,128]{2,1,0:T(8,128)(2,1)S(1)}, u32[]{:S(2)}, u32[]{:S(2)}) collective-permute-start(bf16[32,16,128]{2,1,0:T(8,128)(2,1)S(1)} %get-tuple-element.42), channel_id=1, source_target_pairs={{0,2},{1,3},{2,0},{3,1},{4,6},{5,7},{6,4},{7,5},{8,10},{9,11},{10,... | collective-permute-start | bytes 393224 | tf_op jit(solution)/shard_map/ppermute | solution.py:292
  131.9 10.7 %collective-permute-start.8 = (bf16[32,16,128]{2,1,0:T(8,128)(2,1)S(1)}, bf16[32,16,128]{2,1,0:T(8,128)(2,1)S(1)}, u32[]{:S(2)}, u32[]{:S(2)}) collective-permute-start(bf16[32,16,128]{2,1,0:T(8,128)(2,1)S(1)} %get-tuple-element.43), channel_id=1, source_target_pairs={{0,6},{1,7},{2,4},{3,5},{4,2},{5,3},{6,0},{7,1},{8,14},{9,15},{10,... | collective-permute-start | bytes 393224 | tf_op jit(solution)/shard_map/ppermute | solution.py:292
  143.5 23.4 %all-to-all-start.3 = ((bf16[32,48,128]{2,1,0:T(8,128)(2,1)}), bf16[32,48,128]{2,1,0:T(8,128)(2,1)S(1)}, u32[]{:S(2)}, u32[]{:S(2)}) async-start(bf16[32,48,128]{2,1,0:T(8,128)(2,1)} %shard_map.85), calls=%async_computation.3 | async-start | bytes 786432 | tf_op jit(solution)/shard_map/all_to_all | solution.py:296

commit v5 on v4

--- a/solution.py
+++ b/solution.py
@@ -194,7 +194,15 @@
     lax.fori_loop(0, CHIPS, group, 0, unroll=8)
 
 
-def gather_kernel(token_ref, near_ref, far_ref, rows_ref):
+def gather_kernel(near_any, far_any, token_ref, rows_ref, near_ref, far_ref, sems):
+    chunk = CHIPS // 4
+    copies = []
+    for i in range(4):
+        part = pl.ds(i * chunk, chunk)
+        for j, (source, ref) in enumerate(((near_any, near_ref), (far_any, far_ref))):
+            copies.append(pltpu.make_async_copy(source.at[part], ref.at[part], sems.at[2 * i + j]))
+    for copy in copies:
+        copy.start()
     token_rows = iota((256, GROUP_SLOTS), 0).astype(F32).astype(BF16)
 
     def gather(g, _):
@@ -205,7 +213,10 @@
         rows_ref[:, pl.ds(pl.multiple_of(g * 16, 16), 16), :] = rows.reshape(CHIPS, 16, 128)
         return 0
 
-    lax.fori_loop(0, CHIPS, gather, 0, unroll=8)
+    for i in range(4):
+        copies[2 * i].wait()
+        copies[2 * i + 1].wait()
+        lax.fori_loop(i * chunk, (i + 1) * chunk, gather, 0, unroll=8)
 
 
 def table_grad_kernel(mix_ref, rows_ref, keep_ref, send_ref):
@@ -353,10 +364,16 @@
     (rows,) = call(
         gather_kernel,
         [(CHIPS, GROUP_SLOTS, 128)],
-        tokens,
         near_grads,
         swap_cores(near_grads),
+        tokens,
         us=3,
+        scratch=[
+            pltpu.VMEM((CHIPS, 128, 128), BF16),
+            pltpu.VMEM((CHIPS, 128, 128), BF16),
+            pltpu.SemaphoreType.DMA((8,)),
+        ],
+        spaces=[pl.ANY] * 2,
     )
     keep, send = call(table_grad_kernel, [(4, CHIPS, 16, 128)] * 2, mix, rows, us=2.5)
     near, far = call(

time: 168 us -> 168 us (level)
  no operation moved by 1% of the time
where the time goes in v5:
time: 168 us; the launch traced here: 167 us
  blocking collectives  47.5 us (28%)
  starting transfers between devices  46.6 us (28%)
  Pallas kernels  34.1 us (20%)
  waiting for transfers between devices  31 us (18%)
  local copies, waits for them, and re-layouts  6.98 us (4%)
    all_to_all x1, blocking collectives, exchange(): lax.all_to_all(v, ('x', 'z'), split_axis=0, concat_axis=0, tiled=True)  47.5 us
    pallas_call x11, Pallas kernels, call(): pl.pallas_call(kernel, out_shape=outs, in_specs=[pl.BlockSpec(memory_spac...  34.1 us
    all_to_all x3, starting transfers between devices, exchange(): lax.all_to_all(v, ('x', 'z'), split_axis=0, concat_axis=0, tiled=True)  19.6 us
    ppermute x5, starting transfers between devices, across(): return lax.ppermute(v, 'y', [(i, i ^ bits) for i in range(8)])  19.3 us
    all_to_all x3, waiting for transfers between devices, exchange(): lax.all_to_all(v, ('x', 'z'), split_axis=0, concat_axis=0, tiled=True)  17.7 us
    ppermute x5, waiting for transfers between devices, across(): return lax.ppermute(v, 'y', [(i, i ^ bits) for i in range(8)])  12 us
    ppermute x4, starting transfers between devices, swap_cores(): return lax.ppermute(v, 'core', [(0, 1), (1, 0)])  7.67 us
    unnamed x23, local copies, waits for them, and re-layouts  6.26 us
  transfers between devices with their start and end apart: 12, of which 8 were waited for; matrix products, arithmetic and copies ran while one was open for 1% of the time, Pallas kernels for 18%

profile of v5, /device:TPU:64, one launch (start us, length us, event | category | flops | bytes accessed | tf_op | source)
XLA Modules:
  0.0 167.1 jit_solution(7011873395732787921)
XLA Ops:
  0.6 2.9 %shard_map.76 = (bf16[3,32,128]{2,1,0:T(8,128)(2,1)}, bf16[3,32,128]{2,1,0:T(8,128)(2,1)}, bf16[32,64,128]{2,1,0:T(8,128)(2,1)}, bf16[32,128,128]{2,1,0:T(8,128)(2,1)}) custom-call(s32[2,128]{1,0:T(2,128)} %bitcast.10, s32[32,128]{1,0:T(8,128)} %bitcast.8, f32[32,128]{1,0:T(8,128)} %bitcast.9, bf16[128,4096]{1,0:T(8,128)(2,1)} %table_any.1, ...), custom_call_target="tpu_custom_call" | custom-call | flops 2000000000 | bytes 6600000 | tf_op jit(solution)/shard_map/pallas_call | solution.py:285
  3.5 1.9 %collective-permute-start = (bf16[3,32,128]{2,1,0:T(8,128)(2,1)}, bf16[3,32,128]{2,1,0:T(8,128)(2,1)S(1)}, u32[]{:S(2)}, u32[]{:S(2)}) collective-permute-start(bf16[3,32,128]{2,1,0:T(8,128)(2,1)} %get-tuple-element.26), channel_id=1, source_target_pairs={{0,8},{8,0},{1,9},{9,1},{2,10},{10,2},{3,11},{11,3},{4,12},{12,4},... | collective-permute-start | bytes 73736 | tf_op jit(solution)/shard_map/ppermute | solution.py:299
  5.5 1.4 collective-permute-done.other_ref
  6.8 1.0 copy-done
  7.9 0.7 copy-done.1
  8.6 0.1 shard_map.77
  8.7 47.5 %all_to_all.20.got_ref = bf16[32,160,128]{2,1,0:T(8,128)(2,1)S(1)} all-to-all(bf16[32,160,128]{2,1,0:T(8,128)(2,1)S(1)} %shard_map.77), channel_id=1, replica_groups=mesh['x'=4,'z'=8,'core'=2,'y'=8] {'x','z'}, dimensions={0} | all-to-all | bytes 2621440 | tf_op jit(solution)/shard_map/all_to_all | solution.py:307
  56.2 4.6 %all-to-all-start.1 = ((bf16[32,128,128]{2,1,0:T(8,128)(2,1)}), bf16[32,128,128]{2,1,0:T(8,128)(2,1)}, u32[]{:S(2)}, u32[]{:S(2)}) async-start(bf16[32,128,128]{2,1,0:T(8,128)(2,1)} %get-tuple-element.33), calls=%async_computation.1 | async-start | bytes 2097152 | tf_op jit(solution)/shard_map/all_to_all | solution.py:307
  60.8 0.1 slice.4
  60.9 3.5 %collective-permute-start.1 = (bf16[32,64,128]{2,1,0:T(8,128)(2,1)S(1)}, bf16[32,64,128]{2,1,0:T(8,128)(2,1)S(1)}, u32[]{:S(2)}, u32[]{:S(2)}) collective-permute-start(bf16[32,64,128]{2,1,0:T(8,128)(2,1)S(1)} %slice.4), channel_id=1, source_target_pairs={{0,1},{1,0},{2,3},{3,2},{4,5},{5,4},{6,7},{7,6},{8,9},{9,8},{10,11... | collective-permute-start | bytes 1572872 | tf_op jit(solution)/shard_map/ppermute | solution.py:303
  64.4 8.4 %shard_map.78 = (bf16[32,512,128]{2,1,0:T(8,128)(2,1)S(1)}, bf16[32,512,128]{2,1,0:T(8,128)(2,1)S(1)}, f32[32,8,512]{2,1,0:T(8,128)S(1)}) custom-call(bf16[32,160,128]{2,1,0:T(8,128)(2,1)S(1)} %all_to_all.20.got_ref), custom_call_target="tpu_custom_call" | custom-call | flops 8499999744 | bytes 28050000 | tf_op jit(solution)/shard_map/pallas_call | solution.py:285
  72.8 0.0 copy-start.9
  72.8 2.0 %copy-done.9 = bf16[32,512,128]{2,1,0:T(8,128)(2,1)} copy-done((bf16[32,512,128]{2,1,0:T(8,128)(2,1)}, bf16[32,512,128]{2,1,0:T(8,128)(2,1)S(1)}, u32[]{:S(2)}) %copy-start.9) | copy-done | bytes 4194328
  74.7 1.0 collective-permute-done.1.table_ref
  75.7 5.5 %shard_map.79 = (bf16[32,128,128]{2,1,0:T(8,128)(2,1)S(1)}, bf16[32,128,128]{2,1,0:T(8,128)(2,1)}) custom-call(bf16[32,512,128]{2,1,0:T(8,128)(2,1)S(1)} %get-tuple-element.28.mix_ref, f32[32,8,512]{2,1,0:T(8,128)S(1)} %get-tuple-element.29.token_ref, bf16[32,160,128]{2,1,0:T(8,128)(2,1)S(1)} %all_to_all.20.got_ref, ...), custom_call_target="tpu_custom_call" | custom-call | flops 4499999744 | bytes 14850000 | tf_op jit(solution)/shard_map/pallas_call | solution.py:285
  81.2 0.0 copy-done.4
  81.2 0.0 copy-done.6
  81.2 0.0 copy-done.2
  81.2 1.9 %collective-permute-start.2 = (bf16[32,128,128]{2,1,0:T(8,128)(2,1)}, bf16[32,128,128]{2,1,0:T(8,128)(2,1)S(1)}, u32[]{:S(2)}, u32[]{:S(2)}) collective-permute-start(bf16[32,128,128]{2,1,0:T(8,128)(2,1)} %get-tuple-element.31), channel_id=1, source_target_pairs={{0,8},{8,0},{1,9},{9,1},{2,10},{10,2},{3,11},{11,3},{4,12},{12,4},... | collective-permute-start | bytes 3145736 | tf_op jit(solution)/shard_map/ppermute | solution.py:299
  83.1 6.1 %all-to-all-done.1.near_any = bf16[32,128,128]{2,1,0:T(8,128)(2,1)} async-done(((bf16[32,128,128]{2,1,0:T(8,128)(2,1)}), bf16[32,128,128]{2,1,0:T(8,128)(2,1)}, u32[]{:S(2)}, u32[]{:S(2)}) %all-to-all-start.1) | async-done | bytes 1048608 | tf_op jit(solution)/shard_map/all_to_all | solution.py:307
  89.2 1.9 %collective-permute-start.3 = (bf16[32,128,128]{2,1,0:T(8,128)(2,1)}, bf16[32,128,128]{2,1,0:T(8,128)(2,1)}, u32[]{:S(2)}, u32[]{:S(2)}) collective-permute-start(bf16[32,128,128]{2,1,0:T(8,128)(2,1)} %all-to-all-done.1.near_any), channel_id=1, source_target_pairs={{0,8},{8,0},{1,9},{9,1},{2,10},{10,2},{3,11},{11,3},{4,12},{12,4},... | collective-permute-start | bytes 3145736 | tf_op jit(solution)/shard_map/ppermute | solution.py:299
  91.1 0.0 collective-permute-done.2.far_ref
  91.1 1.2 shard_map.80
  92.3 5.2 %all-to-all-start.2 = ((bf16[32,128,128]{2,1,0:T(8,128)(2,1)}), bf16[32,128,128]{2,1,0:T(8,128)(2,1)S(1)}, u32[]{:S(2)}, u32[]{:S(2)}) async-start(bf16[32,128,128]{2,1,0:T(8,128)(2,1)} %shard_map.80), calls=%async_computation.2 | async-start | bytes 2097152 | tf_op jit(solution)/shard_map/all_to_all | solution.py:307
  97.5 0.0 collective-permute-done.3.far_any
  97.5 0.0 copy-start.7
  97.6 1.2 copy-done.7
  98.7 4.4 %shard_map.81.rows_ref = bf16[32,512,128]{2,1,0:T(8,128)(2,1)S(1)} custom-call(bf16[32,128,128]{2,1,0:T(8,128)(2,1)} %all-to-all-done.1.near_any, bf16[32,128,128]{2,1,0:T(8,128)(2,1)} %collective-permute-done.3.far_any, f32[32,8,512]{2,1,0:T(8,128)S(1)} %copy-done.7), custom_call_target="tpu_custom_call" | custom-call | flops 3000000000 | bytes 9900000 | tf_op jit(solution)/shard_map/pallas_call | solution.py:285
  103.2 2.0 %shard_map.83 = (bf16[4,32,16,128]{3,2,1,0:T(8,128)(2,1)S(1)}, bf16[4,32,16,128]{3,2,1,0:T(8,128)(2,1)S(1)}) custom-call(bf16[32,512,128]{2,1,0:T(8,128)(2,1)S(1)} %copy-done.5, bf16[32,512,128]{2,1,0:T(8,128)(2,1)S(1)} %shard_map.81.rows_ref), custom_call_target="tpu_custom_call" | custom-call | flops 2500000000 | bytes 8250000 | tf_op jit(solution)/shard_map/pallas_call | solution.py:285
  105.1 3.5 %collective-permute-start.5 = (bf16[4,32,16,128]{3,2,1,0:T(8,128)(2,1)S(1)}, bf16[4,32,16,128]{3,2,1,0:T(8,128)(2,1)S(1)}, u32[]{:S(2)}, u32[]{:S(2)}) collective-permute-start(bf16[4,32,16,128]{3,2,1,0:T(8,128)(2,1)S(1)} %get-tuple-element.39), channel_id=1, source_target_pairs={{0,1},{1,0},{2,3},{3,2},{4,5},{5,4},{6,7},{7,6},{8,9},{9,8},{10,11... | collective-permute-start | bytes 1572872 | tf_op jit(solution)/shard_map/ppermute | solution.py:303
  108.6 7.9 %shard_map.82 = (bf16[32,32,128]{2,1,0:T(8,128)(2,1)S(1)}, bf16[32,32,128]{2,1,0:T(8,128)(2,1)S(1)}) custom-call(bf16[32,512,128]{2,1,0:T(8,128)(2,1)S(1)} %shard_map.81.rows_ref, bf16[32,512,128]{2,1,0:T(8,128)(2,1)S(1)} %copy-done.10, f32[32,8,512]{2,1,0:T(8,128)S(1)} %copy-done.8, bf16[32,160,128]{2,1,0:T(8,128)(2,1)S(1)} %all_to_all.20.got_ref, ...), custom_call_target="tpu_custom_call" | custom-call | flops 8000000000 | bytes 26400000 | tf_op jit(solution)/shard_map/pallas_call | solution.py:285
  116.6 1.9 %collective-permute-start.4 = (bf16[32,32,128]{2,1,0:T(8,128)(2,1)S(1)}, bf16[32,32,128]{2,1,0:T(8,128)(2,1)S(1)}, u32[]{:S(2)}, u32[]{:S(2)}) collective-permute-start(bf16[32,32,128]{2,1,0:T(8,128)(2,1)S(1)} %get-tuple-element.37), channel_id=1, source_target_pairs={{0,8},{8,0},{1,9},{9,1},{2,10},{10,2},{3,11},{11,3},{4,12},{12,4},... | collective-permute-start | bytes 786440 | tf_op jit(solution)/shard_map/ppermute | solution.py:299
  118.5 2.3 %collective-permute-done.5.got_ref = bf16[4,32,16,128]{3,2,1,0:T(8,128)(2,1)S(1)} collective-permute-done((bf16[4,32,16,128]{3,2,1,0:T(8,128)(2,1)S(1)}, bf16[4,32,16,128]{3,2,1,0:T(8,128)(2,1)S(1)}, u32[]{:S(2)}, u32[]{:S(2)}) %collective-permute-start.5) | collective-permute-done | bytes 524320 | tf_op jit(solution)/shard_map/ppermute | solution.py:303
  120.8 0.1 shard_map.84
  120.9 7.7 %collective-permute-start.6 = (bf16[32,16,128]{2,1,0:T(8,128)(2,1)S(1)}, bf16[32,16,128]{2,1,0:T(8,128)(2,1)S(1)}, u32[]{:S(2)}, u32[]{:S(2)}) collective-permute-start(bf16[32,16,128]{2,1,0:T(8,128)(2,1)S(1)} %get-tuple-element.41), channel_id=1, source_target_pairs={{0,4},{1,5},{2,6},{3,7},{4,0},{5,1},{6,2},{7,3},{8,12},{9,13},{10,... | collective-permute-start | bytes 393224 | tf_op jit(solution)/shard_map/ppermute | solution.py:303
  128.6 2.7 %collective-permute-start.7 = (bf16[32,16,128]{2,1,0:T(8,128)(2,1)S(1)}, bf16[32,16,128]{2,1,0:T(8,128)(2,1)S(1)}, u32[]{:S(2)}, u32[]{:S(2)}) collective-permute-start(bf16[32,16,128]{2,1,0:T(8,128)(2,1)S(1)} %get-tuple-element.42), channel_id=1, source_target_pairs={{0,2},{1,3},{2,0},{3,1},{4,6},{5,7},{6,4},{7,5},{8,10},{9,11},{10,... | collective-permute-start | bytes 393224 | tf_op jit(solution)/shard_map/ppermute | solution.py:303
  131.3 1.9 %collective-permute-start.8 = (bf16[32,16,128]{2,1,0:T(8,128)(2,1)S(1)}, bf16[32,16,128]{2,1,0:T(8,128)(2,1)S(1)}, u32[]{:S(2)}, u32[]{:S(2)}) collective-permute-start(bf16[32,16,128]{2,1,0:T(8,128)(2,1)S(1)} %get-tuple-element.43), channel_id=1, source_target_pairs={{0,6},{1,7},{2,4},{3,5},{4,2},{5,3},{6,0},{7,1},{8,14},{9,15},{10,... | collective-permute-start | bytes 393224 | tf_op jit(solution)/shard_map/ppermute | solution.py:303
  133.3 0.0 collective-permute-done.4.far_ref
  133.3 1.3 collective-permute-done.6.refs_1_
  134.6 5.8 %collective-permute-done.7.refs_2_ = bf16[32,16,128]{2,1,0:T(8,128)(2,1)S(1)} collective-permute-done((bf16[32,16,128]{2,1,0:T(8,128)(2,1)S(1)}, bf16[32,16,128]{2,1,0:T(8,128)(2,1)S(1)}, u32[]{:S(2)}, u32[]{:S(2)}) %collective-permute-start.7) | collective-permute-done | bytes 131104 | tf_op jit(solution)/shard_map/ppermute | solution.py:303
  140.4 1.6 collective-permute-done.8.refs_3_
  142.0 0.9 shard_map.85
  142.9 0.0 all-to-all-done.2
  142.9 9.8 %all-to-all-start.3 = ((bf16[32,48,128]{2,1,0:T(8,128)(2,1)}), bf16[32,48,128]{2,1,0:T(8,128)(2,1)S(1)}, u32[]{:S(2)}, u32[]{:S(2)}) async-start(bf16[32,48,128]{2,1,0:T(8,128)(2,1)} %shard_map.85), calls=%async_computation.3 | async-start | bytes 786432 | tf_op jit(solution)/shard_map/all_to_all | solution.py:307
  152.7 0.7 copy.8
  153.4 1.3 copy.9
  154.7 11.6 %all-to-all-done.3.got_ref = bf16[32,48,128]{2,1,0:T(8,128)(2,1)S(1)} async-done(((bf16[32,48,128]{2,1,0:T(8,128)(2,1)}), bf16[32,48,128]{2,1,0:T(8,128)(2,1)S(1)}, u32[]{:S(2)}, u32[]{:S(2)}) %all-to-all-start.3) | async-done | bytes 393248 | tf_op jit(solution)/shard_map/all_to_all | solution.py:307
  166.3 0.8 shard_map.86
  (13 shorter events, 0.0 us)
Async XLA Ops:
  3.5 3.3 %collective-permute-start = (bf16[3,32,128]{2,1,0:T(8,128)(2,1)}, bf16[3,32,128]{2,1,0:T(8,128)(2,1)S(1)}, u32[]{:S(2)}, u32[]{:S(2)}) collective-permute-start(bf16[3,32,128]{2,1,0:T(8,128)(2,1)} %get-tuple-element.26), channel_id=1, source_target_pairs={{0,8},{8,0},{1,9},{9,1},{2,10},{10,2},{3,11},{11,3},{4,12},{12,4},... | collective-permute-start | bytes 73736 | tf_op jit(solution)/shard_map/ppermute | solution.py:299
  6.8 1.0 copy-start
  7.9 0.7 copy-start.1
  56.2 33.0 %all-to-all-start.1 = ((bf16[32,128,128]{2,1,0:T(8,128)(2,1)}), bf16[32,128,128]{2,1,0:T(8,128)(2,1)}, u32[]{:S(2)}, u32[]{:S(2)}) async-start(bf16[32,128,128]{2,1,0:T(8,128)(2,1)} %get-tuple-element.33), calls=%async_computation.1 | async-start | bytes 2097152 | tf_op jit(solution)/shard_map/all_to_all | solution.py:307
  60.9 14.8 %collective-permute-start.1 = (bf16[32,64,128]{2,1,0:T(8,128)(2,1)S(1)}, bf16[32,64,128]{2,1,0:T(8,128)(2,1)S(1)}, u32[]{:S(2)}, u32[]{:S(2)}) collective-permute-start(bf16[32,64,128]{2,1,0:T(8,128)(2,1)S(1)} %slice.4), channel_id=1, source_target_pairs={{0,1},{1,0},{2,3},{3,2},{4,5},{5,4},{6,7},{7,6},{8,9},{9,8},{10,11... | collective-permute-start | bytes 1572872 | tf_op jit(solution)/shard_map/ppermute | solution.py:303
  72.8 2.0 %copy-start.9 = (bf16[32,512,128]{2,1,0:T(8,128)(2,1)}, bf16[32,512,128]{2,1,0:T(8,128)(2,1)S(1)}, u32[]{:S(2)}) copy-start(bf16[32,512,128]{2,1,0:T(8,128)(2,1)S(1)} %get-tuple-element.35.pick_ref) | copy-start | bytes 12582916
  74.7 6.5 %copy-start.4 = (bf16[32,512,128]{2,1,0:T(8,128)(2,1)}, bf16[32,512,128]{2,1,0:T(8,128)(2,1)S(1)}, u32[]{:S(2)}) copy-start(bf16[32,512,128]{2,1,0:T(8,128)(2,1)S(1)} %get-tuple-element.28.mix_ref) | copy-start | bytes 12582916
  74.7 6.5 %copy-start.6 = (f32[32,8,512]{2,1,0:T(8,128)}, f32[32,8,512]{2,1,0:T(8,128)S(1)}, u32[]{:S(2)}) copy-start(f32[32,8,512]{2,1,0:T(8,128)S(1)} %get-tuple-element.29.token_ref) | copy-start | bytes 1572868
  75.7 5.5 %copy-start.2 = (bf16[32,64,128]{2,1,0:T(8,128)(2,1)}, bf16[32,64,128]{2,1,0:T(8,128)(2,1)S(1)}, u32[]{:S(2)}) copy-start(bf16[32,64,128]{2,1,0:T(8,128)(2,1)S(1)} %collective-permute-done.1.table_ref) | copy-start | bytes 1572868
  81.2 9.9 %collective-permute-start.2 = (bf16[32,128,128]{2,1,0:T(8,128)(2,1)}, bf16[32,128,128]{2,1,0:T(8,128)(2,1)S(1)}, u32[]{:S(2)}, u32[]{:S(2)}) collective-permute-start(bf16[32,128,128]{2,1,0:T(8,128)(2,1)} %get-tuple-element.31), channel_id=1, source_target_pairs={{0,8},{8,0},{1,9},{9,1},{2,10},{10,2},{3,11},{11,3},{4,12},{12,4},... | collective-permute-start | bytes 3145736 | tf_op jit(solution)/shard_map/ppermute | solution.py:299
  89.2 8.3 %collective-permute-start.3 = (bf16[32,128,128]{2,1,0:T(8,128)(2,1)}, bf16[32,128,128]{2,1,0:T(8,128)(2,1)}, u32[]{:S(2)}, u32[]{:S(2)}) collective-permute-start(bf16[32,128,128]{2,1,0:T(8,128)(2,1)} %all-to-all-done.1.near_any), channel_id=1, source_target_pairs={{0,8},{8,0},{1,9},{9,1},{2,10},{10,2},{3,11},{11,3},{4,12},{12,4},... | collective-permute-start | bytes 3145736 | tf_op jit(solution)/shard_map/ppermute | solution.py:299
  92.3 50.6 %all-to-all-start.2 = ((bf16[32,128,128]{2,1,0:T(8,128)(2,1)}), bf16[32,128,128]{2,1,0:T(8,128)(2,1)S(1)}, u32[]{:S(2)}, u32[]{:S(2)}) async-start(bf16[32,128,128]{2,1,0:T(8,128)(2,1)} %shard_map.80), calls=%async_computation.2 | async-start | bytes 2097152 | tf_op jit(solution)/shard_map/all_to_all | solution.py:307
  97.5 5.6 %copy-start.5 = (bf16[32,512,128]{2,1,0:T(8,128)(2,1)S(1)}, bf16[32,512,128]{2,1,0:T(8,128)(2,1)}, u32[]{:S(2)}) copy-start(bf16[32,512,128]{2,1,0:T(8,128)(2,1)} %copy-done.4) | copy-start | bytes 12582916
  97.5 1.2 copy-start.7
  103.1 5.5 %copy-start.3 = (bf16[32,64,128]{2,1,0:T(8,128)(2,1)S(1)}, bf16[32,64,128]{2,1,0:T(8,128)(2,1)}, u32[]{:S(2)}) copy-start(bf16[32,64,128]{2,1,0:T(8,128)(2,1)} %copy-done.2) | copy-start | bytes 1572868
  103.1 5.5 %copy-start.8 = (f32[32,8,512]{2,1,0:T(8,128)S(1)}, f32[32,8,512]{2,1,0:T(8,128)}, u32[]{:S(2)}) copy-start(f32[32,8,512]{2,1,0:T(8,128)} %copy-done.6) | copy-start | bytes 1572868
  103.1 5.5 %copy-start.10 = (bf16[32,512,128]{2,1,0:T(8,128)(2,1)S(1)}, bf16[32,512,128]{2,1,0:T(8,128)(2,1)}, u32[]{:S(2)}) copy-start(bf16[32,512,128]{2,1,0:T(8,128)(2,1)} %copy-done.9) | copy-start | bytes 12582916
  105.1 15.7 %collective-permute-start.5 = (bf16[4,32,16,128]{3,2,1,0:T(8,128)(2,1)S(1)}, bf16[4,32,16,128]{3,2,1,0:T(8,128)(2,1)S(1)}, u32[]{:S(2)}, u32[]{:S(2)}) collective-permute-start(bf16[4,32,16,128]{3,2,1,0:T(8,128)(2,1)S(1)} %get-tuple-element.39), channel_id=1, source_target_pairs={{0,1},{1,0},{2,3},{3,2},{4,5},{5,4},{6,7},{7,6},{8,9},{9,8},{10,11... | collective-permute-start | bytes 1572872 | tf_op jit(solution)/shard_map/ppermute | solution.py:303
  116.6 16.7 %collective-permute-start.4 = (bf16[32,32,128]{2,1,0:T(8,128)(2,1)S(1)}, bf16[32,32,128]{2,1,0:T(8,128)(2,1)S(1)}, u32[]{:S(2)}, u32[]{:S(2)}) collective-permute-start(bf16[32,32,128]{2,1,0:T(8,128)(2,1)S(1)} %get-tuple-element.37), channel_id=1, source_target_pairs={{0,8},{8,0},{1,9},{9,1},{2,10},{10,2},{3,11},{11,3},{4,12},{12,4},... | collective-permute-start | bytes 786440 | tf_op jit(solution)/shard_map/ppermute | solution.py:299
  120.9 13.7 %collective-permute-start.6 = (bf16[32,16,128]{2,1,0:T(8,128)(2,1)S(1)}, bf16[32,16,128]{2,1,0:T(8,128)(2,1)S(1)}, u32[]{:S(2)}, u32[]{:S(2)}) collective-permute-start(bf16[32,16,128]{2,1,0:T(8,128)(2,1)S(1)} %get-tuple-element.41), channel_id=1, source_target_pairs={{0,4},{1,5},{2,6},{3,7},{4,0},{5,1},{6,2},{7,3},{8,12},{9,13},{10,... | collective-permute-start | bytes 393224 | tf_op jit(solution)/shard_map/ppermute | solution.py:303
  128.6 11.8 %collective-permute-start.7 = (bf16[32,16,128]{2,1,0:T(8,128)(2,1)S(1)}, bf16[32,16,128]{2,1,0:T(8,128)(2,1)S(1)}, u32[]{:S(2)}, u32[]{:S(2)}) collective-permute-start(bf16[32,16,128]{2,1,0:T(8,128)(2,1)S(1)} %get-tuple-element.42), channel_id=1, source_target_pairs={{0,2},{1,3},{2,0},{3,1},{4,6},{5,7},{6,4},{7,5},{8,10},{9,11},{10,... | collective-permute-start | bytes 393224 | tf_op jit(solution)/shard_map/ppermute | solution.py:303
  131.3 10.7 %collective-permute-start.8 = (bf16[32,16,128]{2,1,0:T(8,128)(2,1)S(1)}, bf16[32,16,128]{2,1,0:T(8,128)(2,1)S(1)}, u32[]{:S(2)}, u32[]{:S(2)}) collective-permute-start(bf16[32,16,128]{2,1,0:T(8,128)(2,1)S(1)} %get-tuple-element.43), channel_id=1, source_target_pairs={{0,6},{1,7},{2,4},{3,5},{4,2},{5,3},{6,0},{7,1},{8,14},{9,15},{10,... | collective-permute-start | bytes 393224 | tf_op jit(solution)/shard_map/ppermute | solution.py:303
  142.9 23.4 %all-to-all-start.3 = ((bf16[32,48,128]{2,1,0:T(8,128)(2,1)}), bf16[32,48,128]{2,1,0:T(8,128)(2,1)S(1)}, u32[]{:S(2)}, u32[]{:S(2)}) async-start(bf16[32,48,128]{2,1,0:T(8,128)(2,1)} %shard_map.85), calls=%async_computation.3 | async-start | bytes 786432 | tf_op jit(solution)/shard_map/all_to_all | solution.py:307

commit v6 on v5

--- a/solution.py
+++ b/solution.py
@@ -22,41 +22,34 @@
     return lax.dot_general(a, b, (((da,), (db,)), ((), ())), preferred_element_type=F32)
 
 
-def prepare_kernel(
-    blocks_any,
-    rows_any,
-    weights_any,
-    table_any,
-    grads_any,
-    own_ref,
-    other_ref,
-    half_ref,
-    out_ref,
-    blocks_ref,
-    rows_ref,
-    weights_ref,
-    table_ref,
-    grads_ref,
-    sems,
-):
-    anys = (blocks_any, rows_any, weights_any, grads_any, table_any)
-    refs = (blocks_ref, rows_ref, weights_ref, grads_ref, table_ref)
-    copies = [pltpu.make_async_copy(a, r, sems.at[i]) for i, (a, r) in enumerate(zip(anys, refs))]
+def fetch(sources, refs, sems):
+    copies = [pltpu.make_async_copy(a, r, sems.at[i]) for i, (a, r) in enumerate(zip(sources, refs))]
     for copy in copies:
         copy.start()
-    for copy in copies[:3]:
+    return copies
+
+
+def tag_kernel(blocks_any, rows_any, weights_any, own_ref, other_ref, blocks_ref, rows_ref, weights_ref, sems):
+    copies = fetch(
+        (blocks_any, rows_any, weights_any), (blocks_ref, rows_ref, weights_ref), sems
+    )
+    for copy in copies:
         copy.wait()
     tags(blocks_ref, rows_ref, weights_ref, own_ref, other_ref)
-    copies[3].wait()
-    for j in range(CHIPS):
-        out_ref[j] = grads_ref[:, 128 * j : 128 * (j + 1)]
-    copies[4].wait()
+
+
+def body_kernel(grads_any, table_any, half_ref, out_ref, grads_ref, table_ref, sems):
+    copies = fetch((table_any, grads_any), (table_ref, grads_ref), sems)
     y = lax.axis_index("y")
+    copies[0].wait()
     for i in range(4):
         block = (((y >> 1) ^ i) << 1) | (y & 1)
         rows = pl.ds(pl.multiple_of(block * 16, 16), 16)
         for j in range(CHIPS):
             half_ref[j, 16 * i : 16 * (i + 1), :] = table_ref[rows, 128 * j : 128 * (j + 1)]
+    copies[1].wait()
+    for j in range(CHIPS):
+        out_ref[j] = grads_ref[:, 128 * j : 128 * (j + 1)]
 
 
 def tags(blocks_ref, rows_ref, weights_ref, own_ref, other_ref):
@@ -88,9 +81,9 @@
 
 
 def first_kernel(own_ref, other_ref, half_ref, out_ref):
-    tags = own_ref[...].reshape(96, 128) + other_ref[...].reshape(96, 128)
+    both = own_ref[...].reshape(96, 128) + other_ref[...].reshape(96, 128)
     for j in range(CHIPS):
-        out_ref[j, 0:96, :] = tags
+        out_ref[j, 0:96, :] = both
         out_ref[j, 96:160, :] = half_ref[j]
 
 
@@ -312,27 +305,37 @@
 
 
 def on_device(key_blocks, key_rows, weights, value_table, cotangent):
-    own, other, half, grads = call(
-        prepare_kernel,
-        [(3, 32, 128)] * 2 + [(CHIPS, 64, 128), (CHIPS, 128, 128)],
+    own, other = call(
+        tag_kernel,
+        [(3, 32, 128)] * 2,
         key_blocks.T,
         key_rows.T,
         weights.T,
-        value_table,
-        cotangent,
         us=2,
         scratch=[
             pltpu.VMEM((2, 128), jnp.int32),
             pltpu.VMEM((32, 128), jnp.int32),
             pltpu.VMEM((32, 128), F32),
+            pltpu.SemaphoreType.DMA((3,)),
+        ],
+        limit=60,
+        spaces=[pl.ANY] * 3,
+    )
+    half, grads = call(
+        body_kernel,
+        [(CHIPS, 64, 128), (CHIPS, 128, 128)],
+        after(cotangent, own),
+        value_table,
+        us=2,
+        scratch=[
             pltpu.VMEM((128, 4096), BF16),
             pltpu.VMEM((128, 4096), BF16),
-            pltpu.SemaphoreType.DMA((5,)),
+            pltpu.SemaphoreType.DMA((2,)),
         ],
         limit=60,
-        spaces=[pl.ANY] * 5,
-    )
-    other = swap_cores(other)
+        spaces=[pl.ANY] * 2,
+    )
+    other, half, grads = lax.optimization_barrier((swap_cores(other), half, grads))
     (first,) = call(first_kernel, [(CHIPS, 160, 128)], own, other, half, us=0.4)
     got = exchange(first)
     near_grads = exchange(after(grads, got))

time: 168 us -> 168 us (level)
  Pallas kernels: 34.1 us -> 36.1 us
    pallas_call x11 -> x12, Pallas kernels: 34.1 us -> 36.1 us  [call(): pl.pallas_call(kernel, out_shape=outs, in_specs=[pl.BlockSpec(memory_spac...]
  transfers between devices with their start and end apart: 12 -> 12, of which waited for: 8 -> 7; matrix products, arithmetic and copies ran while one was open for 1% -> 1% of each run, Pallas kernels for 18% -> 20%
where the time goes in v6:
time: 168 us
  blocking collectives  47.8 us (28%)
  starting transfers between devices  46.6 us (28%)
  Pallas kernels  36.1 us (21%)
  waiting for transfers between devices  29.9 us (18%)
  local copies, waits for them, and re-layouts  6.24 us (4%)
    all_to_all x1, blocking collectives, exchange(): lax.all_to_all(v, ('x', 'z'), split_axis=0, concat_axis=0, tiled=True)  47.8 us
    pallas_call x12, Pallas kernels, call(): pl.pallas_call(kernel, out_shape=outs, in_specs=[pl.BlockSpec(memory_spac...  36.1 us
    all_to_all x3, starting transfers between devices, exchange(): lax.all_to_all(v, ('x', 'z'), split_axis=0, concat_axis=0, tiled=True)  19.6 us
    ppermute x5, starting transfers between devices, across(): return lax.ppermute(v, 'y', [(i, i ^ bits) for i in range(8)])  19.3 us
    all_to_all x3, waiting for transfers between devices, exchange(): lax.all_to_all(v, ('x', 'z'), split_axis=0, concat_axis=0, tiled=True)  17.6 us
    ppermute x5, waiting for transfers between devices, across(): return lax.ppermute(v, 'y', [(i, i ^ bits) for i in range(8)])  12.3 us
    ppermute x4, starting transfers between devices, swap_cores(): return lax.ppermute(v, 'core', [(0, 1), (1, 0)])  7.67 us
    unnamed x23, local copies, waits for them, and re-layouts  5.52 us
  transfers between devices with their start and end apart: 12, of which 7 were waited for; matrix products, arithmetic and copies ran while one was open for 1% of the time, Pallas kernels for 20%

profile of v6, /device:TPU:64, one launch (start us, length us, event | category | flops | bytes accessed | tf_op | source)
XLA Modules:
  0.0 167.6 jit_solution(3037632971471722460)
XLA Ops:
  0.6 2.0 %shard_map.76 = (bf16[3,32,128]{2,1,0:T(8,128)(2,1)}, bf16[3,32,128]{2,1,0:T(8,128)(2,1)}) custom-call(s32[2,128]{1,0:T(2,128)} %bitcast.10, s32[32,128]{1,0:T(8,128)} %bitcast.8, f32[32,128]{1,0:T(8,128)} %bitcast.9), custom_call_target="tpu_custom_call" | custom-call | flops 2000000000 | bytes 6600000 | tf_op jit(solution)/shard_map/pallas_call | solution.py:278
  2.7 0.0 copy-start.1
  2.7 1.9 %collective-permute-start = (bf16[3,32,128]{2,1,0:T(8,128)(2,1)}, bf16[3,32,128]{2,1,0:T(8,128)(2,1)S(1)}, u32[]{:S(2)}, u32[]{:S(2)}) collective-permute-start(bf16[3,32,128]{2,1,0:T(8,128)(2,1)} %get-tuple-element.30), channel_id=1, source_target_pairs={{0,8},{8,0},{1,9},{9,1},{2,10},{10,2},{3,11},{11,3},{4,12},{12,4},... | collective-permute-start | bytes 73736 | tf_op jit(solution)/shard_map/ppermute | solution.py:292
  4.6 2.9 %shard_map.77 = (bf16[32,64,128]{2,1,0:T(8,128)(2,1)}, bf16[32,128,128]{2,1,0:T(8,128)(2,1)}) custom-call(bf16[128,4096]{1,0:T(8,128)(2,1)} %grads_any, bf16[128,4096]{1,0:T(8,128)(2,1)} %table_any.1), custom_call_target="tpu_custom_call" | custom-call | flops 2000000000 | bytes 6600000 | tf_op jit(solution)/shard_map/pallas_call | solution.py:278
  7.5 0.0 collective-permute-done.other_ref
  7.5 1.0 copy-done
  8.6 0.1 shard_map.78
  8.7 47.8 %all_to_all.20.got_ref = bf16[32,160,128]{2,1,0:T(8,128)(2,1)S(1)} all-to-all(bf16[32,160,128]{2,1,0:T(8,128)(2,1)S(1)} %shard_map.78), channel_id=1, replica_groups=mesh['x'=4,'z'=8,'core'=2,'y'=8] {'x','z'}, dimensions={0} | all-to-all | bytes 2621440 | tf_op jit(solution)/shard_map/all_to_all | solution.py:300
  56.4 4.7 %all-to-all-start.1 = ((bf16[32,128,128]{2,1,0:T(8,128)(2,1)}), bf16[32,128,128]{2,1,0:T(8,128)(2,1)}, u32[]{:S(2)}, u32[]{:S(2)}) async-start(bf16[32,128,128]{2,1,0:T(8,128)(2,1)} %get-tuple-element.41), calls=%async_computation.1 | async-start | bytes 2097152 | tf_op jit(solution)/shard_map/all_to_all | solution.py:300
  61.1 0.1 slice.4
  61.2 3.5 %collective-permute-start.1 = (bf16[32,64,128]{2,1,0:T(8,128)(2,1)S(1)}, bf16[32,64,128]{2,1,0:T(8,128)(2,1)S(1)}, u32[]{:S(2)}, u32[]{:S(2)}) collective-permute-start(bf16[32,64,128]{2,1,0:T(8,128)(2,1)S(1)} %slice.4), channel_id=1, source_target_pairs={{0,1},{1,0},{2,3},{3,2},{4,5},{5,4},{6,7},{7,6},{8,9},{9,8},{10,11... | collective-permute-start | bytes 1572872 | tf_op jit(solution)/shard_map/ppermute | solution.py:296
  64.7 8.4 %shard_map.79 = (bf16[32,512,128]{2,1,0:T(8,128)(2,1)S(1)}, bf16[32,512,128]{2,1,0:T(8,128)(2,1)S(1)}, f32[32,8,512]{2,1,0:T(8,128)S(1)}) custom-call(bf16[32,160,128]{2,1,0:T(8,128)(2,1)S(1)} %all_to_all.20.got_ref), custom_call_target="tpu_custom_call" | custom-call | flops 8499999744 | bytes 28050000 | tf_op jit(solution)/shard_map/pallas_call | solution.py:278
  73.1 1.9 %copy-done.9 = bf16[32,512,128]{2,1,0:T(8,128)(2,1)} copy-done((bf16[32,512,128]{2,1,0:T(8,128)(2,1)}, bf16[32,512,128]{2,1,0:T(8,128)(2,1)S(1)}, u32[]{:S(2)}) %copy-start.9) | copy-done | bytes 4194328
  75.0 1.3 collective-permute-done.1.table_ref
  76.3 5.5 %shard_map.80 = (bf16[32,128,128]{2,1,0:T(8,128)(2,1)S(1)}, bf16[32,128,128]{2,1,0:T(8,128)(2,1)}) custom-call(bf16[32,512,128]{2,1,0:T(8,128)(2,1)S(1)} %get-tuple-element.36.mix_ref, f32[32,8,512]{2,1,0:T(8,128)S(1)} %get-tuple-element.37.token_ref, bf16[32,160,128]{2,1,0:T(8,128)(2,1)S(1)} %all_to_all.20.got_ref, ...), custom_call_target="tpu_custom_call" | custom-call | flops 4499999744 | bytes 14850000 | tf_op jit(solution)/shard_map/pallas_call | solution.py:278
  81.8 0.0 copy-done.2
  81.8 1.9 %collective-permute-start.2 = (bf16[32,128,128]{2,1,0:T(8,128)(2,1)}, bf16[32,128,128]{2,1,0:T(8,128)(2,1)S(1)}, u32[]{:S(2)}, u32[]{:S(2)}) collective-permute-start(bf16[32,128,128]{2,1,0:T(8,128)(2,1)} %get-tuple-element.39), channel_id=1, source_target_pairs={{0,8},{8,0},{1,9},{9,1},{2,10},{10,2},{3,11},{11,3},{4,12},{12,4},... | collective-permute-start | bytes 3145736 | tf_op jit(solution)/shard_map/ppermute | solution.py:292
  83.7 6.0 %all-to-all-done.1.near_any = bf16[32,128,128]{2,1,0:T(8,128)(2,1)} async-done(((bf16[32,128,128]{2,1,0:T(8,128)(2,1)}), bf16[32,128,128]{2,1,0:T(8,128)(2,1)}, u32[]{:S(2)}, u32[]{:S(2)}) %all-to-all-start.1) | async-done | bytes 1048608 | tf_op jit(solution)/shard_map/all_to_all | solution.py:300
  89.7 1.9 %collective-permute-start.3 = (bf16[32,128,128]{2,1,0:T(8,128)(2,1)}, bf16[32,128,128]{2,1,0:T(8,128)(2,1)}, u32[]{:S(2)}, u32[]{:S(2)}) collective-permute-start(bf16[32,128,128]{2,1,0:T(8,128)(2,1)} %all-to-all-done.1.near_any), channel_id=1, source_target_pairs={{0,8},{8,0},{1,9},{9,1},{2,10},{10,2},{3,11},{11,3},{4,12},{12,4},... | collective-permute-start | bytes 3145736 | tf_op jit(solution)/shard_map/ppermute | solution.py:292
  91.6 0.0 collective-permute-done.2.far_ref
  91.6 1.2 shard_map.81
  92.8 5.2 %all-to-all-start.2 = ((bf16[32,128,128]{2,1,0:T(8,128)(2,1)}), bf16[32,128,128]{2,1,0:T(8,128)(2,1)S(1)}, u32[]{:S(2)}, u32[]{:S(2)}) async-start(bf16[32,128,128]{2,1,0:T(8,128)(2,1)} %shard_map.81), calls=%async_computation.2 | async-start | bytes 2097152 | tf_op jit(solution)/shard_map/all_to_all | solution.py:300
  98.0 0.0 copy-start.5
  98.0 0.0 collective-permute-done.3.far_any
  98.0 1.2 copy-done.7
  99.2 4.4 %shard_map.82.rows_ref = bf16[32,512,128]{2,1,0:T(8,128)(2,1)S(1)} custom-call(bf16[32,128,128]{2,1,0:T(8,128)(2,1)} %all-to-all-done.1.near_any, bf16[32,128,128]{2,1,0:T(8,128)(2,1)} %collective-permute-done.3.far_any, f32[32,8,512]{2,1,0:T(8,128)S(1)} %copy-done.7), custom_call_target="tpu_custom_call" | custom-call | flops 3000000000 | bytes 9900000 | tf_op jit(solution)/shard_map/pallas_call | solution.py:278
  103.6 0.0 copy-done.5
  103.6 0.0 copy-start.3
  103.6 2.0 %shard_map.84 = (bf16[4,32,16,128]{3,2,1,0:T(8,128)(2,1)S(1)}, bf16[4,32,16,128]{3,2,1,0:T(8,128)(2,1)S(1)}) custom-call(bf16[32,512,128]{2,1,0:T(8,128)(2,1)S(1)} %copy-done.5, bf16[32,512,128]{2,1,0:T(8,128)(2,1)S(1)} %shard_map.82.rows_ref), custom_call_target="tpu_custom_call" | custom-call | flops 2500000000 | bytes 8250000 | tf_op jit(solution)/shard_map/pallas_call | solution.py:278
  105.6 3.5 %collective-permute-start.5 = (bf16[4,32,16,128]{3,2,1,0:T(8,128)(2,1)S(1)}, bf16[4,32,16,128]{3,2,1,0:T(8,128)(2,1)S(1)}, u32[]{:S(2)}, u32[]{:S(2)}) collective-permute-start(bf16[4,32,16,128]{3,2,1,0:T(8,128)(2,1)S(1)} %get-tuple-element.47), channel_id=1, source_target_pairs={{0,1},{1,0},{2,3},{3,2},{4,5},{5,4},{6,7},{7,6},{8,9},{9,8},{10,11... | collective-permute-start | bytes 1572872 | tf_op jit(solution)/shard_map/ppermute | solution.py:296
  109.1 7.9 %shard_map.83 = (bf16[32,32,128]{2,1,0:T(8,128)(2,1)S(1)}, bf16[32,32,128]{2,1,0:T(8,128)(2,1)S(1)}) custom-call(bf16[32,512,128]{2,1,0:T(8,128)(2,1)S(1)} %shard_map.82.rows_ref, bf16[32,512,128]{2,1,0:T(8,128)(2,1)S(1)} %copy-done.10, f32[32,8,512]{2,1,0:T(8,128)S(1)} %copy-done.8, bf16[32,160,128]{2,1,0:T(8,128)(2,1)S(1)} %all_to_all.20.got_ref, ...), custom_call_target="tpu_custom_call" | custom-call | flops 8000000000 | bytes 26400000 | tf_op jit(solution)/shard_map/pallas_call | solution.py:278
  117.1 1.9 %collective-permute-start.4 = (bf16[32,32,128]{2,1,0:T(8,128)(2,1)S(1)}, bf16[32,32,128]{2,1,0:T(8,128)(2,1)S(1)}, u32[]{:S(2)}, u32[]{:S(2)}) collective-permute-start(bf16[32,32,128]{2,1,0:T(8,128)(2,1)S(1)} %get-tuple-element.45), channel_id=1, source_target_pairs={{0,8},{8,0},{1,9},{9,1},{2,10},{10,2},{3,11},{11,3},{4,12},{12,4},... | collective-permute-start | bytes 786440 | tf_op jit(solution)/shard_map/ppermute | solution.py:292
  119.0 2.3 %collective-permute-done.5.got_ref = bf16[4,32,16,128]{3,2,1,0:T(8,128)(2,1)S(1)} collective-permute-done((bf16[4,32,16,128]{3,2,1,0:T(8,128)(2,1)S(1)}, bf16[4,32,16,128]{3,2,1,0:T(8,128)(2,1)S(1)}, u32[]{:S(2)}, u32[]{:S(2)}) %collective-permute-start.5) | collective-permute-done | bytes 524320 | tf_op jit(solution)/shard_map/ppermute | solution.py:296
  121.3 0.1 shard_map.85
  121.4 7.7 %collective-permute-start.6 = (bf16[32,16,128]{2,1,0:T(8,128)(2,1)S(1)}, bf16[32,16,128]{2,1,0:T(8,128)(2,1)S(1)}, u32[]{:S(2)}, u32[]{:S(2)}) collective-permute-start(bf16[32,16,128]{2,1,0:T(8,128)(2,1)S(1)} %get-tuple-element.49), channel_id=1, source_target_pairs={{0,4},{1,5},{2,6},{3,7},{4,0},{5,1},{6,2},{7,3},{8,12},{9,13},{10,... | collective-permute-start | bytes 393224 | tf_op jit(solution)/shard_map/ppermute | solution.py:296
  129.1 2.7 %collective-permute-start.7 = (bf16[32,16,128]{2,1,0:T(8,128)(2,1)S(1)}, bf16[32,16,128]{2,1,0:T(8,128)(2,1)S(1)}, u32[]{:S(2)}, u32[]{:S(2)}) collective-permute-start(bf16[32,16,128]{2,1,0:T(8,128)(2,1)S(1)} %get-tuple-element.50), channel_id=1, source_target_pairs={{0,2},{1,3},{2,0},{3,1},{4,6},{5,7},{6,4},{7,5},{8,10},{9,11},{10,... | collective-permute-start | bytes 393224 | tf_op jit(solution)/shard_map/ppermute | solution.py:296
  131.8 1.9 %collective-permute-start.8 = (bf16[32,16,128]{2,1,0:T(8,128)(2,1)S(1)}, bf16[32,16,128]{2,1,0:T(8,128)(2,1)S(1)}, u32[]{:S(2)}, u32[]{:S(2)}) collective-permute-start(bf16[32,16,128]{2,1,0:T(8,128)(2,1)S(1)} %get-tuple-element.51), channel_id=1, source_target_pairs={{0,6},{1,7},{2,4},{3,5},{4,2},{5,3},{6,0},{7,1},{8,14},{9,15},{10,... | collective-permute-start | bytes 393224 | tf_op jit(solution)/shard_map/ppermute | solution.py:296
  133.8 0.0 collective-permute-done.4.far_ref
  133.8 1.3 collective-permute-done.6.refs_1_
  135.1 5.8 %collective-permute-done.7.refs_2_ = bf16[32,16,128]{2,1,0:T(8,128)(2,1)S(1)} collective-permute-done((bf16[32,16,128]{2,1,0:T(8,128)(2,1)S(1)}, bf16[32,16,128]{2,1,0:T(8,128)(2,1)S(1)}, u32[]{:S(2)}, u32[]{:S(2)}) %collective-permute-start.7) | collective-permute-done | bytes 131104 | tf_op jit(solution)/shard_map/ppermute | solution.py:296
  140.9 1.6 collective-permute-done.8.refs_3_
  142.5 0.9 shard_map.86
  143.4 0.0 all-to-all-done.2
  143.4 9.8 %all-to-all-start.3 = ((bf16[32,48,128]{2,1,0:T(8,128)(2,1)}), bf16[32,48,128]{2,1,0:T(8,128)(2,1)S(1)}, u32[]{:S(2)}, u32[]{:S(2)}) async-start(bf16[32,48,128]{2,1,0:T(8,128)(2,1)} %shard_map.86), calls=%async_computation.3 | async-start | bytes 786432 | tf_op jit(solution)/shard_map/all_to_all | solution.py:300
  153.2 0.7 copy.8
  153.9 1.3 copy.9
  155.2 11.6 %all-to-all-done.3.got_ref = bf16[32,48,128]{2,1,0:T(8,128)(2,1)S(1)} async-done(((bf16[32,48,128]{2,1,0:T(8,128)(2,1)}), bf16[32,48,128]{2,1,0:T(8,128)(2,1)S(1)}, u32[]{:S(2)}, u32[]{:S(2)}) %all-to-all-start.3) | async-done | bytes 393248 | tf_op jit(solution)/shard_map/all_to_all | solution.py:300
  166.8 0.8 shard_map.87
  (14 shorter events, 0.0 us)
Async XLA Ops:
  2.7 4.8 %copy-start.1 = (bf16[3,32,128]{2,1,0:T(8,128)(2,1)S(1)}, bf16[3,32,128]{2,1,0:T(8,128)(2,1)}, u32[]{:S(2)}) copy-start(bf16[3,32,128]{2,1,0:T(8,128)(2,1)} %get-tuple-element.29.own_ref) | copy-start | bytes 73732
  2.7 4.8 %collective-permute-start = (bf16[3,32,128]{2,1,0:T(8,128)(2,1)}, bf16[3,32,128]{2,1,0:T(8,128)(2,1)S(1)}, u32[]{:S(2)}, u32[]{:S(2)}) collective-permute-start(bf16[3,32,128]{2,1,0:T(8,128)(2,1)} %get-tuple-element.30), channel_id=1, source_target_pairs={{0,8},{8,0},{1,9},{9,1},{2,10},{10,2},{3,11},{11,3},{4,12},{12,4},... | collective-permute-start | bytes 73736 | tf_op jit(solution)/shard_map/ppermute | solution.py:292
  7.5 1.0 copy-start
  56.4 33.2 %all-to-all-start.1 = ((bf16[32,128,128]{2,1,0:T(8,128)(2,1)}), bf16[32,128,128]{2,1,0:T(8,128)(2,1)}, u32[]{:S(2)}, u32[]{:S(2)}) async-start(bf16[32,128,128]{2,1,0:T(8,128)(2,1)} %get-tuple-element.41), calls=%async_computation.1 | async-start | bytes 2097152 | tf_op jit(solution)/shard_map/all_to_all | solution.py:300
  61.2 15.1 %collective-permute-start.1 = (bf16[32,64,128]{2,1,0:T(8,128)(2,1)S(1)}, bf16[32,64,128]{2,1,0:T(8,128)(2,1)S(1)}, u32[]{:S(2)}, u32[]{:S(2)}) collective-permute-start(bf16[32,64,128]{2,1,0:T(8,128)(2,1)S(1)} %slice.4), channel_id=1, source_target_pairs={{0,1},{1,0},{2,3},{3,2},{4,5},{5,4},{6,7},{7,6},{8,9},{9,8},{10,11... | collective-permute-start | bytes 1572872 | tf_op jit(solution)/shard_map/ppermute | solution.py:296
  73.1 2.0 %copy-start.9 = (bf16[32,512,128]{2,1,0:T(8,128)(2,1)}, bf16[32,512,128]{2,1,0:T(8,128)(2,1)S(1)}, u32[]{:S(2)}) copy-start(bf16[32,512,128]{2,1,0:T(8,128)(2,1)S(1)} %get-tuple-element.43.pick_ref) | copy-start | bytes 12582916
  75.0 6.7 %copy-start.4 = (bf16[32,512,128]{2,1,0:T(8,128)(2,1)}, bf16[32,512,128]{2,1,0:T(8,128)(2,1)S(1)}, u32[]{:S(2)}) copy-start(bf16[32,512,128]{2,1,0:T(8,128)(2,1)S(1)} %get-tuple-element.36.mix_ref) | copy-start | bytes 12582916
  75.0 6.7 %copy-start.6 = (f32[32,8,512]{2,1,0:T(8,128)}, f32[32,8,512]{2,1,0:T(8,128)S(1)}, u32[]{:S(2)}) copy-start(f32[32,8,512]{2,1,0:T(8,128)S(1)} %get-tuple-element.37.token_ref) | copy-start | bytes 1572868
  76.3 5.5 %copy-start.2 = (bf16[32,64,128]{2,1,0:T(8,128)(2,1)}, bf16[32,64,128]{2,1,0:T(8,128)(2,1)S(1)}, u32[]{:S(2)}) copy-start(bf16[32,64,128]{2,1,0:T(8,128)(2,1)S(1)} %collective-permute-done.1.table_ref) | copy-start | bytes 1572868
  81.8 9.8 %collective-permute-start.2 = (bf16[32,128,128]{2,1,0:T(8,128)(2,1)}, bf16[32,128,128]{2,1,0:T(8,128)(2,1)S(1)}, u32[]{:S(2)}, u32[]{:S(2)}) collective-permute-start(bf16[32,128,128]{2,1,0:T(8,128)(2,1)} %get-tuple-element.39), channel_id=1, source_target_pairs={{0,8},{8,0},{1,9},{9,1},{2,10},{10,2},{3,11},{11,3},{4,12},{12,4},... | collective-permute-start | bytes 3145736 | tf_op jit(solution)/shard_map/ppermute | solution.py:292
  89.7 8.3 %collective-permute-start.3 = (bf16[32,128,128]{2,1,0:T(8,128)(2,1)}, bf16[32,128,128]{2,1,0:T(8,128)(2,1)}, u32[]{:S(2)}, u32[]{:S(2)}) collective-permute-start(bf16[32,128,128]{2,1,0:T(8,128)(2,1)} %all-to-all-done.1.near_any), channel_id=1, source_target_pairs={{0,8},{8,0},{1,9},{9,1},{2,10},{10,2},{3,11},{11,3},{4,12},{12,4},... | collective-permute-start | bytes 3145736 | tf_op jit(solution)/shard_map/ppermute | solution.py:292
  92.8 50.6 %all-to-all-start.2 = ((bf16[32,128,128]{2,1,0:T(8,128)(2,1)}), bf16[32,128,128]{2,1,0:T(8,128)(2,1)S(1)}, u32[]{:S(2)}, u32[]{:S(2)}) async-start(bf16[32,128,128]{2,1,0:T(8,128)(2,1)} %shard_map.81), calls=%async_computation.2 | async-start | bytes 2097152 | tf_op jit(solution)/shard_map/all_to_all | solution.py:300
  98.0 5.6 %copy-start.5 = (bf16[32,512,128]{2,1,0:T(8,128)(2,1)S(1)}, bf16[32,512,128]{2,1,0:T(8,128)(2,1)}, u32[]{:S(2)}) copy-start(bf16[32,512,128]{2,1,0:T(8,128)(2,1)} %copy-done.4) | copy-start | bytes 12582916
  98.0 1.2 copy-start.7
  103.6 5.5 %copy-start.3 = (bf16[32,64,128]{2,1,0:T(8,128)(2,1)S(1)}, bf16[32,64,128]{2,1,0:T(8,128)(2,1)}, u32[]{:S(2)}) copy-start(bf16[32,64,128]{2,1,0:T(8,128)(2,1)} %copy-done.2) | copy-start | bytes 1572868
  103.6 5.5 %copy-start.8 = (f32[32,8,512]{2,1,0:T(8,128)S(1)}, f32[32,8,512]{2,1,0:T(8,128)}, u32[]{:S(2)}) copy-start(f32[32,8,512]{2,1,0:T(8,128)} %copy-done.6) | copy-start | bytes 1572868
  103.6 5.5 %copy-start.10 = (bf16[32,512,128]{2,1,0:T(8,128)(2,1)S(1)}, bf16[32,512,128]{2,1,0:T(8,128)(2,1)}, u32[]{:S(2)}) copy-start(bf16[32,512,128]{2,1,0:T(8,128)(2,1)} %copy-done.9) | copy-start | bytes 12582916
  105.6 15.7 %collective-permute-start.5 = (bf16[4,32,16,128]{3,2,1,0:T(8,128)(2,1)S(1)}, bf16[4,32,16,128]{3,2,1,0:T(8,128)(2,1)S(1)}, u32[]{:S(2)}, u32[]{:S(2)}) collective-permute-start(bf16[4,32,16,128]{3,2,1,0:T(8,128)(2,1)S(1)} %get-tuple-element.47), channel_id=1, source_target_pairs={{0,1},{1,0},{2,3},{3,2},{4,5},{5,4},{6,7},{7,6},{8,9},{9,8},{10,11... | collective-permute-start | bytes 1572872 | tf_op jit(solution)/shard_map/ppermute | solution.py:296
  117.1 16.7 %collective-permute-start.4 = (bf16[32,32,128]{2,1,0:T(8,128)(2,1)S(1)}, bf16[32,32,128]{2,1,0:T(8,128)(2,1)S(1)}, u32[]{:S(2)}, u32[]{:S(2)}) collective-permute-start(bf16[32,32,128]{2,1,0:T(8,128)(2,1)S(1)} %get-tuple-element.45), channel_id=1, source_target_pairs={{0,8},{8,0},{1,9},{9,1},{2,10},{10,2},{3,11},{11,3},{4,12},{12,4},... | collective-permute-start | bytes 786440 | tf_op jit(solution)/shard_map/ppermute | solution.py:292
  121.4 13.7 %collective-permute-start.6 = (bf16[32,16,128]{2,1,0:T(8,128)(2,1)S(1)}, bf16[32,16,128]{2,1,0:T(8,128)(2,1)S(1)}, u32[]{:S(2)}, u32[]{:S(2)}) collective-permute-start(bf16[32,16,128]{2,1,0:T(8,128)(2,1)S(1)} %get-tuple-element.49), channel_id=1, source_target_pairs={{0,4},{1,5},{2,6},{3,7},{4,0},{5,1},{6,2},{7,3},{8,12},{9,13},{10,... | collective-permute-start | bytes 393224 | tf_op jit(solution)/shard_map/ppermute | solution.py:296
  129.1 11.8 %collective-permute-start.7 = (bf16[32,16,128]{2,1,0:T(8,128)(2,1)S(1)}, bf16[32,16,128]{2,1,0:T(8,128)(2,1)S(1)}, u32[]{:S(2)}, u32[]{:S(2)}) collective-permute-start(bf16[32,16,128]{2,1,0:T(8,128)(2,1)S(1)} %get-tuple-element.50), channel_id=1, source_target_pairs={{0,2},{1,3},{2,0},{3,1},{4,6},{5,7},{6,4},{7,5},{8,10},{9,11},{10,... | collective-permute-start | bytes 393224 | tf_op jit(solution)/shard_map/ppermute | solution.py:296
  131.8 10.7 %collective-permute-start.8 = (bf16[32,16,128]{2,1,0:T(8,128)(2,1)S(1)}, bf16[32,16,128]{2,1,0:T(8,128)(2,1)S(1)}, u32[]{:S(2)}, u32[]{:S(2)}) collective-permute-start(bf16[32,16,128]{2,1,0:T(8,128)(2,1)S(1)} %get-tuple-element.51), channel_id=1, source_target_pairs={{0,6},{1,7},{2,4},{3,5},{4,2},{5,3},{6,0},{7,1},{8,14},{9,15},{10,... | collective-permute-start | bytes 393224 | tf_op jit(solution)/shard_map/ppermute | solution.py:296
  143.4 23.4 %all-to-all-start.3 = ((bf16[32,48,128]{2,1,0:T(8,128)(2,1)}), bf16[32,48,128]{2,1,0:T(8,128)(2,1)S(1)}, u32[]{:S(2)}, u32[]{:S(2)}) async-start(bf16[32,48,128]{2,1,0:T(8,128)(2,1)} %shard_map.86), calls=%async_computation.3 | async-start | bytes 786432 | tf_op jit(solution)/shard_map/all_to_all | solution.py:300

commit v7 on v4

--- a/solution.py
+++ b/solution.py
@@ -371,7 +371,7 @@
         scratch=[pltpu.VMEM((CHIPS, GROUP_SLOTS, 128), BF16)],
     )
     halves = call(fold_kernel, [(CHIPS, 16, 128)] * 4, keep, across(send, 1), us=0.3)
-    parts = [halves[0]] + [across(halves[i], 2 * i) for i in (2, 1, 3)]
+    parts = [halves[0]] + [across(halves[i], 2 * i) for i in (1, 3, 2)]
     (last,) = call(last_kernel, [(CHIPS, 48, 128)], near, swap_cores(far), *parts, us=0.8)
     got_last = exchange(after(last, got_out))
     memory_out = jnp.transpose(got_out, (1, 0, 2)).reshape(128, 4096)

time: 168 us -> 170 us (1.012)
    ppermute x5, waiting for transfers between devices: 12 us -> 14.2 us  [across(): return lax.ppermute(v, 'y', [(i, i ^ bits) for i in range(8)])]
  transfers between devices with their start and end apart: 12 -> 12, of which waited for: 8 -> 7; matrix products, arithmetic and copies ran while one was open for 1% -> 1% of each run, Pallas kernels for 18% -> 18%
where the time goes in v7:
time: 170 us; the launch traced here: 169 us
  blocking collectives  47.5 us (28%)
  starting transfers between devices  46.6 us (27%)
  Pallas kernels  34.6 us (20%)
  waiting for transfers between devices  32.2 us (19%)
  local copies, waits for them, and re-layouts  6.98 us (4%)
    all_to_all x1, blocking collectives, exchange(): lax.all_to_all(v, ('x', 'z'), split_axis=0, concat_axis=0, tiled=True)  47.5 us
    pallas_call x11, Pallas kernels, call(): pl.pallas_call(kernel, out_shape=outs, in_specs=[pl.BlockSpec(memory_spac...  34.6 us
    all_to_all x3, starting transfers between devices, exchange(): lax.all_to_all(v, ('x', 'z'), split_axis=0, concat_axis=0, tiled=True)  19.6 us
    ppermute x5, starting transfers between devices, across(): return lax.ppermute(v, 'y', [(i, i ^ bits) for i in range(8)])  19.3 us
    all_to_all x3, waiting for transfers between devices, exchange(): lax.all_to_all(v, ('x', 'z'), split_axis=0, concat_axis=0, tiled=True)  16.7 us
    ppermute x5, waiting for transfers between devices, across(): return lax.ppermute(v, 'y', [(i, i ^ bits) for i in range(8)])  14.2 us
    ppermute x4, starting transfers between devices, swap_cores(): return lax.ppermute(v, 'core', [(0, 1), (1, 0)])  7.67 us
    unnamed x23, local copies, waits for them, and re-layouts  6.26 us
  transfers between devices with their start and end apart: 12, of which 7 were waited for; matrix products, arithmetic and copies ran while one was open for 1% of the time, Pallas kernels for 18%

profile of v7, /device:TPU:64, one launch (start us, length us, event | category | flops | bytes accessed | tf_op | source)
XLA Modules:
  0.0 168.8 jit_solution(17600204523162608106)
XLA Ops:
  0.6 2.9 %shard_map.76 = (bf16[3,32,128]{2,1,0:T(8,128)(2,1)}, bf16[3,32,128]{2,1,0:T(8,128)(2,1)}, bf16[32,64,128]{2,1,0:T(8,128)(2,1)}, bf16[32,128,128]{2,1,0:T(8,128)(2,1)}) custom-call(s32[2,128]{1,0:T(2,128)} %bitcast.10, s32[32,128]{1,0:T(8,128)} %bitcast.8, f32[32,128]{1,0:T(8,128)} %bitcast.9, bf16[128,4096]{1,0:T(8,128)(2,1)} %table_any.1, ...), custom_call_target="tpu_custom_call" | custom-call | flops 2000000000 | bytes 6600000 | tf_op jit(solution)/shard_map/pallas_call | solution.py:274
  3.5 1.9 %collective-permute-start = (bf16[3,32,128]{2,1,0:T(8,128)(2,1)}, bf16[3,32,128]{2,1,0:T(8,128)(2,1)S(1)}, u32[]{:S(2)}, u32[]{:S(2)}) collective-permute-start(bf16[3,32,128]{2,1,0:T(8,128)(2,1)} %get-tuple-element.26), channel_id=1, source_target_pairs={{0,8},{8,0},{1,9},{9,1},{2,10},{10,2},{3,11},{11,3},{4,12},{12,4},... | collective-permute-start | bytes 73736 | tf_op jit(solution)/shard_map/ppermute | solution.py:288
  5.5 1.4 collective-permute-done.other_ref
  6.8 1.0 copy-done
  7.9 0.7 copy-done.1
  8.6 0.1 shard_map.77
  8.7 47.5 %all_to_all.20.got_ref = bf16[32,160,128]{2,1,0:T(8,128)(2,1)S(1)} all-to-all(bf16[32,160,128]{2,1,0:T(8,128)(2,1)S(1)} %shard_map.77), channel_id=1, replica_groups=mesh['x'=4,'z'=8,'core'=2,'y'=8] {'x','z'}, dimensions={0} | all-to-all | bytes 2621440 | tf_op jit(solution)/shard_map/all_to_all | solution.py:296
  56.2 4.6 %all-to-all-start.1 = ((bf16[32,128,128]{2,1,0:T(8,128)(2,1)}), bf16[32,128,128]{2,1,0:T(8,128)(2,1)}, u32[]{:S(2)}, u32[]{:S(2)}) async-start(bf16[32,128,128]{2,1,0:T(8,128)(2,1)} %get-tuple-element.33), calls=%async_computation.1 | async-start | bytes 2097152 | tf_op jit(solution)/shard_map/all_to_all | solution.py:296
  60.8 0.1 slice.4
  60.9 3.5 %collective-permute-start.1 = (bf16[32,64,128]{2,1,0:T(8,128)(2,1)S(1)}, bf16[32,64,128]{2,1,0:T(8,128)(2,1)S(1)}, u32[]{:S(2)}, u32[]{:S(2)}) collective-permute-start(bf16[32,64,128]{2,1,0:T(8,128)(2,1)S(1)} %slice.4), channel_id=1, source_target_pairs={{0,1},{1,0},{2,3},{3,2},{4,5},{5,4},{6,7},{7,6},{8,9},{9,8},{10,11... | collective-permute-start | bytes 1572872 | tf_op jit(solution)/shard_map/ppermute | solution.py:292
  64.4 8.4 %shard_map.78 = (bf16[32,512,128]{2,1,0:T(8,128)(2,1)S(1)}, bf16[32,512,128]{2,1,0:T(8,128)(2,1)S(1)}, f32[32,8,512]{2,1,0:T(8,128)S(1)}) custom-call(bf16[32,160,128]{2,1,0:T(8,128)(2,1)S(1)} %all_to_all.20.got_ref), custom_call_target="tpu_custom_call" | custom-call | flops 8499999744 | bytes 28050000 | tf_op jit(solution)/shard_map/pallas_call | solution.py:274
  72.8 0.0 copy-start.9
  72.8 2.0 %copy-done.9 = bf16[32,512,128]{2,1,0:T(8,128)(2,1)} copy-done((bf16[32,512,128]{2,1,0:T(8,128)(2,1)}, bf16[32,512,128]{2,1,0:T(8,128)(2,1)S(1)}, u32[]{:S(2)}) %copy-start.9) | copy-done | bytes 4194328
  74.7 1.0 collective-permute-done.1.table_ref
  75.7 5.5 %shard_map.79 = (bf16[32,128,128]{2,1,0:T(8,128)(2,1)S(1)}, bf16[32,128,128]{2,1,0:T(8,128)(2,1)}) custom-call(bf16[32,512,128]{2,1,0:T(8,128)(2,1)S(1)} %get-tuple-element.28.mix_ref, f32[32,8,512]{2,1,0:T(8,128)S(1)} %get-tuple-element.29.token_ref, bf16[32,160,128]{2,1,0:T(8,128)(2,1)S(1)} %all_to_all.20.got_ref, ...), custom_call_target="tpu_custom_call" | custom-call | flops 4499999744 | bytes 14850000 | tf_op jit(solution)/shard_map/pallas_call | solution.py:274
  81.2 0.0 copy-done.4
  81.2 0.0 copy-done.6
  81.2 0.0 copy-done.2
  81.2 1.9 %collective-permute-start.2 = (bf16[32,128,128]{2,1,0:T(8,128)(2,1)}, bf16[32,128,128]{2,1,0:T(8,128)(2,1)S(1)}, u32[]{:S(2)}, u32[]{:S(2)}) collective-permute-start(bf16[32,128,128]{2,1,0:T(8,128)(2,1)} %get-tuple-element.31), channel_id=1, source_target_pairs={{0,8},{8,0},{1,9},{9,1},{2,10},{10,2},{3,11},{11,3},{4,12},{12,4},... | collective-permute-start | bytes 3145736 | tf_op jit(solution)/shard_map/ppermute | solution.py:288
  83.1 6.1 %all-to-all-done.1.near_ref = bf16[32,128,128]{2,1,0:T(8,128)(2,1)} async-done(((bf16[32,128,128]{2,1,0:T(8,128)(2,1)}), bf16[32,128,128]{2,1,0:T(8,128)(2,1)}, u32[]{:S(2)}, u32[]{:S(2)}) %all-to-all-start.1) | async-done | bytes 1048608 | tf_op jit(solution)/shard_map/all_to_all | solution.py:296
  89.2 1.9 %collective-permute-start.3 = (bf16[32,128,128]{2,1,0:T(8,128)(2,1)}, bf16[32,128,128]{2,1,0:T(8,128)(2,1)}, u32[]{:S(2)}, u32[]{:S(2)}) collective-permute-start(bf16[32,128,128]{2,1,0:T(8,128)(2,1)} %all-to-all-done.1.near_ref), channel_id=1, source_target_pairs={{0,8},{8,0},{1,9},{9,1},{2,10},{10,2},{3,11},{11,3},{4,12},{12,4},... | collective-permute-start | bytes 3145736 | tf_op jit(solution)/shard_map/ppermute | solution.py:288
  91.1 0.0 collective-permute-done.2.far_ref
  91.1 1.2 shard_map.80
  92.3 5.2 %all-to-all-start.2 = ((bf16[32,128,128]{2,1,0:T(8,128)(2,1)}), bf16[32,128,128]{2,1,0:T(8,128)(2,1)S(1)}, u32[]{:S(2)}, u32[]{:S(2)}) async-start(bf16[32,128,128]{2,1,0:T(8,128)(2,1)} %shard_map.80), calls=%async_computation.2 | async-start | bytes 2097152 | tf_op jit(solution)/shard_map/all_to_all | solution.py:296
  97.5 0.0 copy-start.5
  97.5 0.0 collective-permute-done.3.far_ref
  97.6 1.2 copy-done.7
  98.7 4.9 %shard_map.81.rows_ref = bf16[32,512,128]{2,1,0:T(8,128)(2,1)S(1)} custom-call(f32[32,8,512]{2,1,0:T(8,128)S(1)} %copy-done.7, bf16[32,128,128]{2,1,0:T(8,128)(2,1)} %all-to-all-done.1.near_ref, bf16[32,128,128]{2,1,0:T(8,128)(2,1)} %collective-permute-done.3.far_ref), custom_call_target="tpu_custom_call" | custom-call | flops 3000000000 | bytes 9900000 | tf_op jit(solution)/shard_map/pallas_call | solution.py:274
  103.7 2.0 %shard_map.83 = (bf16[4,32,16,128]{3,2,1,0:T(8,128)(2,1)S(1)}, bf16[4,32,16,128]{3,2,1,0:T(8,128)(2,1)S(1)}) custom-call(bf16[32,512,128]{2,1,0:T(8,128)(2,1)S(1)} %copy-done.5, bf16[32,512,128]{2,1,0:T(8,128)(2,1)S(1)} %shard_map.81.rows_ref), custom_call_target="tpu_custom_call" | custom-call | flops 2500000000 | bytes 8250000 | tf_op jit(solution)/shard_map/pallas_call | solution.py:274
  105.6 3.5 %collective-permute-start.5 = (bf16[4,32,16,128]{3,2,1,0:T(8,128)(2,1)S(1)}, bf16[4,32,16,128]{3,2,1,0:T(8,128)(2,1)S(1)}, u32[]{:S(2)}, u32[]{:S(2)}) collective-permute-start(bf16[4,32,16,128]{3,2,1,0:T(8,128)(2,1)S(1)} %get-tuple-element.39), channel_id=1, source_target_pairs={{0,1},{1,0},{2,3},{3,2},{4,5},{5,4},{6,7},{7,6},{8,9},{9,8},{10,11... | collective-permute-start | bytes 1572872 | tf_op jit(solution)/shard_map/ppermute | solution.py:292
  109.2 7.9 %shard_map.82 = (bf16[32,32,128]{2,1,0:T(8,128)(2,1)S(1)}, bf16[32,32,128]{2,1,0:T(8,128)(2,1)S(1)}) custom-call(bf16[32,512,128]{2,1,0:T(8,128)(2,1)S(1)} %shard_map.81.rows_ref, bf16[32,512,128]{2,1,0:T(8,128)(2,1)S(1)} %copy-done.10, f32[32,8,512]{2,1,0:T(8,128)S(1)} %copy-done.8, bf16[32,160,128]{2,1,0:T(8,128)(2,1)S(1)} %all_to_all.20.got_ref, ...), custom_call_target="tpu_custom_call" | custom-call | flops 8000000000 | bytes 26400000 | tf_op jit(solution)/shard_map/pallas_call | solution.py:274
  117.1 1.9 %collective-permute-start.4 = (bf16[32,32,128]{2,1,0:T(8,128)(2,1)S(1)}, bf16[32,32,128]{2,1,0:T(8,128)(2,1)S(1)}, u32[]{:S(2)}, u32[]{:S(2)}) collective-permute-start(bf16[32,32,128]{2,1,0:T(8,128)(2,1)S(1)} %get-tuple-element.37), channel_id=1, source_target_pairs={{0,8},{8,0},{1,9},{9,1},{2,10},{10,2},{3,11},{11,3},{4,12},{12,4},... | collective-permute-start | bytes 786440 | tf_op jit(solution)/shard_map/ppermute | solution.py:288
  119.0 2.3 %collective-permute-done.5.got_ref = bf16[4,32,16,128]{3,2,1,0:T(8,128)(2,1)S(1)} collective-permute-done((bf16[4,32,16,128]{3,2,1,0:T(8,128)(2,1)S(1)}, bf16[4,32,16,128]{3,2,1,0:T(8,128)(2,1)S(1)}, u32[]{:S(2)}, u32[]{:S(2)}) %collective-permute-start.5) | collective-permute-done | bytes 524320 | tf_op jit(solution)/shard_map/ppermute | solution.py:292
  121.3 0.1 shard_map.84
  121.4 4.5 %collective-permute-start.6 = (bf16[32,16,128]{2,1,0:T(8,128)(2,1)S(1)}, bf16[32,16,128]{2,1,0:T(8,128)(2,1)S(1)}, u32[]{:S(2)}, u32[]{:S(2)}) collective-permute-start(bf16[32,16,128]{2,1,0:T(8,128)(2,1)S(1)} %get-tuple-element.41), channel_id=1, source_target_pairs={{0,2},{1,3},{2,0},{3,1},{4,6},{5,7},{6,4},{7,5},{8,10},{9,11},{10,... | collective-permute-start | bytes 393224 | tf_op jit(solution)/shard_map/ppermute | solution.py:292
  125.9 5.7 %collective-permute-start.7 = (bf16[32,16,128]{2,1,0:T(8,128)(2,1)S(1)}, bf16[32,16,128]{2,1,0:T(8,128)(2,1)S(1)}, u32[]{:S(2)}, u32[]{:S(2)}) collective-permute-start(bf16[32,16,128]{2,1,0:T(8,128)(2,1)S(1)} %get-tuple-element.42), channel_id=1, source_target_pairs={{0,6},{1,7},{2,4},{3,5},{4,2},{5,3},{6,0},{7,1},{8,14},{9,15},{10,... | collective-permute-start | bytes 393224 | tf_op jit(solution)/shard_map/ppermute | solution.py:292
  131.6 2.2 %collective-permute-start.8 = (bf16[32,16,128]{2,1,0:T(8,128)(2,1)S(1)}, bf16[32,16,128]{2,1,0:T(8,128)(2,1)S(1)}, u32[]{:S(2)}, u32[]{:S(2)}) collective-permute-start(bf16[32,16,128]{2,1,0:T(8,128)(2,1)S(1)} %get-tuple-element.43), channel_id=1, source_target_pairs={{0,4},{1,5},{2,6},{3,7},{4,0},{5,1},{6,2},{7,3},{8,12},{9,13},{10,... | collective-permute-start | bytes 393224 | tf_op jit(solution)/shard_map/ppermute | solution.py:292
  133.8 0.0 collective-permute-done.4.far_ref
  133.8 0.0 collective-permute-done.6.refs_1_
  133.8 7.9 %collective-permute-done.7.refs_2_ = bf16[32,16,128]{2,1,0:T(8,128)(2,1)S(1)} collective-permute-done((bf16[32,16,128]{2,1,0:T(8,128)(2,1)S(1)}, bf16[32,16,128]{2,1,0:T(8,128)(2,1)S(1)}, u32[]{:S(2)}, u32[]{:S(2)}) %collective-permute-start.7) | collective-permute-done | bytes 131104 | tf_op jit(solution)/shard_map/ppermute | solution.py:292
  141.8 3.0 %collective-permute-done.8.refs_3_ = bf16[32,16,128]{2,1,0:T(8,128)(2,1)S(1)} collective-permute-done((bf16[32,16,128]{2,1,0:T(8,128)(2,1)S(1)}, bf16[32,16,128]{2,1,0:T(8,128)(2,1)S(1)}, u32[]{:S(2)}, u32[]{:S(2)}) %collective-permute-start.8) | collective-permute-done | bytes 131104 | tf_op jit(solution)/shard_map/ppermute | solution.py:292
  144.7 0.9 shard_map.85
  145.6 0.0 all-to-all-done.2
  145.6 9.7 %all-to-all-start.3 = ((bf16[32,48,128]{2,1,0:T(8,128)(2,1)}), bf16[32,48,128]{2,1,0:T(8,128)(2,1)S(1)}, u32[]{:S(2)}, u32[]{:S(2)}) async-start(bf16[32,48,128]{2,1,0:T(8,128)(2,1)} %shard_map.85), calls=%async_computation.3 | async-start | bytes 786432 | tf_op jit(solution)/shard_map/all_to_all | solution.py:296
  155.4 0.7 copy.8
  156.1 1.3 copy.9
  157.4 10.6 %all-to-all-done.3.got_ref = bf16[32,48,128]{2,1,0:T(8,128)(2,1)S(1)} async-done(((bf16[32,48,128]{2,1,0:T(8,128)(2,1)}), bf16[32,48,128]{2,1,0:T(8,128)(2,1)S(1)}, u32[]{:S(2)}, u32[]{:S(2)}) %all-to-all-start.3) | async-done | bytes 393248 | tf_op jit(solution)/shard_map/all_to_all | solution.py:296
  168.0 0.8 shard_map.86
  (13 shorter events, 0.0 us)
Async XLA Ops:
  3.5 3.3 %collective-permute-start = (bf16[3,32,128]{2,1,0:T(8,128)(2,1)}, bf16[3,32,128]{2,1,0:T(8,128)(2,1)S(1)}, u32[]{:S(2)}, u32[]{:S(2)}) collective-permute-start(bf16[3,32,128]{2,1,0:T(8,128)(2,1)} %get-tuple-element.26), channel_id=1, source_target_pairs={{0,8},{8,0},{1,9},{9,1},{2,10},{10,2},{3,11},{11,3},{4,12},{12,4},... | collective-permute-start | bytes 73736 | tf_op jit(solution)/shard_map/ppermute | solution.py:288
  6.8 1.0 copy-start
  7.9 0.7 copy-start.1
  56.2 33.0 %all-to-all-start.1 = ((bf16[32,128,128]{2,1,0:T(8,128)(2,1)}), bf16[32,128,128]{2,1,0:T(8,128)(2,1)}, u32[]{:S(2)}, u32[]{:S(2)}) async-start(bf16[32,128,128]{2,1,0:T(8,128)(2,1)} %get-tuple-element.33), calls=%async_computation.1 | async-start | bytes 2097152 | tf_op jit(solution)/shard_map/all_to_all | solution.py:296
  60.9 14.8 %collective-permute-start.1 = (bf16[32,64,128]{2,1,0:T(8,128)(2,1)S(1)}, bf16[32,64,128]{2,1,0:T(8,128)(2,1)S(1)}, u32[]{:S(2)}, u32[]{:S(2)}) collective-permute-start(bf16[32,64,128]{2,1,0:T(8,128)(2,1)S(1)} %slice.4), channel_id=1, source_target_pairs={{0,1},{1,0},{2,3},{3,2},{4,5},{5,4},{6,7},{7,6},{8,9},{9,8},{10,11... | collective-permute-start | bytes 1572872 | tf_op jit(solution)/shard_map/ppermute | solution.py:292
  72.8 2.0 %copy-start.9 = (bf16[32,512,128]{2,1,0:T(8,128)(2,1)}, bf16[32,512,128]{2,1,0:T(8,128)(2,1)S(1)}, u32[]{:S(2)}) copy-start(bf16[32,512,128]{2,1,0:T(8,128)(2,1)S(1)} %get-tuple-element.35.pick_ref) | copy-start | bytes 12582916
  74.7 6.5 %copy-start.4 = (bf16[32,512,128]{2,1,0:T(8,128)(2,1)}, bf16[32,512,128]{2,1,0:T(8,128)(2,1)S(1)}, u32[]{:S(2)}) copy-start(bf16[32,512,128]{2,1,0:T(8,128)(2,1)S(1)} %get-tuple-element.28.mix_ref) | copy-start | bytes 12582916
  74.7 6.5 %copy-start.6 = (f32[32,8,512]{2,1,0:T(8,128)}, f32[32,8,512]{2,1,0:T(8,128)S(1)}, u32[]{:S(2)}) copy-start(f32[32,8,512]{2,1,0:T(8,128)S(1)} %get-tuple-element.29.token_ref) | copy-start | bytes 1572868
  75.7 5.5 %copy-start.2 = (bf16[32,64,128]{2,1,0:T(8,128)(2,1)}, bf16[32,64,128]{2,1,0:T(8,128)(2,1)S(1)}, u32[]{:S(2)}) copy-start(bf16[32,64,128]{2,1,0:T(8,128)(2,1)S(1)} %collective-permute-done.1.table_ref) | copy-start | bytes 1572868
  81.2 9.9 %collective-permute-start.2 = (bf16[32,128,128]{2,1,0:T(8,128)(2,1)}, bf16[32,128,128]{2,1,0:T(8,128)(2,1)S(1)}, u32[]{:S(2)}, u32[]{:S(2)}) collective-permute-start(bf16[32,128,128]{2,1,0:T(8,128)(2,1)} %get-tuple-element.31), channel_id=1, source_target_pairs={{0,8},{8,0},{1,9},{9,1},{2,10},{10,2},{3,11},{11,3},{4,12},{12,4},... | collective-permute-start | bytes 3145736 | tf_op jit(solution)/shard_map/ppermute | solution.py:288
  89.2 8.3 %collective-permute-start.3 = (bf16[32,128,128]{2,1,0:T(8,128)(2,1)}, bf16[32,128,128]{2,1,0:T(8,128)(2,1)}, u32[]{:S(2)}, u32[]{:S(2)}) collective-permute-start(bf16[32,128,128]{2,1,0:T(8,128)(2,1)} %all-to-all-done.1.near_ref), channel_id=1, source_target_pairs={{0,8},{8,0},{1,9},{9,1},{2,10},{10,2},{3,11},{11,3},{4,12},{12,4},... | collective-permute-start | bytes 3145736 | tf_op jit(solution)/shard_map/ppermute | solution.py:288
  92.3 53.3 %all-to-all-start.2 = ((bf16[32,128,128]{2,1,0:T(8,128)(2,1)}), bf16[32,128,128]{2,1,0:T(8,128)(2,1)S(1)}, u32[]{:S(2)}, u32[]{:S(2)}) async-start(bf16[32,128,128]{2,1,0:T(8,128)(2,1)} %shard_map.80), calls=%async_computation.2 | async-start | bytes 2097152 | tf_op jit(solution)/shard_map/all_to_all | solution.py:296
  97.5 6.1 %copy-start.5 = (bf16[32,512,128]{2,1,0:T(8,128)(2,1)S(1)}, bf16[32,512,128]{2,1,0:T(8,128)(2,1)}, u32[]{:S(2)}) copy-start(bf16[32,512,128]{2,1,0:T(8,128)(2,1)} %copy-done.4) | copy-start | bytes 12582916
  97.5 1.2 copy-start.7
  103.6 5.5 %copy-start.3 = (bf16[32,64,128]{2,1,0:T(8,128)(2,1)S(1)}, bf16[32,64,128]{2,1,0:T(8,128)(2,1)}, u32[]{:S(2)}) copy-start(bf16[32,64,128]{2,1,0:T(8,128)(2,1)} %copy-done.2) | copy-start | bytes 1572868
  103.7 5.5 %copy-start.8 = (f32[32,8,512]{2,1,0:T(8,128)S(1)}, f32[32,8,512]{2,1,0:T(8,128)}, u32[]{:S(2)}) copy-start(f32[32,8,512]{2,1,0:T(8,128)} %copy-done.6) | copy-start | bytes 1572868
  103.7 5.5 %copy-start.10 = (bf16[32,512,128]{2,1,0:T(8,128)(2,1)S(1)}, bf16[32,512,128]{2,1,0:T(8,128)(2,1)}, u32[]{:S(2)}) copy-start(bf16[32,512,128]{2,1,0:T(8,128)(2,1)} %copy-done.9) | copy-start | bytes 12582916
  105.6 15.7 %collective-permute-start.5 = (bf16[4,32,16,128]{3,2,1,0:T(8,128)(2,1)S(1)}, bf16[4,32,16,128]{3,2,1,0:T(8,128)(2,1)S(1)}, u32[]{:S(2)}, u32[]{:S(2)}) collective-permute-start(bf16[4,32,16,128]{3,2,1,0:T(8,128)(2,1)S(1)} %get-tuple-element.39), channel_id=1, source_target_pairs={{0,1},{1,0},{2,3},{3,2},{4,5},{5,4},{6,7},{7,6},{8,9},{9,8},{10,11... | collective-permute-start | bytes 1572872 | tf_op jit(solution)/shard_map/ppermute | solution.py:292
  117.1 16.7 %collective-permute-start.4 = (bf16[32,32,128]{2,1,0:T(8,128)(2,1)S(1)}, bf16[32,32,128]{2,1,0:T(8,128)(2,1)S(1)}, u32[]{:S(2)}, u32[]{:S(2)}) collective-permute-start(bf16[32,32,128]{2,1,0:T(8,128)(2,1)S(1)} %get-tuple-element.37), channel_id=1, source_target_pairs={{0,8},{8,0},{1,9},{9,1},{2,10},{10,2},{3,11},{11,3},{4,12},{12,4},... | collective-permute-start | bytes 786440 | tf_op jit(solution)/shard_map/ppermute | solution.py:288
  121.4 12.4 %collective-permute-start.6 = (bf16[32,16,128]{2,1,0:T(8,128)(2,1)S(1)}, bf16[32,16,128]{2,1,0:T(8,128)(2,1)S(1)}, u32[]{:S(2)}, u32[]{:S(2)}) collective-permute-start(bf16[32,16,128]{2,1,0:T(8,128)(2,1)S(1)} %get-tuple-element.41), channel_id=1, source_target_pairs={{0,2},{1,3},{2,0},{3,1},{4,6},{5,7},{6,4},{7,5},{8,10},{9,11},{10,... | collective-permute-start | bytes 393224 | tf_op jit(solution)/shard_map/ppermute | solution.py:292
  125.9 15.8 %collective-permute-start.7 = (bf16[32,16,128]{2,1,0:T(8,128)(2,1)S(1)}, bf16[32,16,128]{2,1,0:T(8,128)(2,1)S(1)}, u32[]{:S(2)}, u32[]{:S(2)}) collective-permute-start(bf16[32,16,128]{2,1,0:T(8,128)(2,1)S(1)} %get-tuple-element.42), channel_id=1, source_target_pairs={{0,6},{1,7},{2,4},{3,5},{4,2},{5,3},{6,0},{7,1},{8,14},{9,15},{10,... | collective-permute-start | bytes 393224 | tf_op jit(solution)/shard_map/ppermute | solution.py:292
  131.6 13.1 %collective-permute-start.8 = (bf16[32,16,128]{2,1,0:T(8,128)(2,1)S(1)}, bf16[32,16,128]{2,1,0:T(8,128)(2,1)S(1)}, u32[]{:S(2)}, u32[]{:S(2)}) collective-permute-start(bf16[32,16,128]{2,1,0:T(8,128)(2,1)S(1)} %get-tuple-element.43), channel_id=1, source_target_pairs={{0,4},{1,5},{2,6},{3,7},{4,0},{5,1},{6,2},{7,3},{8,12},{9,13},{10,... | collective-permute-start | bytes 393224 | tf_op jit(solution)/shard_map/ppermute | solution.py:292
  145.6 22.4 %all-to-all-start.3 = ((bf16[32,48,128]{2,1,0:T(8,128)(2,1)}), bf16[32,48,128]{2,1,0:T(8,128)(2,1)S(1)}, u32[]{:S(2)}, u32[]{:S(2)}) async-start(bf16[32,48,128]{2,1,0:T(8,128)(2,1)} %shard_map.85), calls=%async_computation.3 | async-start | bytes 786432 | tf_op jit(solution)/shard_map/all_to_all | solution.py:296
